TPU v7x, 32 devices: a whole 2x2x4 slice. The times are simulated.
32 devices in a mesh: tm: 4 (over y, x), azim: 8 (over z, core).
Axes of the slice: x: 2, y: 2, z: 4, core: 2. Of those that a mesh axis runs over, the one named last changes fastest.
Arguments:
- rotor_coeffs: float32 [64, 2, 8, 16384], P('tm', None, 'azim'), may hold values from -1.5 to 1.5
- mortar_weights: float32 [64, 2, 8, 16384], P('tm', None, 'azim'), may hold values from 0.2 to 1
- block_shifts: int32 [64], P('tm'), may hold values from 0 to 7
- stencil_offsets: int32 [64, 2], P('tm'), may hold values from -1 to 1
- reluctivity: float32 [8, 16384], P('azim'), may hold values from 0.5 to 2
- source: float32 [64, 2, 8, 16384], P('tm', None, 'azim'), may hold values from -3 to 3
Outputs:
- residual: float32 [64, 2, 8, 16384], P('tm', None, 'azim')
All inputs are finite; a program needn't handle non-finite values.
Results may differ from a plain program's by a relative error of at most 0.0001.
Values sent between devices are 32-bit elements; how exact they have to be, the bound alone decides.
No kernel may reach another device: no remote copies, remote signals or barrier semaphores. Data moves between devices by JAX's collectives and lax.ppermute only.
A program may use at most 128 MiB of HBM per device.

v0:
```python
import jax
import jax.numpy as jnp
from jax import lax
from jax.sharding import PartitionSpec as P

KC = 64
NT = 64


def shifted(value, axis, steps):
    count = lax.axis_size(axis)
    pairs = [(source, (source + steps) % count) for source in range(count)]
    return lax.ppermute(value, axis, pairs)


def with_halo(value, sides, width):
    for axis, dim in sides:
        devices, length = (lax.axis_size(axis), value.shape[dim])
        up = [(i, (i + 1) % devices) for i in range(devices)]
        down = [(j, i) for i, j in up]
        last = lax.slice_in_dim(value, length - width, length, axis=dim)
        initial = lax.slice_in_dim(value, 0, width, axis=dim)
        before = lax.ppermute(last, axis, up)
        after = lax.ppermute(initial, axis, down)
        value = jnp.concatenate([before, value, after], axis=dim)
    return value


def harmonic_basis(sample_rows, coefficient_count):
    column = jnp.arange(coefficient_count, dtype=jnp.int32)
    harmonic_order = 2 * (column // 2) + 1
    phase_index = harmonic_order[None, :] * (2 * sample_rows[:, None] + 1) % (4 * NT)
    phase_angle = phase_index.astype(jnp.float32) * (jnp.pi / (2 * NT))
    return jnp.where(column[None, :] % 2 == 0, jnp.cos(phase_angle), jnp.sin(phase_angle))


def body(rotor_coeffs, mortar_weights, block_shifts, stencil_offsets, reluctivity, source):
    sample_rows = mortar_weights.shape[0]
    stencil_count = mortar_weights.shape[1]
    full_table = harmonic_basis(jnp.arange(NT, dtype=jnp.int32), KC)
    spread = jnp.einsum(
        "jc,cabp->jabp",
        full_table,
        lax.all_to_all(rotor_coeffs, "tm", split_axis=3, concat_axis=0, tiled=True),
        precision=lax.Precision.HIGHEST,
    )
    samples = lax.all_to_all(spread, "tm", split_axis=0, concat_axis=3, tiled=True)
    turned = samples
    for bit_level in range((lax.axis_size("azim") - 1).bit_length()):
        moved = shifted(turned, "azim", 1 << bit_level)
        chosen = block_shifts >> bit_level & 1 == 1
        turned = jnp.where(chosen[:, None, None, None], moved, turned)
    padded = with_halo(turned, (("azim", 2),), 1)
    airgap_field = jnp.zeros_like(samples)
    for stencil_entry in range(stencil_count):
        pick_index = stencil_offsets[:, stencil_entry] + 1
        neighbour = jnp.zeros_like(samples)
        for position in range(3):
            neighbour = neighbour + jnp.where(
                (pick_index == position)[:, None, None, None],
                padded[:, :, position : position + 1],
                0.0,
            )
        airgap_field = airgap_field + mortar_weights[:, stencil_entry][:, None] * neighbour
    square = jnp.sum(airgap_field * airgap_field, axis=1, keepdims=True)
    field_flux = reluctivity[None, None] * (1.0 + square / (1.0 + square)) * airgap_field
    first_sample = lax.axis_index("tm") * sample_rows
    local_table = harmonic_basis(first_sample + jnp.arange(sample_rows, dtype=jnp.int32), KC) * (
        2.0 / NT
    )
    summed = lax.psum_scatter(
        jnp.einsum("jc,jabp->cabp", local_table, field_flux, precision=lax.Precision.HIGHEST),
        "tm",
        scatter_dimension=0,
        tiled=True,
    )
    return summed - source


def solution(mesh):
    in_specs = (
        P("tm", None, "azim", None),
        P("tm", None, "azim", None),
        P("tm"),
        P("tm", None),
        P("azim", None),
        P("tm", None, "azim", None),
    )
    out_specs = P("tm", None, "azim", None)
    return jax.shard_map(body, mesh=mesh, in_specs=in_specs, out_specs=out_specs, check_vma=False)
```

profile of v0, /device:TPU:0, one launch (start us, length us, event | category | flops | bytes accessed | tf_op | source)
XLA Modules:
  0.0 505.0 jit_solution(13953862369489338871)
XLA Ops:
  6.5 21.0 %copy.24 = f32[16,2,1,16384]{0,1,2,3:T(2,128)} copy(f32[16,2,1,16384]{3,2,1,0:T(1,128)} %param.6) | data formatting | bytes 4194304 | tf_op args[0]
  27.6 25.4 %reshape.162 = f32[4,1,131072]{2,1,0:T(1,128)} reshape(f32[16384,1,2,16]{3,2,1,0:T(2,128)} %bitcast.42) | data formatting | bytes 4194304
  52.9 5.2 %all-to-all-start = ((f32[4,1,131072]{2,1,0:T(1,128)}), f32[4,1,131072]{2,1,0:T(1,128)S(1)}, u32[]{:S(2)}, u32[]{:S(2)}) async-start(f32[4,1,131072]{2,1,0:T(1,128)} %reshape.162), calls=%async_computation | async-start | bytes 4194304 | tf_op jit(solution)/shard_map/all_to_all | solution.py:44
  58.1 0.3 reduce-scatter.2.cloned.1.call-start
  58.4 24.5 %all-to-all-done = f32[4,1,131072]{2,1,0:T(1,128)S(1)} async-done(((f32[4,1,131072]{2,1,0:T(1,128)}), f32[4,1,131072]{2,1,0:T(1,128)S(1)}, u32[]{:S(2)}, u32[]{:S(2)}) %all-to-all-start) | async-done | bytes 2097184 | tf_op jit(solution)/shard_map/all_to_all | solution.py:44
  83.0 0.0 copy-start.1
  83.0 1.3 copy-done.1
  84.3 0.5 broadcast.266
  84.8 7.7 %reduce.1 = f32[4,131072]{1,0:T(4,128)S(1)} reduce(f32[4,1,131072]{2,1,0:T(1,128)} %copy-done.1, f32[]{:T(128)} %broadcast.266), dimensions={1}, to_apply=%all_to_all.24.reduce_sub_computation | reduce | bytes 4194308 | tf_op jit(solution)/shard_map/all_to_all | solution.py:44
  92.5 29.0 %reshape.163 = f32[16384,1,2,16]{3,2,1,0:T(2,128)} reshape(f32[4,131072]{1,0:T(4,128)S(1)} %reduce.1) | data formatting | bytes 4194304
  121.6 20.6 %copy.31 = f32[16,2,1,4,4096]{4,3,0,1,2:T(4,128)S(1)} copy(f32[16,2,1,4,4096]{0,1,4,3,2:T(2,128)} %bitcast.41) | data formatting | bytes 4194304 | tf_op jit(solution)/shard_map/all_to_all | solution.py:44
  142.1 1.2 copy.26
  143.3 2.2 convolution_bitcast_fusion.1
  145.5 1.6 copy.27
  147.1 27.3 %all_to_all.33 = f32[64,2,1,4096]{3,1,2,0:T(2,128)S(1)} all-to-all(f32[64,2,1,4096]{3,1,2,0:T(2,128)S(1)} %copy.27), channel_id=1, replica_groups=mesh['tm'=4,'azim'=8] {'tm'}, dimensions={0} | all-to-all | bytes 4194304 | tf_op jit(solution)/shard_map/all_to_all | solution.py:47
  174.5 2.7 copy.28
  177.1 0.0 copy-start.6
  177.1 2.7 all_to_all.30
  179.9 0.0 copy-start
  179.9 0.1 collective-permute-start
  179.9 0.0 copy-done.6
  180.0 27.2 %collective-permute-done = f32[16,2,1,16384]{3,0,1,2:T(8,128)S(1)} collective-permute-done((f32[16,2,1,16384]{3,0,1,2:T(8,128)S(1)}, f32[16,2,1,16384]{3,0,1,2:T(8,128)S(1)}, u32[]{:S(2)}, u32[]{:S(2)}) %collective-permute-start) | collective-permute-done | bytes 2097184 | tf_op jit(solution)/shard_map/ppermute | solution.py:13
  207.2 0.0 copy-done
  207.2 0.0 copy-start.5
  207.2 1.9 broadcast_select_fusion
  209.1 0.1 collective-permute-start.1
  209.2 0.0 copy-done.5
  209.2 47.0 %collective-permute-done.1 = f32[16,2,1,16384]{3,0,1,2:T(8,128)} collective-permute-done((f32[16,2,1,16384]{3,0,1,2:T(8,128)S(1)}, f32[16,2,1,16384]{3,0,1,2:T(8,128)}, u32[]{:S(2)}, u32[]{:S(2)}) %collective-permute-start.1) | collective-permute-done | bytes 2097184 | tf_op jit(solution)/shard_map/ppermute | solution.py:13
  256.1 2.0 broadcast_select_fusion.1
  258.2 0.9 collective-permute-start.2
  259.0 0.0 copy-done.3
  259.0 0.1 fusion.55
  259.2 89.1 %collective-permute-done.2 = f32[16,2,1,16384]{3,0,1,2:T(8,128)S(1)} collective-permute-done((f32[16,2,1,16384]{3,0,1,2:T(8,128)S(1)}, f32[16,2,1,16384]{3,0,1,2:T(8,128)S(1)}, u32[]{:S(2)}, u32[]{:S(2)}) %collective-permute-start.2) | collective-permute-done | bytes 2097184 | tf_op jit(solution)/shard_map/ppermute | solution.py:13
  348.3 0.3 broadcast_select_fusion.2
  348.5 0.1 collective-permute-start.4
  348.6 0.5 collective-permute-start.3
  349.1 1.2 copy_bitcast_fusion
  350.3 44.1 %collective-permute-done.4 = f32[16,2,1,16384]{3,0,1,2:T(8,128)S(1)} collective-permute-done((f32[16,2,1,16384]{3,0,1,2:T(8,128)S(1)}, f32[16,2,1,16384]{3,0,1,2:T(8,128)S(1)}, u32[]{:S(2)}, u32[]{:S(2)}) %collective-permute-start.4) | collective-permute-done | bytes 2097184 | tf_op jit(solution)/shard_map/ppermute | solution.py:24
  394.4 1.7 collective-permute-done.3
  396.1 1.1 multiply_reduce_fusion
  397.3 0.0 copy-done.4
  397.3 0.2 fusion.3
  397.5 9.4 %convolution_bitcast_fusion = f32[64,2,1,16384]{3,0,1,2:T(8,128)} fusion(f32[16,2,1,16384]{3,0,1,2:T(8,128)S(1)} %get-tuple-element.6, f32[16,16384]{1,0:T(8,128)S(1)} %fusion.3, s32[16]{0:T(128)S(1)} %multiply_add_fusion.2, s32[64]{0:T(128)S(1)} %get-tuple-element.18, pred[64]{0:T(512)(128)(4,1)S(1)} %fusion.43), kind=kOutput, calls=%fused_computation | convolution fusion | flops 403193856 | bytes 11534720 | tf_op jit(solution)/shard_map/jc,jabp->cabp/dot_general | solution.py:72
  406.9 0.0 reduce-scatter.2.cloned.1.call-update
  406.9 84.7 %reduce-scatter.2.cloned.1.call-done = f32[16,2,1,16384]{3,0,1,2:T(8,128)} async-done(((f32[64,2,1,16384]{3,0,1,2:T(8,128)}), f32[16,2,1,16384]{3,0,1,2:T(8,128)}) %reduce-scatter.2.cloned.1.call-update) | async-done | bytes 2097168 | tf_op jit(solution)/shard_map/reduce_scatter | solution.py:71
  491.6 0.0 copy-done.2
  491.6 2.9 copy_subtract_fusion
  494.5 3.5 copy.30
  (8 shorter events, 0.0 us)
Async XLA Ops:
  52.9 30.0 %all-to-all-start = ((f32[4,1,131072]{2,1,0:T(1,128)}), f32[4,1,131072]{2,1,0:T(1,128)S(1)}, u32[]{:S(2)}, u32[]{:S(2)}) async-start(f32[4,1,131072]{2,1,0:T(1,128)} %reshape.162), calls=%async_computation | async-start | bytes 4194304 | tf_op jit(solution)/shard_map/all_to_all | solution.py:44
  58.1 433.5 %reduce-scatter.2.cloned.1.call-start = ((), (), s32[]{:S(2)}) async-start(), calls=%async_computation.3 | async-start | bytes 10485760 | tf_op jit(solution)/shard_map/reduce_scatter | solution.py:71
  83.0 1.3 copy-start.1
  177.1 2.8 copy-start.6
  179.9 27.3 %copy-start = (f32[16,2,1,16384]{3,0,1,2:T(8,128)}, f32[16,2,1,16384]{3,0,1,2:T(8,128)S(1)}, u32[]{:S(2)}) copy-start(f32[16,2,1,16384]{3,0,1,2:T(8,128)S(1)} %all_to_all.30) | copy-start | bytes 6291460
  179.9 27.3 %collective-permute-start = (f32[16,2,1,16384]{3,0,1,2:T(8,128)S(1)}, f32[16,2,1,16384]{3,0,1,2:T(8,128)S(1)}, u32[]{:S(2)}, u32[]{:S(2)}) collective-permute-start(f32[16,2,1,16384]{3,0,1,2:T(8,128)S(1)} %all_to_all.30), channel_id=1, source_target_pairs={{0,1},{1,2},{2,3},{3,4},{4,5},{5,6},{6,7},{7,0},{8,9},{9,10},{10,1... | collective-permute-start | bytes 6291464 | tf_op jit(solution)/shard_map/ppermute | solution.py:13
  207.2 2.0 copy-start.5
  209.1 47.1 %collective-permute-start.1 = (f32[16,2,1,16384]{3,0,1,2:T(8,128)S(1)}, f32[16,2,1,16384]{3,0,1,2:T(8,128)}, u32[]{:S(2)}, u32[]{:S(2)}) collective-permute-start(f32[16,2,1,16384]{3,0,1,2:T(8,128)S(1)} %broadcast_select_fusion), channel_id=1, source_target_pairs={{0,2},{1,3},{2,4},{3,5},{4,6},{5,7},{6,0},{7,1},{8,10},{9,11},{10,... | collective-permute-start | bytes 6291464 | tf_op jit(solution)/shard_map/ppermute | solution.py:13
  256.1 2.9 copy-start.3
  258.2 90.1 %collective-permute-start.2 = (f32[16,2,1,16384]{3,0,1,2:T(8,128)S(1)}, f32[16,2,1,16384]{3,0,1,2:T(8,128)S(1)}, u32[]{:S(2)}, u32[]{:S(2)}) collective-permute-start(f32[16,2,1,16384]{3,0,1,2:T(8,128)S(1)} %broadcast_select_fusion.1), channel_id=1, source_target_pairs={{0,4},{1,5},{2,6},{3,7},{4,0},{5,1},{6,2},{7,3},{8,12},{9,13},{10,... | collective-permute-start | bytes 6291464 | tf_op jit(solution)/shard_map/ppermute | solution.py:13
  348.5 45.9 %collective-permute-start.4 = (f32[16,2,1,16384]{3,0,1,2:T(8,128)S(1)}, f32[16,2,1,16384]{3,0,1,2:T(8,128)S(1)}, u32[]{:S(2)}, u32[]{:S(2)}) collective-permute-start(f32[16,2,1,16384]{3,0,1,2:T(8,128)S(1)} %broadcast_select_fusion.2), channel_id=1, source_target_pairs={{1,0},{2,1},{3,2},{4,3},{5,4},{6,5},{7,6},{0,7},{9,8},{10,9},{11,1... | collective-permute-start | bytes 6291464 | tf_op jit(solution)/shard_map/ppermute | solution.py:24
  348.6 47.5 %collective-permute-start.3 = (f32[16,2,1,16384]{3,0,1,2:T(8,128)S(1)}, f32[16,2,1,16384]{3,0,1,2:T(8,128)S(1)}, u32[]{:S(2)}, u32[]{:S(2)}) collective-permute-start(f32[16,2,1,16384]{3,0,1,2:T(8,128)S(1)} %broadcast_select_fusion.2), channel_id=1, source_target_pairs={{0,1},{1,2},{2,3},{3,4},{4,5},{5,6},{6,7},{7,0},{8,9},{9,10},{10,1... | collective-permute-start | bytes 6291464 | tf_op jit(solution)/shard_map/ppermute | solution.py:23
  396.1 1.2 copy-start.4
  406.9 84.7 %copy-start.2 = (f32[16,2,1,16384]{3,2,1,0:T(1,128)S(1)}, f32[16,2,1,16384]{3,2,1,0:T(1,128)}, u32[]{:S(2)}) copy-start(f32[16,2,1,16384]{3,2,1,0:T(1,128)} %param.11) | copy-start | bytes 6291460
Sparse Core Ops, SparseCore 0:
  407.0 84.5 reduce-scatter.1
where the time goes:
time: 511 us; the launch traced here: 505 us
  waiting for transfers between devices  318 us (62%)
  local copies, waits for them, and re-layouts  111 us (22%)
  blocking collectives  27.3 us (5%)
  other arithmetic  16.1 us (3%)
  between operations  13.8 us (3%)
  matrix products  11.6 us (2%)
  starting transfers between devices  6.98 us (1%)
    ppermute x3, waiting for transfers between devices, shifted(): return lax.ppermute(value, axis, pairs)  163 us
    reduce_scatter x1, waiting for transfers between devices, body(): lax.psum_scatter(jnp.einsum('jc,jabp->cabp', local_table, field_flux, pre...  84.7 us
    unnamed x18, local copies, waits for them, and re-layouts  78 us
    ppermute x1, waiting for transfers between devices, with_halo(): after = lax.ppermute(initial, axis, down)  44.1 us
    all_to_all x1, blocking collectives, body(): lax.all_to_all(spread, 'tm', split_axis=0, concat_axis=3, tiled=True)  27.3 us
    all_to_all x1, waiting for transfers between devices, body(): lax.all_to_all(rotor_coeffs, 'tm', split_axis=3, concat_axis=0, tiled=True)  24.5 us
    all_to_all x3, local copies, waits for them, and re-layouts, body(): lax.all_to_all(rotor_coeffs, 'tm', split_axis=3, concat_axis=0, tiled=True)  22.3 us
  transfers between devices with their start and end apart: 7, of which 7 were waited for; matrix products, arithmetic and copies ran while one was open for 0% of the time, Pallas kernels for 0%

commit v1 on v0

v1 whole, which is shorter than its diff:
```python
import functools

import jax
import jax.numpy as jnp
import ml_dtypes
import numpy as np
from jax import lax
from jax.experimental import pallas as pl
from jax.experimental.pallas import tpu as pltpu
from jax.sharding import PartitionSpec as P

LANES = 128
CHUNKS = 4
VMEM = pl.BlockSpec(memory_space=pltpu.VMEM)
SMEM = pl.BlockSpec(memory_space=pltpu.SMEM)
LIMIT = 48 * 1024 * 1024


def basis_table(sample_count, coefficient_count):
    column = np.arange(coefficient_count)
    order = 2 * (column // 2) + 1
    phase = order[None, :] * (2 * np.arange(sample_count)[:, None] + 1) % (4 * sample_count)
    angle = phase * (np.pi / (2 * sample_count))
    return np.where(column[None, :] % 2 == 0, np.cos(angle), np.sin(angle)).astype(np.float32)


def split_table(table):
    high = table.astype(ml_dtypes.bfloat16)
    low = (table - high.astype(np.float32)).astype(ml_dtypes.bfloat16)
    return np.concatenate([high, high, low], axis=1)


def table_dot(parts, value):
    high = value.astype(jnp.bfloat16)
    low = (value - high.astype(jnp.float32)).astype(jnp.bfloat16)
    return jnp.dot(
        parts, jnp.concatenate([high, low, high], axis=0), preferred_element_type=jnp.float32
    )


def call(kernel, out_shape, inputs, scratch=(), flops=0):
    size = sum(4 * np.prod(x.shape) for x in (*inputs, *out_shape))
    return pl.pallas_call(
        kernel,
        out_shape=[jax.ShapeDtypeStruct(x.shape, x.dtype) for x in out_shape],
        in_specs=[SMEM] + [VMEM] * (len(inputs) - 1),
        out_specs=[VMEM] * len(out_shape),
        scratch_shapes=list(scratch),
        compiler_params=pltpu.CompilerParams(vmem_limit_bytes=LIMIT),
        cost_estimate=pl.CostEstimate(flops=flops, bytes_accessed=int(size), transcendentals=0),
    )(*inputs)


def f32(*shape):
    return jax.ShapeDtypeStruct(shape, jnp.float32)


def xor_permute(value, axis, step):
    count = lax.axis_size(axis)
    return lax.ppermute(value, axis, [(i, i ^ step) for i in range(count)])


def pack_kernel(parts, widths, quarter_rows, place, x, *outs):
    outer = outs[0].shape[1]
    stride = x.shape[0] // outer
    for i in range(parts):
        first = (place[0] ^ i) * quarter_rows
        for comp in range(2):
            r = 0
            for g, width in enumerate(widths):
                for lane in range(0, width, LANES):
                    start = comp * (stride // 2) + first + r
                    outs[i * len(widths) + g][comp, :, lane : lane + LANES] = x[
                        pl.ds(start, outer, stride=stride), :
                    ]
                    r += 1


def gather_kernel(parts, chunk_count, place, *refs):
    pieces, outs = refs[:parts], refs[parts:]
    rows = pieces[0].shape[1]
    width = outs[0].shape[2]
    for i in range(parts):
        first = pl.multiple_of((place[0] ^ i) * rows, rows)
        for k in range(chunk_count):
            outs[k][:, pl.ds(first, rows), :] = pieces[i][:, :, k * width : (k + 1) * width]


def in_first(me, base, size, shifts):
    offset = (me - base + 1 + shifts) & (2 * size - 1)
    return ((base - 1 - shifts + offset - me) & (4 * size - 1)) == 0


def choose(me, size, shifts):
    clear = ~(size - 1)
    kept = in_first(me, me & clear, size, shifts)
    sent = in_first(me, (me ^ size) & clear, size, shifts)
    return kept, sent


def is_outer(me, count):
    return ((me // (count // 2)) ^ (me // (count // 4))) & 1 == 0


def sample_step(count, place, table, shifts, own, far, send, keep):
    me = place[1]
    kept, sent = choose(me, count // 4, shifts[0])
    parts = table[...]
    for comp in range(2):
        near_samples = table_dot(parts, own[comp])
        far_samples = table_dot(parts, far[comp])
        for lane in range(0, own.shape[2], LANES):
            here = slice(lane, lane + LANES)
            keep[comp, :, here] = jnp.where(kept, near_samples[:, here], far_samples[:, here])
            send[comp, :, here] = jnp.where(sent, near_samples[:, here], far_samples[:, here])


def first_kernel(count, place, table, shifts, own, arrived, following, send, keep):
    outer = is_outer(place[1], count)

    @pl.when(outer)
    def _():
        send[...] = following[...]
        keep[...] = own[...]

    @pl.when(jnp.logical_not(outer))
    def _():
        sample_step(count, place, table, shifts, own, arrived, send, keep)


def second_kernel(count, place, table, shifts, own, arrived, following, kept, send, keep):
    outer = is_outer(place[1], count)

    @pl.when(outer)
    def _():
        sample_step(count, place, table, shifts, own, arrived, send, keep)

    @pl.when(jnp.logical_not(outer))
    def _():
        send[...] = following[...]
        keep[...] = kept[...]


def middle_kernel(count, size, place, shifts, first, slot_a, slot_b, send, keep):
    me = place[1]
    outer = is_outer(me, count)
    kept, sent = choose(me, size, shifts[0])
    for comp in range(2):
        for lane in range(0, first.shape[2], LANES):
            here = slice(lane, lane + LANES)
            one = first[comp, :, here]
            two = jnp.where(outer, slot_a[comp, :, here], slot_b[comp, :, here])
            keep[comp, :, here] = jnp.where(kept, one, two)
            send[comp, :, here] = jnp.where(sent, one, two)


def flux_kernel(count, parts, row0, lane0, place, table, plan, iron, *refs):
    keep, slot_a, slot_b, far_keep, far_a, far_b = refs[:6]
    weights = refs[6 : 6 + parts]
    outs = refs[6 + parts : 6 + 2 * parts]
    flux, result, ordered = refs[6 + 2 * parts :]
    width = keep.shape[2]
    samples = keep.shape[1]
    rows = samples // parts
    tm, me = place[0], place[1]
    for i in range(parts):
        first = pl.multiple_of((tm ^ i) * rows, rows)
        ordered[:, pl.ds(first, rows), :] = weights[i][:, :, lane0 : lane0 + width]
    source = [((me + plan[1 + m] - plan[0]) ^ me) & 3 for m in range(2)]
    is_near = [s == 0 for s in source]
    is_two = [s == 2 for s in source]
    is_one = [s == 1 for s in source]
    quarter = tm * (iron.shape[0] // parts) + row0

    def fields(slot, far_slot):
        for lane in range(0, width, LANES):
            here = slice(lane, lane + LANES)
            weight = [ordered[m, :, here] for m in range(2)]
            field = []
            for comp in range(2):
                blocks = [ref[comp, :, here] for ref in (keep, slot, far_keep, far_slot)]
                terms = [
                    weight[m]
                    * jnp.where(
                        is_near[m],
                        blocks[0],
                        jnp.where(is_two[m], blocks[1], jnp.where(is_one[m], blocks[2], blocks[3])),
                    )
                    for m in range(2)
                ]
                field.append(terms[0] + terms[1])
            square = field[0] * field[0] + field[1] * field[1]
            gain = iron[pl.ds(quarter + lane // LANES, 1), :] * (1.0 + square / (1.0 + square))
            for comp in range(2):
                flux[:, comp * width + lane : comp * width + lane + LANES] = gain * field[comp]

    outer = is_outer(me, count)

    @pl.when(outer)
    def _():
        fields(slot_a, far_a)

    @pl.when(jnp.logical_not(outer))
    def _():
        fields(slot_b, far_b)

    result[...] = table_dot(table[...], flux[...])
    rows = result.shape[0] // parts
    for i in range(parts):
        first = pl.multiple_of((tm ^ i) * rows, rows)
        for comp in range(2):
            outs[i][comp] = result[pl.ds(first, rows), comp * width : (comp + 1) * width]


def finish_kernel(parts, chunks, quarter_rows, place, source, *refs):
    pieces, out = refs[:-1], refs[-1]
    outer, width = pieces[0].shape[1:]
    stride = source.shape[0] // outer
    for k in range(chunks):
        for i in range(parts):
            piece = pieces[k * parts + i]
            first = (place[0] ^ i) * quarter_rows + k * (width // LANES)
            for comp in range(2):
                for r in range(width // LANES):
                    here = pl.ds(comp * (stride // 2) + first + r, outer, stride=stride)
                    out[here, :] = piece[comp, :, r * LANES : (r + 1) * LANES] - source[here, :]


def body(rotor_coeffs, mortar_weights, block_shifts, stencil_offsets, reluctivity, source):
    parts, count = lax.axis_size("tm"), lax.axis_size("azim")
    coeff_rows, comps, _, nodes = rotor_coeffs.shape
    sample_rows = mortar_weights.shape[0]
    coeffs, samples = coeff_rows * parts, sample_rows * parts
    share = nodes // parts
    chunks = CHUNKS
    width = share // chunks
    share_rows = share // LANES
    place = jnp.stack([lax.axis_index("tm"), lax.axis_index("azim")]).astype(jnp.int32)
    table = basis_table(samples, coeffs)
    forward = jnp.asarray(split_table(table))
    backward = jnp.asarray(split_table(np.ascontiguousarray(table.T) * np.float32(2.0 / samples)))

    def as_rows(x):
        return x.reshape(-1, LANES)

    def pack(x, widths):
        outs = call(
            functools.partial(pack_kernel, parts, widths, share_rows),
            [f32(2, x.shape[0], w) for i in range(parts) for w in widths],
            (place, as_rows(x)),
        )
        return [outs[i * len(widths) : (i + 1) * len(widths)] for i in range(parts)]

    def swap(pieces):
        return [pieces[0]] + [xor_permute(pieces[i], "tm", i) for i in range(1, parts)]

    local_plan = jnp.concatenate([block_shifts[:, None], stencil_offsets], axis=1)
    plan = lax.all_gather(local_plan, "tm", axis=0, tiled=True)
    plan = jnp.broadcast_to(plan.T[:, :, None], (3, samples, LANES))

    packed = pack(rotor_coeffs, (width, share - width))
    head = swap([p[0] for p in packed])
    rest = swap([p[1] for p in packed])

    def gather(pieces, number):
        return call(
            functools.partial(gather_kernel, parts, number),
            [f32(2, coeffs, width)] * number,
            (place, *pieces),
        )

    own = gather(head, 1) + gather(rest, chunks - 1)
    mortar_weights, _ = lax.optimization_barrier((mortar_weights, rest[1]))
    weights = swap([p[0] for p in pack(mortar_weights, (share,))])

    half, fourth = count // 2, count // 4
    outer = [d for d in range(count) if is_outer(d, count)]
    inner = [d for d in range(count) if not is_outer(d, count)]
    coeff_a = [(d, d ^ half) for d in outer]
    coeff_b = [(d, d ^ half) for d in inner]
    sample_a = [(d, d ^ fourth) for d in inner]
    sample_b = [(d, d ^ fourth) for d in outer]
    block = f32(2, samples, width)
    dot_flops = 4 * 2 * samples * 3 * coeffs * width
    slots_a, slots_b, keeps = [], [], []
    send_a = send_b = own[0]
    for k in range(chunks):
        slots_a.append(lax.ppermute(send_a, "azim", coeff_a + (sample_a if k else [])))
        slots_b.append(lax.ppermute(send_b, "azim", coeff_b + (sample_b if k else [])))
        following = own[min(k + 1, chunks - 1)]
        send_a, kept = call(
            functools.partial(first_kernel, count),
            [block, block],
            (place, forward, plan, own[k], slots_a[k], following),
            flops=dot_flops,
        )
        send_b, kept = call(
            functools.partial(second_kernel, count),
            [block, block],
            (place, forward, plan, own[k], slots_b[k], following, kept),
            flops=dot_flops,
        )
        keeps.append(kept)
    slots_a.append(lax.ppermute(send_a, "azim", sample_a))
    slots_b.append(lax.ppermute(send_b, "azim", sample_b))

    pieces = []
    for k in range(chunks):
        keep, slot_a, slot_b = keeps[k], slots_a[k + 1], slots_b[k + 1]
        size = count // 8
        while size >= 2:
            send, keep = call(
                functools.partial(middle_kernel, count, size),
                [block, block],
                (place, plan, keep, slot_a, slot_b),
            )
            slot_a = slot_b = xor_permute(send, "azim", size)
            size //= 2
        far_keep = xor_permute(keep, "azim", 1)
        far_a = xor_permute(slot_a, "azim", 1)
        far_b = far_a if slot_b is slot_a else xor_permute(slot_b, "azim", 1)
        made = call(
            functools.partial(flux_kernel, count, parts, k * (width // LANES), k * width),
            [f32(2, coeff_rows, width)] * parts,
            (
                place,
                backward,
                plan,
                as_rows(reluctivity),
                keep,
                slot_a,
                slot_b,
                far_keep,
                far_a,
                far_b,
                *weights,
            ),
            scratch=(
                pltpu.VMEM((samples, 2 * width), jnp.float32),
                pltpu.VMEM((coeffs, 2 * width), jnp.float32),
                pltpu.VMEM((2, samples, width), jnp.float32),
            ),
            flops=dot_flops // 2,
        )
        pieces += swap(made)
    (out,) = call(
        functools.partial(finish_kernel, parts, chunks, share_rows),
        [f32(coeff_rows * comps * (nodes // LANES), LANES)],
        (place, as_rows(source), *pieces),
    )
    return out.reshape(source.shape)


def solution(mesh):
    wide = P("tm", None, "azim", None)
    in_specs = (wide, wide, P("tm"), P("tm", None), P("azim", None), wide)
    return jax.shard_map(body, mesh=mesh, in_specs=in_specs, out_specs=wide, check_vma=False)
```

time: 511 us -> 173 us (0.34); the launches traced: 505 us -> 172 us
  waiting for transfers between devices: 318 us -> 70.4 us
  local copies, waits for them, and re-layouts: 111 us -> 1.79 us
  starting transfers between devices: 6.98 us -> 61.7 us
  Pallas kernels: 0 us -> 21.4 us
  other arithmetic: 16.1 us -> 0.08 us
  between operations: 13.8 us -> 0.37 us
  matrix products: 11.6 us -> 0 us
  blocking collectives: 27.3 us -> 16.7 us
    ppermute x5 -> x43, waiting for transfers between devices: 209 us -> 70.4 us  [the longest x4 44.2 us: body(): lax.ppermute(send_b, 'azim', coeff_b + (sample_b if k else []))]
    reduce_scatter x1 -> x0, waiting for transfers between devices: 84.7 us -> none  [body(): lax.psum_scatter(jnp.einsum('jc,jabp->cabp', local_table, field_flux, pre...]
    unnamed x18 -> x17, local copies, waits for them, and re-layouts: 78 us -> 1.71 us
    ppermute x5 -> x43, starting transfers between devices: 1.53 us -> 61.7 us  [the longest x33 31.2 us: xor_permute(): return lax.ppermute(value, axis, [(i, i ^ step) for i in range(count)])]
    all_to_all x5 -> x0, local copies, waits for them, and re-layouts: 27.7 us -> none  [the longest x3 22.3 us: body(): lax.all_to_all(rotor_coeffs, 'tm', split_axis=3, concat_axis=0, tiled=True)]
    all_to_all x1 -> x0, blocking collectives: 27.3 us -> none  [body(): lax.all_to_all(spread, 'tm', split_axis=0, concat_axis=3, tiled=True)]
    all_to_all x1 -> x0, waiting for transfers between devices: 24.5 us -> none  [body(): lax.all_to_all(rotor_coeffs, 'tm', split_axis=3, concat_axis=0, tiled=True)]
    pallas_call x0 -> x17, Pallas kernels: none -> 21.4 us  [call(): pl.pallas_call(kernel, out_shape=[jax.ShapeDtypeStruct(x.shape, x.dtype)...]
  transfers between devices with their start and end apart: 7 -> 43, of which waited for: 7 -> 16; matrix products, arithmetic and copies ran while one was open for 0% -> 0% of each run, Pallas kernels for 0% -> 8%
where the time goes in v1:
time: 173 us; the launch traced here: 172 us
  waiting for transfers between devices  70.4 us (41%)
  starting transfers between devices  61.7 us (36%)
  Pallas kernels  21.4 us (12%)
  blocking collectives  16.7 us (10%)
  local copies, waits for them, and re-layouts  1.79 us (1%)
    ppermute x4, waiting for transfers between devices, body(): lax.ppermute(send_b, 'azim', coeff_b + (sample_b if k else []))  44.2 us
    ppermute x33, starting transfers between devices, xor_permute(): return lax.ppermute(value, axis, [(i, i ^ step) for i in range(count)])  31.2 us
    pallas_call x17, Pallas kernels, call(): pl.pallas_call(kernel, out_shape=[jax.ShapeDtypeStruct(x.shape, x.dtype)...  21.4 us
    all_gather x1, blocking collectives, body(): plan = lax.all_gather(local_plan, 'tm', axis=0, tiled=True)  16.7 us
    ppermute x33, waiting for transfers between devices, xor_permute(): return lax.ppermute(value, axis, [(i, i ^ step) for i in range(count)])  15.3 us
    ppermute x4, starting transfers between devices, body(): lax.ppermute(send_b, 'azim', coeff_b + (sample_b if k else []))  13.1 us
    ppermute x4, starting transfers between devices, body(): lax.ppermute(send_a, 'azim', coeff_a + (sample_a if k else []))  11.6 us
    ppermute x1, waiting for transfers between devices, body(): slots_a.append(lax.ppermute(send_a, 'azim', sample_a))  9.61 us
  transfers between devices with their start and end apart: 43, of which 16 were waited for; matrix products, arithmetic and copies ran while one was open for 0% of the time, Pallas kernels for 8%

profile of v1, /device:TPU:0, one launch (start us, length us, event | category | flops | bytes accessed | tf_op | source)
XLA Modules:
  0.0 172.4 jit_solution(2170223380926442866)
XLA Ops:
  0.1 1.6 copy-done.2
  1.7 2.6 %shard_map.82 = (f32[2,16,1024]{2,1,0:T(8,128)S(1)}, f32[2,16,3072]{2,1,0:T(8,128)S(1)}, f32[2,16,1024]{2,1,0:T(8,128)S(1)}, f32[2,16,3072]{2,1,0:T(8,128)}, f32...) custom-call(s32[2]{0:T(128)S(1)} %pad_add_fusion.place, ...), custom_call_target="tpu_custom_call" | custom-call | bytes 4194312 | tf_op jit(solution)/shard_map/pallas_call | solution.py:43
  4.3 2.9 %collective-permute-start = (f32[2,16,1024]{2,1,0:T(8,128)S(1)}, f32[2,16,1024]{2,1,0:T(8,128)S(1)}, u32[]{:S(2)}, u32[]{:S(2)}) collective-permute-start(f32[2,16,1024]{2,1,0:T(8,128)S(1)} %get-tuple-element.54), channel_id=1, source_target_pairs={{0,8},{8,0},{16,24},{24,16},{1,9},{9,1},{17,25},{25,17},{2,10},{10... | collective-permute-start | bytes 393224 | tf_op jit(solution)/shard_map/ppermute | solution.py:60
  7.2 1.5 collective-permute-start.1
  8.8 2.4 %collective-permute-done.refs_1_ = f32[2,16,1024]{2,1,0:T(8,128)S(1)} collective-permute-done((f32[2,16,1024]{2,1,0:T(8,128)S(1)}, f32[2,16,1024]{2,1,0:T(8,128)S(1)}, u32[]{:S(2)}, u32[]{:S(2)}) %collective-permute-start) | collective-permute-done | bytes 131104 | tf_op jit(solution)/shard_map/ppermute | solution.py:60
  11.2 3.9 %collective-permute-done.1.refs_2_ = f32[2,16,1024]{2,1,0:T(8,128)S(1)} collective-permute-done((f32[2,16,1024]{2,1,0:T(8,128)S(1)}, f32[2,16,1024]{2,1,0:T(8,128)S(1)}, u32[]{:S(2)}, u32[]{:S(2)}) %collective-permute-start.1) | collective-permute-done | bytes 131104 | tf_op jit(solution)/shard_map/ppermute | solution.py:60
  15.6 4.5 %collective-permute-start.7 = (f32[2,64,1024]{2,1,0:T(8,128)S(1)}, f32[2,64,1024]{2,1,0:T(8,128)S(1)}, u32[]{:S(2)}, u32[]{:S(2)}) collective-permute-start(f32[2,64,1024]{2,1,0:T(8,128)S(1)} %shard_map.83.own), channel_id=1, source_target_pairs={{0,4},{1,5},{6,2},{7,3},{8,12},{9,13},{14,10},{15,11},{16,20},{17,... | collective-permute-start | bytes 1572872 | tf_op jit(solution)/shard_map/ppermute | solution.py:288
  20.1 1.3 collective-permute-start.4
  22.3 1.4 collective-permute-start.6
  23.7 1.3 collective-permute-start.3
  25.0 16.7 %all-gather = s32[4,16,3]{1,2,0:T(4,128)S(1)} all-gather(s32[1,16,3]{1,2,0:T(4,128)S(1)} %add_bitcast_fusion), channel_id=1, replica_groups=mesh['tm'=4,'azim'=8] {'tm'}, dimensions={0}, use_global_device_ids=true | all-gather | bytes 960 | tf_op jit(solution)/shard_map/all_gather | solution.py:258
  43.3 11.1 %collective-permute-done.3.arrived = f32[2,64,1024]{2,1,0:T(8,128)S(1)} collective-permute-done((f32[2,64,1024]{2,1,0:T(8,128)S(1)}, f32[2,64,1024]{2,1,0:T(8,128)S(1)}, u32[]{:S(2)}, u32[]{:S(2)}) %collective-permute-start.3) | collective-permute-done | bytes 524320 | tf_op jit(solution)/shard_map/ppermute | solution.py:289
  54.4 1.0 shard_map.86
  56.1 3.3 %collective-permute-start.19 = (f32[2,64,1024]{2,1,0:T(8,128)S(1)}, f32[2,64,1024]{2,1,0:T(8,128)S(1)}, u32[]{:S(2)}, u32[]{:S(2)}) collective-permute-start(f32[2,64,1024]{2,1,0:T(8,128)S(1)} %get-tuple-element.78), channel_id=1, source_target_pairs={{0,4},{1,5},{6,2},{7,3},{2,0},{3,1},{4,6},{5,7},{8,12},{9,13},{14,... | collective-permute-start | bytes 1572872 | tf_op jit(solution)/shard_map/ppermute | solution.py:288
  59.4 1.8 %shard_map.87 = (f32[2,16,4096]{2,1,0:T(8,128)S(1)}, f32[2,16,4096]{2,1,0:T(8,128)S(1)}, f32[2,16,4096]{2,1,0:T(8,128)S(1)}, f32[2,16,4096]{2,1,0:T(8,128)S(1)}) custom-call(s32[2]{0:T(128)S(1)} %pad_add_fusion.place, f32[4096,128]{1,0:T(8,128)S(1)} %bitcast.15), custom_call_target="tpu_custom_call" | custom-call | bytes 4194312 | tf_op jit(solution)/shard_map/pallas_call | solution.py:43
  61.1 1.7 collective-permute-start.13
  62.8 18.5 %collective-permute-done.9.refs_2_.arrived = f32[2,64,1024]{2,1,0:T(8,128)S(1)} collective-permute-done((f32[2,64,1024]{2,1,0:T(8,128)S(1)}, f32[2,64,1024]{2,1,0:T(8,128)S(1)}, u32[]{:S(2)}, u32[]{:S(2)}) %collective-permute-start.9) | collective-permute-done | bytes 524320 | tf_op jit(solution)/shard_map/ppermute | solution.py:289
  81.4 1.0 shard_map.90
  82.5 3.1 %collective-permute-start.15 = (f32[2,16,4096]{2,1,0:T(8,128)S(1)}, f32[2,16,4096]{2,1,0:T(8,128)S(1)}, u32[]{:S(2)}, u32[]{:S(2)}) collective-permute-start(f32[2,16,4096]{2,1,0:T(8,128)S(1)} %get-tuple-element.70), channel_id=1, source_target_pairs={{0,24},{8,16},{16,8},{24,0},{1,25},{9,17},{17,9},{25,1},{2,26},{10... | collective-permute-start | bytes 1572872 | tf_op jit(solution)/shard_map/ppermute | solution.py:60
  86.8 5.8 %collective-permute-done.20.refs_2_.arrived = f32[2,64,1024]{2,1,0:T(8,128)S(1)} collective-permute-done((f32[2,64,1024]{2,1,0:T(8,128)S(1)}, f32[2,64,1024]{2,1,0:T(8,128)S(1)}, u32[]{:S(2)}, u32[]{:S(2)}) %collective-permute-start.20) | collective-permute-done | bytes 524320 | tf_op jit(solution)/shard_map/ppermute | solution.py:289
  92.6 3.7 %collective-permute-start.27 = (f32[2,64,1024]{2,1,0:T(8,128)S(1)}, f32[2,64,1024]{2,1,0:T(8,128)S(1)}, u32[]{:S(2)}, u32[]{:S(2)}) collective-permute-start(f32[2,64,1024]{2,1,0:T(8,128)S(1)} %get-tuple-element.87), channel_id=1, source_target_pairs={{0,4},{1,5},{6,2},{7,3},{2,0},{3,1},{4,6},{5,7},{8,12},{9,13},{14,... | collective-permute-start | bytes 1572872 | tf_op jit(solution)/shard_map/ppermute | solution.py:288
  96.2 1.0 shard_map.93
  97.3 11.7 %collective-permute-start.28 = (f32[2,64,1024]{2,1,0:T(8,128)S(1)}, f32[2,64,1024]{2,1,0:T(8,128)S(1)}, u32[]{:S(2)}, u32[]{:S(2)}) collective-permute-start(f32[2,64,1024]{2,1,0:T(8,128)S(1)} %get-tuple-element.88), channel_id=1, source_target_pairs={{2,6},{3,7},{4,0},{5,1},{0,2},{1,3},{6,4},{7,5},{10,14},{11,15},{1... | collective-permute-start | bytes 1572872 | tf_op jit(solution)/shard_map/ppermute | solution.py:289
  110.6 8.9 %collective-permute-done.28.refs_2_.arrived = f32[2,64,1024]{2,1,0:T(8,128)S(1)} collective-permute-done((f32[2,64,1024]{2,1,0:T(8,128)S(1)}, f32[2,64,1024]{2,1,0:T(8,128)S(1)}, u32[]{:S(2)}, u32[]{:S(2)}) %collective-permute-start.28) | collective-permute-done | bytes 524320 | tf_op jit(solution)/shard_map/ppermute | solution.py:289
  119.5 1.0 shard_map.96
  120.5 1.3 collective-permute-start.35
  121.8 4.6 %collective-permute-start.36 = (f32[2,64,1024]{2,1,0:T(8,128)S(1)}, f32[2,64,1024]{2,1,0:T(8,128)S(1)}, u32[]{:S(2)}, u32[]{:S(2)}) collective-permute-start(f32[2,64,1024]{2,1,0:T(8,128)S(1)} %get-tuple-element.96), channel_id=1, source_target_pairs={{0,2},{1,3},{6,4},{7,5},{8,10},{9,11},{14,12},{15,13},{16,18},{17,... | collective-permute-start | bytes 1572872 | tf_op jit(solution)/shard_map/ppermute | solution.py:305
  127.1 9.6 %collective-permute-done.35.refs_1_ = f32[2,64,1024]{2,1,0:T(8,128)S(1)} collective-permute-done((f32[2,64,1024]{2,1,0:T(8,128)S(1)}, f32[2,64,1024]{2,1,0:T(8,128)S(1)}, u32[]{:S(2)}, u32[]{:S(2)}) %collective-permute-start.35) | collective-permute-done | bytes 524320 | tf_op jit(solution)/shard_map/ppermute | solution.py:304
  136.7 1.2 collective-permute-done.36.refs_2_
  137.9 1.2 shard_map.88
  139.2 1.7 collective-permute-start.16
  141.4 1.2 shard_map.91
  142.6 1.4 shard_map.94
  144.0 1.2 collective-permute-done.16.refs_1_
  145.1 1.6 collective-permute-start.18
  147.1 1.6 collective-permute-start.25
  148.6 1.6 collective-permute-start.26
  150.6 1.2 shard_map.97
  152.4 1.0 collective-permute-start.33
  154.2 2.7 %collective-permute-start.34 = (f32[2,16,1024]{2,1,0:T(8,128)S(1)}, f32[2,16,1024]{2,1,0:T(8,128)S(1)}, u32[]{:S(2)}, u32[]{:S(2)}) collective-permute-start(f32[2,16,1024]{2,1,0:T(8,128)S(1)} %get-tuple-element.92), channel_id=1, source_target_pairs={{0,24},{8,16},{16,8},{24,0},{1,25},{9,17},{17,9},{25,1},{2,26},{10... | collective-permute-start | bytes 393224 | tf_op jit(solution)/shard_map/ppermute | solution.py:60
  156.9 1.2 collective-permute-start.40
  158.0 0.9 collective-permute-start.41
  159.8 2.7 %collective-permute-start.42 = (f32[2,16,1024]{2,1,0:T(8,128)S(1)}, f32[2,16,1024]{2,1,0:T(8,128)S(1)}, u32[]{:S(2)}, u32[]{:S(2)}) collective-permute-start(f32[2,16,1024]{2,1,0:T(8,128)S(1)} %get-tuple-element.100), channel_id=1, source_target_pairs={{0,24},{8,16},{16,8},{24,0},{1,25},{9,17},{17,9},{25,1},{2,26},{10... | collective-permute-start | bytes 393224 | tf_op jit(solution)/shard_map/ppermute | solution.py:60
  162.5 1.2 collective-permute-done.34.refs_11_
  163.7 1.8 %collective-permute-done.40.refs_13_ = f32[2,16,1024]{2,1,0:T(8,128)S(1)} collective-permute-done((f32[2,16,1024]{2,1,0:T(8,128)S(1)}, f32[2,16,1024]{2,1,0:T(8,128)S(1)}, u32[]{:S(2)}, u32[]{:S(2)}) %collective-permute-start.40) | collective-permute-done | bytes 131104 | tf_op jit(solution)/shard_map/ppermute | solution.py:60
  165.4 1.0 collective-permute-done.41.refs_14_
  166.5 1.5 collective-permute-done.42.refs_15_
  168.0 4.4 %shard_map.98 = f32[4096,128]{1,0:T(8,128)} custom-call(s32[2]{0:T(128)S(1)} %pad_add_fusion.place, f32[4096,128]{1,0:T(8,128)S(1)} %bitcast.13, f32[2,16,1024]{2,1,0:T(8,128)S(1)} %get-tuple-element.71.refs_0_, f32[2,16,1024]{2,1,0:T(8,128)S(1)} %collective-permute-done.16.refs_1_, f32[2,16,1024]{2,1,0:T(8,128)S(1)} %collective-permute-done.17.refs_2_, ...), custom_call_target="tpu_custom_call" | custom-call | bytes 6291464 | tf_op jit(solution)/shard_map/pallas_call | solution.py:43
  (77 shorter events, 10.9 us)
Async XLA Ops:
  0.0 25.0 %copy-start.6 = (s32[16,2]{0,1:T(2,128)S(1)}, s32[16,2]{0,1:T(2,128)}, u32[]{:S(2)}) copy-start(s32[16,2]{0,1:T(2,128)} %param.11) | copy-start | bytes 388
  0.0 25.0 %copy-start.7 = (s32[16]{0:T(128)S(1)}, s32[16]{0:T(128)}, u32[]{:S(2)}) copy-start(s32[16]{0:T(128)} %param.10) | copy-start | bytes 196
  1.7 40.9 %copy-start = (bf16[64,192]{1,0:T(8,128)(2,1)S(1)}, bf16[64,192]{1,0:T(8,128)(2,1)}, u32[]{:S(2)}) copy-start(bf16[64,192]{1,0:T(8,128)(2,1)} %constant.12.clone.table) | copy-start | bytes 73732
  4.3 6.8 %collective-permute-start = (f32[2,16,1024]{2,1,0:T(8,128)S(1)}, f32[2,16,1024]{2,1,0:T(8,128)S(1)}, u32[]{:S(2)}, u32[]{:S(2)}) collective-permute-start(f32[2,16,1024]{2,1,0:T(8,128)S(1)} %get-tuple-element.54), channel_id=1, source_target_pairs={{0,8},{8,0},{16,24},{24,16},{1,9},{9,1},{17,25},{25,17},{2,10},{10... | collective-permute-start | bytes 393224 | tf_op jit(solution)/shard_map/ppermute | solution.py:60
  7.2 7.8 %collective-permute-start.1 = (f32[2,16,1024]{2,1,0:T(8,128)S(1)}, f32[2,16,1024]{2,1,0:T(8,128)S(1)}, u32[]{:S(2)}, u32[]{:S(2)}) collective-permute-start(f32[2,16,1024]{2,1,0:T(8,128)S(1)} %get-tuple-element.55), channel_id=1, source_target_pairs={{0,16},{8,24},{16,0},{24,8},{1,17},{9,25},{17,1},{25,9},{2,18},{10... | collective-permute-start | bytes 393224 | tf_op jit(solution)/shard_map/ppermute | solution.py:60
  8.8 6.3 %collective-permute-start.2 = (f32[2,16,1024]{2,1,0:T(8,128)S(1)}, f32[2,16,1024]{2,1,0:T(8,128)S(1)}, u32[]{:S(2)}, u32[]{:S(2)}) collective-permute-start(f32[2,16,1024]{2,1,0:T(8,128)S(1)} %get-tuple-element.56), channel_id=1, source_target_pairs={{0,24},{8,16},{16,8},{24,0},{1,25},{9,17},{17,9},{25,1},{2,26},{10... | collective-permute-start | bytes 393224 | tf_op jit(solution)/shard_map/ppermute | solution.py:60
  15.6 26.9 %collective-permute-start.7 = (f32[2,64,1024]{2,1,0:T(8,128)S(1)}, f32[2,64,1024]{2,1,0:T(8,128)S(1)}, u32[]{:S(2)}, u32[]{:S(2)}) collective-permute-start(f32[2,64,1024]{2,1,0:T(8,128)S(1)} %shard_map.83.own), channel_id=1, source_target_pairs={{0,4},{1,5},{6,2},{7,3},{8,12},{9,13},{14,10},{15,11},{16,20},{17,... | collective-permute-start | bytes 1572872 | tf_op jit(solution)/shard_map/ppermute | solution.py:288
  20.1 21.6 %collective-permute-start.4 = (f32[2,16,3072]{2,1,0:T(8,128)}, f32[2,16,3072]{2,1,0:T(8,128)S(1)}, u32[]{:S(2)}, u32[]{:S(2)}) collective-permute-start(f32[2,16,3072]{2,1,0:T(8,128)} %get-tuple-element.58), channel_id=1, source_target_pairs={{0,8},{8,0},{16,24},{24,16},{1,9},{9,1},{17,25},{25,17},{2,10},{10... | collective-permute-start | bytes 1179656 | tf_op jit(solution)/shard_map/ppermute | solution.py:60
  21.4 20.4 %collective-permute-start.5 = (f32[2,16,3072]{2,1,0:T(8,128)}, f32[2,16,3072]{2,1,0:T(8,128)S(1)}, u32[]{:S(2)}, u32[]{:S(2)}) collective-permute-start(f32[2,16,3072]{2,1,0:T(8,128)} %get-tuple-element.59), channel_id=1, source_target_pairs={{0,16},{8,24},{16,0},{24,8},{1,17},{9,25},{17,1},{25,9},{2,18},{10... | collective-permute-start | bytes 1179656 | tf_op jit(solution)/shard_map/ppermute | solution.py:60
  22.3 19.5 %collective-permute-start.6 = (f32[2,16,3072]{2,1,0:T(8,128)}, f32[2,16,3072]{2,1,0:T(8,128)S(1)}, u32[]{:S(2)}, u32[]{:S(2)}) collective-permute-start(f32[2,16,3072]{2,1,0:T(8,128)} %get-tuple-element.60), channel_id=1, source_target_pairs={{0,24},{8,16},{16,8},{24,0},{1,25},{9,17},{17,9},{25,1},{2,26},{10... | collective-permute-start | bytes 1179656 | tf_op jit(solution)/shard_map/ppermute | solution.py:60
  23.7 30.7 %collective-permute-start.3 = (f32[2,64,1024]{2,1,0:T(8,128)S(1)}, f32[2,64,1024]{2,1,0:T(8,128)S(1)}, u32[]{:S(2)}, u32[]{:S(2)}) collective-permute-start(f32[2,64,1024]{2,1,0:T(8,128)S(1)} %shard_map.83.own), channel_id=1, source_target_pairs={{2,6},{3,7},{4,0},{5,1},{10,14},{11,15},{12,8},{13,9},{18,22},{19,... | collective-permute-start | bytes 1572872 | tf_op jit(solution)/shard_map/ppermute | solution.py:289
  43.2 12.2 %collective-permute-start.8 = (f32[2,64,1024]{2,1,0:T(8,128)S(1)}, f32[2,64,1024]{2,1,0:T(8,128)S(1)}, u32[]{:S(2)}, u32[]{:S(2)}) collective-permute-start(f32[2,64,1024]{2,1,0:T(8,128)S(1)} %get-tuple-element.64), channel_id=1, source_target_pairs={{0,4},{1,5},{6,2},{7,3},{2,0},{3,1},{4,6},{5,7},{8,12},{9,13},{14,... | collective-permute-start | bytes 1572872 | tf_op jit(solution)/shard_map/ppermute | solution.py:288
  55.3 26.0 %collective-permute-start.9 = (f32[2,64,1024]{2,1,0:T(8,128)S(1)}, f32[2,64,1024]{2,1,0:T(8,128)S(1)}, u32[]{:S(2)}, u32[]{:S(2)}) collective-permute-start(f32[2,64,1024]{2,1,0:T(8,128)S(1)} %get-tuple-element.65), channel_id=1, source_target_pairs={{2,6},{3,7},{4,0},{5,1},{0,2},{1,3},{6,4},{7,5},{10,14},{11,15},{1... | collective-permute-start | bytes 1572872 | tf_op jit(solution)/shard_map/ppermute | solution.py:289
  56.1 29.5 %collective-permute-start.19 = (f32[2,64,1024]{2,1,0:T(8,128)S(1)}, f32[2,64,1024]{2,1,0:T(8,128)S(1)}, u32[]{:S(2)}, u32[]{:S(2)}) collective-permute-start(f32[2,64,1024]{2,1,0:T(8,128)S(1)} %get-tuple-element.78), channel_id=1, source_target_pairs={{0,4},{1,5},{6,2},{7,3},{2,0},{3,1},{4,6},{5,7},{8,12},{9,13},{14,... | collective-permute-start | bytes 1572872 | tf_op jit(solution)/shard_map/ppermute | solution.py:288
  61.1 25.1 %collective-permute-start.13 = (f32[2,16,4096]{2,1,0:T(8,128)S(1)}, f32[2,16,4096]{2,1,0:T(8,128)S(1)}, u32[]{:S(2)}, u32[]{:S(2)}) collective-permute-start(f32[2,16,4096]{2,1,0:T(8,128)S(1)} %get-tuple-element.68), channel_id=1, source_target_pairs={{0,8},{8,0},{16,24},{24,16},{1,9},{9,1},{17,25},{25,17},{2,10},{10... | collective-permute-start | bytes 1572872 | tf_op jit(solution)/shard_map/ppermute | solution.py:60
  82.3 10.2 %collective-permute-start.20 = (f32[2,64,1024]{2,1,0:T(8,128)S(1)}, f32[2,64,1024]{2,1,0:T(8,128)S(1)}, u32[]{:S(2)}, u32[]{:S(2)}) collective-permute-start(f32[2,64,1024]{2,1,0:T(8,128)S(1)} %get-tuple-element.79), channel_id=1, source_target_pairs={{2,6},{3,7},{4,0},{5,1},{0,2},{1,3},{6,4},{7,5},{10,14},{11,15},{1... | collective-permute-start | bytes 1572872 | tf_op jit(solution)/shard_map/ppermute | solution.py:289
  82.4 14.9 %collective-permute-start.14 = (f32[2,16,4096]{2,1,0:T(8,128)S(1)}, f32[2,16,4096]{2,1,0:T(8,128)S(1)}, u32[]{:S(2)}, u32[]{:S(2)}) collective-permute-start(f32[2,16,4096]{2,1,0:T(8,128)S(1)} %get-tuple-element.69), channel_id=1, source_target_pairs={{0,16},{8,24},{16,0},{24,8},{1,17},{9,25},{17,1},{25,9},{2,18},{10... | collective-permute-start | bytes 1572872 | tf_op jit(solution)/shard_map/ppermute | solution.py:60
  82.5 26.5 %collective-permute-start.15 = (f32[2,16,4096]{2,1,0:T(8,128)S(1)}, f32[2,16,4096]{2,1,0:T(8,128)S(1)}, u32[]{:S(2)}, u32[]{:S(2)}) collective-permute-start(f32[2,16,4096]{2,1,0:T(8,128)S(1)} %get-tuple-element.70), channel_id=1, source_target_pairs={{0,24},{8,16},{16,8},{24,0},{1,25},{9,17},{17,9},{25,1},{2,26},{10... | collective-permute-start | bytes 1572872 | tf_op jit(solution)/shard_map/ppermute | solution.py:60
  85.6 23.4 %collective-permute-start.10 = (f32[2,64,1024]{2,1,0:T(8,128)S(1)}, f32[2,64,1024]{2,1,0:T(8,128)S(1)}, u32[]{:S(2)}, u32[]{:S(2)}) collective-permute-start(f32[2,64,1024]{2,1,0:T(8,128)S(1)} %get-tuple-element.63.refs_0_), channel_id=1, source_target_pairs={{0,1},{1,0},{2,3},{3,2},{4,5},{5,4},{6,7},{7,6},{8,9},{9,8},{10,11... | collective-permute-start | bytes 1572872 | tf_op jit(solution)/shard_map/ppermute | solution.py:60
  86.2 23.2 %collective-permute-start.11 = (f32[2,64,1024]{2,1,0:T(8,128)S(1)}, f32[2,64,1024]{2,1,0:T(8,128)S(1)}, u32[]{:S(2)}, u32[]{:S(2)}) collective-permute-start(f32[2,64,1024]{2,1,0:T(8,128)S(1)} %collective-permute-done.8.refs_1_.arrived), channel_id=1, source_target_pairs={{0,1},{1,0},{2,3},{3,2},{4,5},{5,4},{6,7},{7,6},{8,9},{9,8},{10,11... | collective-permute-start | bytes 1572872 | tf_op jit(solution)/shard_map/ppermute | solution.py:60
  92.6 17.0 %collective-permute-start.27 = (f32[2,64,1024]{2,1,0:T(8,128)S(1)}, f32[2,64,1024]{2,1,0:T(8,128)S(1)}, u32[]{:S(2)}, u32[]{:S(2)}) collective-permute-start(f32[2,64,1024]{2,1,0:T(8,128)S(1)} %get-tuple-element.87), channel_id=1, source_target_pairs={{0,4},{1,5},{6,2},{7,3},{2,0},{3,1},{4,6},{5,7},{8,12},{9,13},{14,... | collective-permute-start | bytes 1572872 | tf_op jit(solution)/shard_map/ppermute | solution.py:288
  97.2 40.7 %copy-start.4 = (f32[1,16384]{1,0:T(1,128)S(1)}, f32[1,16384]{1,0:T(1,128)}, u32[]{:S(2)}) copy-start(f32[1,16384]{1,0:T(1,128)} %param.12) | copy-start | bytes 196612
  97.2 40.7 %copy-start.5 = (bf16[64,192]{1,0:T(8,128)(2,1)S(1)}, bf16[64,192]{1,0:T(8,128)(2,1)}, u32[]{:S(2)}) copy-start(bf16[64,192]{1,0:T(8,128)(2,1)} %constant.13.clone.table) | copy-start | bytes 73732
  97.3 22.2 %collective-permute-start.28 = (f32[2,64,1024]{2,1,0:T(8,128)S(1)}, f32[2,64,1024]{2,1,0:T(8,128)S(1)}, u32[]{:S(2)}, u32[]{:S(2)}) collective-permute-start(f32[2,64,1024]{2,1,0:T(8,128)S(1)} %get-tuple-element.88), channel_id=1, source_target_pairs={{2,6},{3,7},{4,0},{5,1},{0,2},{1,3},{6,4},{7,5},{10,14},{11,15},{1... | collective-permute-start | bytes 1572872 | tf_op jit(solution)/shard_map/ppermute | solution.py:289
  108.9 11.5 %collective-permute-start.12 = (f32[2,64,1024]{2,1,0:T(8,128)S(1)}, f32[2,64,1024]{2,1,0:T(8,128)S(1)}, u32[]{:S(2)}, u32[]{:S(2)}) collective-permute-start(f32[2,64,1024]{2,1,0:T(8,128)S(1)} %collective-permute-done.9.refs_2_.arrived), channel_id=1, source_target_pairs={{0,1},{1,0},{2,3},{3,2},{4,5},{5,4},{6,7},{7,6},{8,9},{9,8},{10,11... | collective-permute-start | bytes 1572872 | tf_op jit(solution)/shard_map/ppermute | solution.py:60
  109.0 12.8 %collective-permute-start.21 = (f32[2,64,1024]{2,1,0:T(8,128)S(1)}, f32[2,64,1024]{2,1,0:T(8,128)S(1)}, u32[]{:S(2)}, u32[]{:S(2)}) collective-permute-start(f32[2,64,1024]{2,1,0:T(8,128)S(1)} %get-tuple-element.77.refs_0_), channel_id=1, source_target_pairs={{0,1},{1,0},{2,3},{3,2},{4,5},{5,4},{6,7},{7,6},{8,9},{9,8},{10,11... | collective-permute-start | bytes 1572872 | tf_op jit(solution)/shard_map/ppermute | solution.py:60
  109.5 17.0 %collective-permute-start.22 = (f32[2,64,1024]{2,1,0:T(8,128)S(1)}, f32[2,64,1024]{2,1,0:T(8,128)S(1)}, u32[]{:S(2)}, u32[]{:S(2)}) collective-permute-start(f32[2,64,1024]{2,1,0:T(8,128)S(1)} %collective-permute-done.19.refs_1_.arrived), channel_id=1, source_target_pairs={{0,1},{1,0},{2,3},{3,2},{4,5},{5,4},{6,7},{7,6},{8,9},{9,8},{10,11... | collective-permute-start | bytes 1572872 | tf_op jit(solution)/shard_map/ppermute | solution.py:60
  109.5 17.0 %collective-permute-start.23 = (f32[2,64,1024]{2,1,0:T(8,128)S(1)}, f32[2,64,1024]{2,1,0:T(8,128)S(1)}, u32[]{:S(2)}, u32[]{:S(2)}) collective-permute-start(f32[2,64,1024]{2,1,0:T(8,128)S(1)} %collective-permute-done.20.refs_2_.arrived), channel_id=1, source_target_pairs={{0,1},{1,0},{2,3},{3,2},{4,5},{5,4},{6,7},{7,6},{8,9},{9,8},{10,11... | collective-permute-start | bytes 1572872 | tf_op jit(solution)/shard_map/ppermute | solution.py:60
  119.5 7.5 %collective-permute-start.29 = (f32[2,64,1024]{2,1,0:T(8,128)S(1)}, f32[2,64,1024]{2,1,0:T(8,128)S(1)}, u32[]{:S(2)}, u32[]{:S(2)}) collective-permute-start(f32[2,64,1024]{2,1,0:T(8,128)S(1)} %get-tuple-element.86.refs_0_), channel_id=1, source_target_pairs={{0,1},{1,0},{2,3},{3,2},{4,5},{5,4},{6,7},{7,6},{8,9},{9,8},{10,11... | collective-permute-start | bytes 1572872 | tf_op jit(solution)/shard_map/ppermute | solution.py:60
  120.5 16.2 %collective-permute-start.35 = (f32[2,64,1024]{2,1,0:T(8,128)S(1)}, f32[2,64,1024]{2,1,0:T(8,128)S(1)}, u32[]{:S(2)}, u32[]{:S(2)}) collective-permute-start(f32[2,64,1024]{2,1,0:T(8,128)S(1)} %get-tuple-element.95), channel_id=1, source_target_pairs={{2,0},{3,1},{4,6},{5,7},{10,8},{11,9},{12,14},{13,15},{18,16},{19,... | collective-permute-start | bytes 1572872 | tf_op jit(solution)/shard_map/ppermute | solution.py:304
  121.8 16.1 %collective-permute-start.36 = (f32[2,64,1024]{2,1,0:T(8,128)S(1)}, f32[2,64,1024]{2,1,0:T(8,128)S(1)}, u32[]{:S(2)}, u32[]{:S(2)}) collective-permute-start(f32[2,64,1024]{2,1,0:T(8,128)S(1)} %get-tuple-element.96), channel_id=1, source_target_pairs={{0,2},{1,3},{6,4},{7,5},{8,10},{9,11},{14,12},{15,13},{16,18},{17,... | collective-permute-start | bytes 1572872 | tf_op jit(solution)/shard_map/ppermute | solution.py:305
  126.4 12.7 %collective-permute-start.30 = (f32[2,64,1024]{2,1,0:T(8,128)S(1)}, f32[2,64,1024]{2,1,0:T(8,128)S(1)}, u32[]{:S(2)}, u32[]{:S(2)}) collective-permute-start(f32[2,64,1024]{2,1,0:T(8,128)S(1)} %collective-permute-done.27.refs_1_.arrived), channel_id=1, source_target_pairs={{0,1},{1,0},{2,3},{3,2},{4,5},{5,4},{6,7},{7,6},{8,9},{9,8},{10,11... | collective-permute-start | bytes 1572872 | tf_op jit(solution)/shard_map/ppermute | solution.py:60
  126.5 14.4 %collective-permute-start.31 = (f32[2,64,1024]{2,1,0:T(8,128)S(1)}, f32[2,64,1024]{2,1,0:T(8,128)S(1)}, u32[]{:S(2)}, u32[]{:S(2)}) collective-permute-start(f32[2,64,1024]{2,1,0:T(8,128)S(1)} %collective-permute-done.28.refs_2_.arrived), channel_id=1, source_target_pairs={{0,1},{1,0},{2,3},{3,2},{4,5},{5,4},{6,7},{7,6},{8,9},{9,8},{10,11... | collective-permute-start | bytes 1572872 | tf_op jit(solution)/shard_map/ppermute | solution.py:60
  127.0 20.0 %collective-permute-start.37 = (f32[2,64,1024]{2,1,0:T(8,128)S(1)}, f32[2,64,1024]{2,1,0:T(8,128)S(1)}, u32[]{:S(2)}, u32[]{:S(2)}) collective-permute-start(f32[2,64,1024]{2,1,0:T(8,128)S(1)} %get-tuple-element.94.refs_0_), channel_id=1, source_target_pairs={{0,1},{1,0},{2,3},{3,2},{4,5},{5,4},{6,7},{7,6},{8,9},{9,8},{10,11... | collective-permute-start | bytes 1572872 | tf_op jit(solution)/shard_map/ppermute | solution.py:60
  136.7 11.9 %collective-permute-start.38 = (f32[2,64,1024]{2,1,0:T(8,128)S(1)}, f32[2,64,1024]{2,1,0:T(8,128)S(1)}, u32[]{:S(2)}, u32[]{:S(2)}) collective-permute-start(f32[2,64,1024]{2,1,0:T(8,128)S(1)} %collective-permute-done.35.refs_1_), channel_id=1, source_target_pairs={{0,1},{1,0},{2,3},{3,2},{4,5},{5,4},{6,7},{7,6},{8,9},{9,8},{10,11... | collective-permute-start | bytes 1572872 | tf_op jit(solution)/shard_map/ppermute | solution.py:60
  137.9 12.3 %collective-permute-start.39 = (f32[2,64,1024]{2,1,0:T(8,128)S(1)}, f32[2,64,1024]{2,1,0:T(8,128)S(1)}, u32[]{:S(2)}, u32[]{:S(2)}) collective-permute-start(f32[2,64,1024]{2,1,0:T(8,128)S(1)} %collective-permute-done.36.refs_2_), channel_id=1, source_target_pairs={{0,1},{1,0},{2,3},{3,2},{4,5},{5,4},{6,7},{7,6},{8,9},{9,8},{10,11... | collective-permute-start | bytes 1572872 | tf_op jit(solution)/shard_map/ppermute | solution.py:60
  139.2 6.0 %collective-permute-start.16 = (f32[2,16,1024]{2,1,0:T(8,128)S(1)}, f32[2,16,1024]{2,1,0:T(8,128)S(1)}, u32[]{:S(2)}, u32[]{:S(2)}) collective-permute-start(f32[2,16,1024]{2,1,0:T(8,128)S(1)} %get-tuple-element.72), channel_id=1, source_target_pairs={{0,8},{8,0},{16,24},{24,16},{1,9},{9,1},{17,25},{25,17},{2,10},{10... | collective-permute-start | bytes 393224 | tf_op jit(solution)/shard_map/ppermute | solution.py:60
  140.9 5.8 %collective-permute-start.17 = (f32[2,16,1024]{2,1,0:T(8,128)S(1)}, f32[2,16,1024]{2,1,0:T(8,128)S(1)}, u32[]{:S(2)}, u32[]{:S(2)}) collective-permute-start(f32[2,16,1024]{2,1,0:T(8,128)S(1)} %get-tuple-element.73), channel_id=1, source_target_pairs={{0,16},{8,24},{16,0},{24,8},{1,17},{9,25},{17,1},{25,9},{2,18},{10... | collective-permute-start | bytes 393224 | tf_op jit(solution)/shard_map/ppermute | solution.py:60
  145.1 7.3 %collective-permute-start.18 = (f32[2,16,1024]{2,1,0:T(8,128)S(1)}, f32[2,16,1024]{2,1,0:T(8,128)S(1)}, u32[]{:S(2)}, u32[]{:S(2)}) collective-permute-start(f32[2,16,1024]{2,1,0:T(8,128)S(1)} %get-tuple-element.74), channel_id=1, source_target_pairs={{0,24},{8,16},{16,8},{24,0},{1,25},{9,17},{17,9},{25,1},{2,26},{10... | collective-permute-start | bytes 393224 | tf_op jit(solution)/shard_map/ppermute | solution.py:60
  146.7 7.5 %collective-permute-start.24 = (f32[2,16,1024]{2,1,0:T(8,128)S(1)}, f32[2,16,1024]{2,1,0:T(8,128)S(1)}, u32[]{:S(2)}, u32[]{:S(2)}) collective-permute-start(f32[2,16,1024]{2,1,0:T(8,128)S(1)} %get-tuple-element.81), channel_id=1, source_target_pairs={{0,8},{8,0},{16,24},{24,16},{1,9},{9,1},{17,25},{25,17},{2,10},{10... | collective-permute-start | bytes 393224 | tf_op jit(solution)/shard_map/ppermute | solution.py:60
  147.1 9.8 %collective-permute-start.25 = (f32[2,16,1024]{2,1,0:T(8,128)S(1)}, f32[2,16,1024]{2,1,0:T(8,128)S(1)}, u32[]{:S(2)}, u32[]{:S(2)}) collective-permute-start(f32[2,16,1024]{2,1,0:T(8,128)S(1)} %get-tuple-element.82), channel_id=1, source_target_pairs={{0,16},{8,24},{16,0},{24,8},{1,17},{9,25},{17,1},{25,9},{2,18},{10... | collective-permute-start | bytes 393224 | tf_op jit(solution)/shard_map/ppermute | solution.py:60
  148.6 9.4 %collective-permute-start.26 = (f32[2,16,1024]{2,1,0:T(8,128)S(1)}, f32[2,16,1024]{2,1,0:T(8,128)S(1)}, u32[]{:S(2)}, u32[]{:S(2)}) collective-permute-start(f32[2,16,1024]{2,1,0:T(8,128)S(1)} %get-tuple-element.83), channel_id=1, source_target_pairs={{0,24},{8,16},{16,8},{24,0},{1,25},{9,17},{17,9},{25,1},{2,26},{10... | collective-permute-start | bytes 393224 | tf_op jit(solution)/shard_map/ppermute | solution.py:60
  150.2 9.6 %collective-permute-start.32 = (f32[2,16,1024]{2,1,0:T(8,128)S(1)}, f32[2,16,1024]{2,1,0:T(8,128)S(1)}, u32[]{:S(2)}, u32[]{:S(2)}) collective-permute-start(f32[2,16,1024]{2,1,0:T(8,128)S(1)} %get-tuple-element.90), channel_id=1, source_target_pairs={{0,8},{8,0},{16,24},{24,16},{1,9},{9,1},{17,25},{25,17},{2,10},{10... | collective-permute-start | bytes 393224 | tf_op jit(solution)/shard_map/ppermute | solution.py:60
  152.4 10.1 %collective-permute-start.33 = (f32[2,16,1024]{2,1,0:T(8,128)S(1)}, f32[2,16,1024]{2,1,0:T(8,128)S(1)}, u32[]{:S(2)}, u32[]{:S(2)}) collective-permute-start(f32[2,16,1024]{2,1,0:T(8,128)S(1)} %get-tuple-element.91), channel_id=1, source_target_pairs={{0,16},{8,24},{16,0},{24,8},{1,17},{9,25},{17,1},{25,9},{2,18},{10... | collective-permute-start | bytes 393224 | tf_op jit(solution)/shard_map/ppermute | solution.py:60
  154.2 9.5 %collective-permute-start.34 = (f32[2,16,1024]{2,1,0:T(8,128)S(1)}, f32[2,16,1024]{2,1,0:T(8,128)S(1)}, u32[]{:S(2)}, u32[]{:S(2)}) collective-permute-start(f32[2,16,1024]{2,1,0:T(8,128)S(1)} %get-tuple-element.92), channel_id=1, source_target_pairs={{0,24},{8,16},{16,8},{24,0},{1,25},{9,17},{17,9},{25,1},{2,26},{10... | collective-permute-start | bytes 393224 | tf_op jit(solution)/shard_map/ppermute | solution.py:60
  156.9 8.5 %collective-permute-start.40 = (f32[2,16,1024]{2,1,0:T(8,128)S(1)}, f32[2,16,1024]{2,1,0:T(8,128)S(1)}, u32[]{:S(2)}, u32[]{:S(2)}) collective-permute-start(f32[2,16,1024]{2,1,0:T(8,128)S(1)} %get-tuple-element.98), channel_id=1, source_target_pairs={{0,8},{8,0},{16,24},{24,16},{1,9},{9,1},{17,25},{25,17},{2,10},{10... | collective-permute-start | bytes 393224 | tf_op jit(solution)/shard_map/ppermute | solution.py:60
  158.0 8.4 %collective-permute-start.41 = (f32[2,16,1024]{2,1,0:T(8,128)S(1)}, f32[2,16,1024]{2,1,0:T(8,128)S(1)}, u32[]{:S(2)}, u32[]{:S(2)}) collective-permute-start(f32[2,16,1024]{2,1,0:T(8,128)S(1)} %get-tuple-element.99), channel_id=1, source_target_pairs={{0,16},{8,24},{16,0},{24,8},{1,17},{9,25},{17,1},{25,9},{2,18},{10... | collective-permute-start | bytes 393224 | tf_op jit(solution)/shard_map/ppermute | solution.py:60
  159.8 8.2 %collective-permute-start.42 = (f32[2,16,1024]{2,1,0:T(8,128)S(1)}, f32[2,16,1024]{2,1,0:T(8,128)S(1)}, u32[]{:S(2)}, u32[]{:S(2)}) collective-permute-start(f32[2,16,1024]{2,1,0:T(8,128)S(1)} %get-tuple-element.100), channel_id=1, source_target_pairs={{0,24},{8,16},{16,8},{24,0},{1,25},{9,17},{17,9},{25,1},{2,26},{10... | collective-permute-start | bytes 393224 | tf_op jit(solution)/shard_map/ppermute | solution.py:60
  (3 other events, 35.5 us)

commit v2 on v1

v2 whole, which is shorter than its diff:
```python
import functools

import jax
import jax.numpy as jnp
import ml_dtypes
import numpy as np
from jax import lax
from jax.experimental import pallas as pl
from jax.experimental.pallas import tpu as pltpu
from jax.sharding import PartitionSpec as P

LANES = 128
CHUNK_SHARES = (8, 8, 8, 8)
FLUX_GROUPS = ((0, 1), (2,), (3,))
WEIGHTS_TOGETHER = False
RESULTS_TOGETHER = False
REST_TOGETHER = False
RELEASE = 2
PAIR_AFTER = True
PAIR_GATE = 1
FLUX_GATE = 2
SEEN_GATE = 9
PACK_GATE = 1
WEIGHT_GATE = 3
REST_FIRST = True
HEAD_LIMIT = True
VMEM = pl.BlockSpec(memory_space=pltpu.VMEM)
SMEM = pl.BlockSpec(memory_space=pltpu.SMEM)
HBM = pl.BlockSpec(memory_space=pltpu.HBM)
SUBLANES = 8
LIMIT = 48 * 1024 * 1024
FULL = 62 * 1024 * 1024


def basis_table(sample_count, coefficient_count):
    column = np.arange(coefficient_count)
    order = 2 * (column // 2) + 1
    phase = order[None, :] * (2 * np.arange(sample_count)[:, None] + 1) % (4 * sample_count)
    angle = phase * (np.pi / (2 * sample_count))
    return np.where(column[None, :] % 2 == 0, np.cos(angle), np.sin(angle)).astype(np.float32)


def split_table(table):
    high = table.astype(ml_dtypes.bfloat16)
    low = (table - high.astype(np.float32)).astype(ml_dtypes.bfloat16)
    return np.concatenate([high, high, low], axis=1)


def table_dot(parts, value):
    high = value.astype(jnp.bfloat16)
    low = (value - high.astype(jnp.float32)).astype(jnp.bfloat16)
    return jnp.dot(
        parts, jnp.concatenate([high, low, high], axis=0), preferred_element_type=jnp.float32
    )


def f32(*shape):
    return jax.ShapeDtypeStruct(shape, jnp.float32)


TOKEN = f32(SUBLANES, LANES)


def call(kernel, out_shape, inputs, after=(), scratch=(), flops=0, smem=(0,), hbm=(), out_hbm=False, limit=LIMIT):
    count, tokens, made = len(inputs), len(after), len(out_shape)
    size = sum(4 * np.prod(x.shape) for x in (*inputs, *out_shape))

    def run(*refs):
        outs = refs[count + tokens : count + tokens + made]
        token, rest = refs[count + tokens + made], refs[count + tokens + made + 1 :]
        token[...] = jnp.zeros_like(token)
        kernel(*refs[:count], *outs, *rest)

    return pl.pallas_call(
        run,
        name=kernel.func.__name__,
        out_shape=[jax.ShapeDtypeStruct(x.shape, x.dtype) for x in (*out_shape, TOKEN)],
        in_specs=[SMEM if n in smem else HBM if n in hbm else VMEM for n in range(count)] + [VMEM] * tokens,
        out_specs=[HBM if out_hbm else VMEM] * made + [VMEM],
        scratch_shapes=list(scratch),
        compiler_params=pltpu.CompilerParams(vmem_limit_bytes=limit),
        cost_estimate=pl.CostEstimate(flops=flops, bytes_accessed=int(size), transcendentals=0),
    )(*inputs, *after)


def xor_permute(value, axis, step):
    count = lax.axis_size(axis)
    return lax.ppermute(value, axis, [(i, i ^ step) for i in range(count)])


def store_rows(block, row, spans, outs):
    turned = jnp.swapaxes(block, 0, 1)
    for r in range(SUBLANES):
        for (first, length), out in zip(spans, outs):
            if first <= row + r < first + length:
                lane = (row + r - first) * LANES
                out[:, lane : lane + LANES] = turned[r]


def pack_kernel(parts, spans, together, place, x, *refs):
    outs, (staged, sems) = refs[:-2], refs[-2:]
    if together:
        outs = [out.at[i] for i in range(parts) for out in outs]
    share_rows = x.shape[2] // parts
    low = spans[0][0] // SUBLANES * SUBLANES
    copies = []
    for i in range(parts):
        part = i if together else place[0] ^ i
        first = pl.multiple_of(part * share_rows + low, SUBLANES)
        copies.append(
            pltpu.make_async_copy(x.at[:, :, pl.ds(first, staged.shape[3]), :], staged.at[i], sems.at[i])
        )
        copies[i].start()
    for i in range(parts):
        copies[i].wait()
        for comp in range(2):
            for row in range(0, staged.shape[3], SUBLANES):
                store_rows(
                    staged[i, :, comp, row : row + SUBLANES, :],
                    low + row,
                    spans,
                    [out.at[comp] for out in outs[i * len(spans) : (i + 1) * len(spans)]],
                )


def head_kernel(parts, spans, together, place, x, shifts, offsets, *refs):
    outs = refs[: parts * len(spans)]
    pack_kernel(parts, spans, together, place, x, *refs)
    rows = shifts.shape[0]
    row = lax.broadcasted_iota(jnp.int32, (rows, LANES), 0)
    lane = lax.broadcasted_iota(jnp.int32, (rows, LANES), 1)
    plan = jnp.zeros((rows, LANES), jnp.int32)
    for j in range(rows):
        numbers = jnp.where(lane == 0, shifts[j], jnp.where(lane == 1, offsets[0, j], offsets[1, j]))
        plan = jnp.where(row == j, numbers, plan)
    for i in range(parts):
        outs[i * len(spans)][2, :, :LANES] = plan.astype(jnp.float32)


def seen_kernel(place, *pieces):
    pass


def gather_kernel(parts, together, place, *refs):
    if together:
        pieces, outs = [refs[0].at[q] for q in range(parts)], refs[1:]
    else:
        pieces, outs = refs[:parts], refs[parts:]
    rows = pieces[0].shape[1]
    for i in range(parts):
        first = i * rows if together else pl.multiple_of((place[0] ^ i) * rows, rows)
        lane = 0
        for out in outs:
            out[:, pl.ds(first, rows), :] = pieces[i][:2, :, lane : lane + out.shape[2]]
            lane += out.shape[2]


def head_gather_kernel(parts, place, *refs):
    pieces, (own, plan) = refs[:parts], refs[parts:]
    gather_kernel(parts, False, place, *pieces, own)
    rows = pieces[0].shape[1]
    for i in range(parts):
        first = pl.multiple_of((place[0] ^ i) * rows, rows)
        numbers = pieces[i][2, :, :LANES].astype(jnp.int32)
        for n in range(3):
            plan[n, pl.ds(first, rows), :] = jnp.broadcast_to(numbers[:, n : n + 1], (rows, LANES))


def in_first(me, base, size, shifts):
    offset = (me - base + 1 + shifts) & (2 * size - 1)
    return ((base - 1 - shifts + offset - me) & (4 * size - 1)) == 0


def choose(me, size, shifts):
    clear = ~(size - 1)
    kept = in_first(me, me & clear, size, shifts)
    sent = in_first(me, (me ^ size) & clear, size, shifts)
    return kept, sent


def is_outer(me, count):
    return ((me // (count // 2)) ^ (me // (count // 4))) & 1 == 0


def sample_step(count, place, table, shifts, own, far, send, keep):
    me = place[1]
    kept, sent = choose(me, count // 4, shifts[0])
    parts = table[...]
    for comp in range(2):
        near_samples = table_dot(parts, own[comp])
        far_samples = table_dot(parts, far[comp, :, : own.shape[2]])
        for lane in range(0, own.shape[2], LANES):
            here = slice(lane, lane + LANES)
            keep[comp, :, here] = jnp.where(kept, near_samples[:, here], far_samples[:, here])
            send[comp, :, here] = jnp.where(sent, near_samples[:, here], far_samples[:, here])


def copy_lanes(source, target):
    width = min(source.shape[2], target.shape[2])
    target[:, :, :width] = source[:, :, :width]


def first_kernel(count, place, table, shifts, own, arrived, following, send, keep):
    outer = is_outer(place[1], count)

    @pl.when(outer)
    def _():
        copy_lanes(following, send)
        keep[...] = own[...]

    @pl.when(jnp.logical_not(outer))
    def _():
        sample_step(count, place, table, shifts, own, arrived, send, keep)


def second_kernel(count, place, table, shifts, own, arrived, following, kept, send, keep):
    outer = is_outer(place[1], count)

    @pl.when(outer)
    def _():
        sample_step(count, place, table, shifts, own, arrived, send, keep)

    @pl.when(jnp.logical_not(outer))
    def _():
        copy_lanes(following, send)
        keep[...] = kept[...]


def middle_kernel(count, size, place, shifts, first, slot_a, slot_b, send, keep):
    me = place[1]
    outer = is_outer(me, count)
    kept, sent = choose(me, size, shifts[0])
    for comp in range(2):
        for lane in range(0, first.shape[2], LANES):
            here = slice(lane, lane + LANES)
            one = first[comp, :, here]
            two = jnp.where(outer, slot_a[comp, :, here], slot_b[comp, :, here])
            keep[comp, :, here] = jnp.where(kept, one, two)
            send[comp, :, here] = jnp.where(sent, one, two)


def pair_kernel(count, place, keep, slot_a, slot_b, pair):
    outer = is_outer(place[1], count)
    pair[0:2] = keep[...]

    @pl.when(outer)
    def _():
        pair[2:4] = slot_a[:, :, : pair.shape[2]]

    @pl.when(jnp.logical_not(outer))
    def _():
        pair[2:4] = slot_b[:, :, : pair.shape[2]]


def flux_kernel(parts, together, chunks, row0, place, table, plan, iron, weights, *refs):
    pairs, fars = refs[:chunks], refs[chunks : 2 * chunks]
    flux, result = refs[-2:]
    outs = [refs[2 * chunks].at[q] for q in range(parts)] if together else refs[2 * chunks : -2]
    total = outs[0].shape[2]
    tm, me = place[0], place[1]
    source = [((me + plan[1 + m] - plan[0]) ^ me) & 3 for m in range(2)]
    is_near = [s == 0 for s in source]
    is_two = [s == 2 for s in source]
    is_one = [s == 1 for s in source]
    quarter = tm * (iron.shape[0] // parts) + row0
    lane = 0
    for k in range(chunks):
        for inner in range(0, pairs[k].shape[2], LANES):
            here = slice(inner, inner + LANES)
            there = slice(row0 * LANES + lane, row0 * LANES + lane + LANES)
            field = []
            for comp in range(2):
                blocks = [ref[c, :, here] for ref in (pairs[k], fars[k]) for c in (comp, 2 + comp)]
                terms = [
                    weights[m, :, there]
                    * jnp.where(
                        is_near[m],
                        blocks[0],
                        jnp.where(is_two[m], blocks[1], jnp.where(is_one[m], blocks[2], blocks[3])),
                    )
                    for m in range(2)
                ]
                field.append(terms[0] + terms[1])
            square = field[0] * field[0] + field[1] * field[1]
            gain = iron[pl.ds(quarter + lane // LANES, 1), :] * (1.0 + square / (1.0 + square))
            for comp in range(2):
                flux[:, comp * total + lane : comp * total + lane + LANES] = gain * field[comp]
            lane += LANES
    result[...] = table_dot(table[...], flux[...])
    rows = result.shape[0] // parts
    for i in range(parts):
        first = i * rows if together else pl.multiple_of((tm ^ i) * rows, rows)
        for comp in range(2):
            outs[i][comp] = result[pl.ds(first, rows), comp * total : (comp + 1) * total]


def finish_kernel(parts, together, groups, place, source, *refs):
    pieces, (out, made, sems) = refs[:-3], refs[-3:]
    if together:
        pieces = [piece.at[q] for piece in pieces for q in range(parts)]
    share_rows = source.shape[2] // parts
    copies = []
    for i in range(parts):
        first = pl.multiple_of((i if together else place[0] ^ i) * share_rows, SUBLANES)
        for comp in range(2):
            rows = [
                pieces[g * parts + i][comp, :, lane : lane + LANES]
                for g in range(groups)
                for lane in range(0, pieces[g * parts].shape[2], LANES)
            ]
            for row in range(0, share_rows, SUBLANES):
                turned = jnp.swapaxes(jnp.stack(rows[row : row + SUBLANES]), 0, 1)
                made[i, :, comp, row : row + SUBLANES, :] = turned - source[:, comp, pl.ds(first + row, SUBLANES), :]
        copies.append(
            pltpu.make_async_copy(made.at[i], out.at[:, :, pl.ds(first, share_rows), :], sems.at[i])
        )
        copies[i].start()
    for copy in copies:
        copy.wait()


def body(rotor_coeffs, mortar_weights, block_shifts, stencil_offsets, reluctivity, source):
    parts, count = lax.axis_size("tm"), lax.axis_size("azim")
    coeff_rows, comps, _, nodes = rotor_coeffs.shape
    sample_rows = mortar_weights.shape[0]
    coeffs, samples = coeff_rows * parts, sample_rows * parts
    share_rows = nodes // parts // LANES
    bounds = np.cumsum((0,) + CHUNK_SHARES) * share_rows // sum(CHUNK_SHARES)
    heights = [int(h) for h in np.diff(bounds)]
    widths = [h * LANES for h in heights]
    chunks = len(heights)
    place = jnp.stack([lax.axis_index("tm"), lax.axis_index("azim")]).astype(jnp.int32)
    table = basis_table(samples, coeffs)
    forward = jnp.asarray(split_table(table))
    backward = jnp.asarray(split_table(np.ascontiguousarray(table.T) * np.float32(2.0 / samples)))
    gates = {}

    def in_rows(x):
        return x.reshape(x.shape[0], comps, nodes // LANES, LANES)

    def pack(x, spans, after=(), plan=(), together=False):
        low = spans[0][0] // SUBLANES * SUBLANES
        high = -(-(spans[-1][0] + spans[-1][1]) // SUBLANES) * SUBLANES
        shape = (3 if plan else 2, x.shape[0], spans[0][1] * LANES)
        *outs, token = call(
            functools.partial(head_kernel if plan else pack_kernel, parts, spans, together),
            [f32(parts, *shape)] if together else [f32(*shape)] * parts,
            (place, in_rows(x), *plan),
            after=after,
            scratch=(
                pltpu.VMEM((parts, x.shape[0], comps, high - low, LANES), jnp.float32),
                pltpu.SemaphoreType.DMA((parts,)),
            ),
            smem=(0, 2, 3) if plan else (0,),
            hbm=(1,),
            limit=FULL if plan else LIMIT,
        )
        return outs, token

    def swap(pieces):
        if len(pieces) == 1:
            return [lax.all_to_all(pieces[0], "tm", split_axis=0, concat_axis=0, tiled=True)]
        return [pieces[0]] + [xor_permute(pieces[i], "tm", i) for i in range(1, parts)]

    def gather(pieces, lanes, rows, after=()):
        *outs, token = call(
            functools.partial(gather_kernel, parts, len(pieces) == 1),
            [f32(2, rows, w) for w in lanes],
            (place, *pieces),
            after=after,
        )
        return outs, token

    head, token = pack(rotor_coeffs, [(0, heights[0])], plan=(block_shifts, stencil_offsets.T))
    rest_span = [(heights[0], share_rows - heights[0])]
    if REST_FIRST:
        rest, token = pack(rotor_coeffs, rest_span, after=(token,), together=REST_TOGETHER)
    own_first, plan, token = call(
        functools.partial(head_gather_kernel, parts),
        [f32(2, coeffs, widths[0]), jax.ShapeDtypeStruct((3, samples, LANES), jnp.int32)],
        (place, *swap(head)),
        after=(token,) if REST_FIRST else (),
    )
    if not REST_FIRST:
        rest, token = pack(rotor_coeffs, rest_span, after=(token,), together=REST_TOGETHER)
    own_rest, token = gather(swap(rest), widths[1:], coeffs, (token,))
    own = [own_first] + own_rest
    weights, token = pack(mortar_weights, [(0, share_rows)], after=(token,), together=WEIGHTS_TOGETHER)
    gates[PACK_GATE] = [token]
    (weights,), token = gather(swap(weights), [share_rows * LANES], samples)
    gates.setdefault(WEIGHT_GATE, []).append(token)

    half, fourth = count // 2, count // 4
    outer = [d for d in range(count) if is_outer(d, count)]
    inner = [d for d in range(count) if not is_outer(d, count)]
    coeff_a = [(d, d ^ half) for d in outer]
    coeff_b = [(d, d ^ half) for d in inner]
    sample_a = [(d, d ^ fourth) for d in inner]
    sample_b = [(d, d ^ fourth) for d in outer]

    def neighbours(keep, slot_a, slot_b, after):
        size = count // 8
        while size >= 2:
            send, keep, _ = call(
                functools.partial(middle_kernel, count, size), [keep, keep], (place, plan, keep, slot_a, slot_b)
            )
            slot_a = slot_b = xor_permute(send, "azim", size)
            size //= 2
        pair, token = call(
            functools.partial(pair_kernel, count),
            [f32(4, samples, keep.shape[2])],
            (place, keep, slot_a, slot_b),
            after=after,
        )
        return pair, xor_permute(pair, "azim", 1), token

    iron = reluctivity.reshape(nodes // LANES, LANES)

    def flux(group, pairs):
        total = sum(widths[k] for k in group)
        *made, token = call(
            functools.partial(flux_kernel, parts, RESULTS_TOGETHER, len(group), sum(heights[: group[0]])),
            [f32(parts, 2, coeff_rows, total)] if RESULTS_TOGETHER else [f32(2, coeff_rows, total)] * parts,
            (place, backward, plan, iron, weights, *[pairs[k][0] for k in group], *[pairs[k][1] for k in group]),
            scratch=(pltpu.VMEM((samples, 2 * total), jnp.float32), pltpu.VMEM((coeffs, 2 * total), jnp.float32)),
            flops=4 * samples * 3 * coeffs * total,
        )
        return swap(made), token

    slots_a, slots_b, keeps, pairs, pieces = [], [], [], [], []
    send_a = send_b = own[0]
    for k in range(chunks):
        slots_a.append(lax.ppermute(send_a, "azim", coeff_a + (sample_a if k else [])))
        slots_b.append(lax.ppermute(send_b, "azim", coeff_b + (sample_b if k else [])))
        after = own[k + 1] if k + 1 < chunks else own[k]
        block, sent = f32(2, samples, widths[k]), f32(2, samples, max(widths[k], after.shape[2]))
        flops = 8 * samples * 3 * coeffs * widths[k]
        send_a, kept, _ = call(
            functools.partial(first_kernel, count),
            [sent, block],
            (place, forward, plan, own[k], slots_a[k], after),
            after=gates.get(k, ()),
            flops=flops,
        )
        send_b, kept, token = call(
            functools.partial(second_kernel, count),
            [sent, block],
            (place, forward, plan, own[k], slots_b[k], after, kept),
            flops=flops,
        )
        keeps.append(kept)
        if k:
            *pair, token = neighbours(keeps[k - 1], slots_a[k], slots_b[k], (token,) if PAIR_AFTER else ())
            gates.setdefault(k + PAIR_GATE, []).append(token)
            pairs.append(pair)
            for group in FLUX_GROUPS:
                if group[-1] == k - 1:
                    made, token = flux(group, pairs)
                    pieces += made
                    gates.setdefault(min(k + FLUX_GATE, chunks), []).append(token)
                    if k + SEEN_GATE <= chunks:
                        (token,) = call(functools.partial(seen_kernel), [], (place, *made))
                        gates.setdefault(k + SEEN_GATE, []).append(token)
    slot_a = lax.ppermute(send_a, "azim", sample_a)
    slot_b = lax.ppermute(send_b, "azim", sample_b)
    *pair, _ = neighbours(keeps[-1], slot_a, slot_b, gates.get(chunks, ()))
    pairs.append(pair)
    pieces += flux(FLUX_GROUPS[-1], pairs)[0]
    out, _ = call(
        functools.partial(finish_kernel, parts, RESULTS_TOGETHER, len(FLUX_GROUPS)),
        [f32(coeff_rows, comps, nodes // LANES, LANES)],
        (place, in_rows(source), *pieces),
        scratch=(
            pltpu.VMEM((parts, coeff_rows, comps, share_rows, LANES), jnp.float32),
            pltpu.SemaphoreType.DMA((parts,)),
        ),
        out_hbm=True,
    )
    return out.reshape(source.shape)


def solution(mesh):
    wide = P("tm", None, "azim", None)
    in_specs = (wide, wide, P("tm"), P("tm", None), P("azim", None), wide)
    return jax.shard_map(body, mesh=mesh, in_specs=in_specs, out_specs=wide, check_vma=False)
```

time: 173 us -> 166 us (0.960)
  waiting for transfers between devices: 70.4 us -> 87.5 us
  blocking collectives: 16.7 us -> 0 us
  starting transfers between devices: 61.7 us -> 46.3 us
  Pallas kernels: 21.4 us -> 27.4 us
  local copies, waits for them, and re-layouts: 1.79 us -> 3.62 us
    ppermute x4, waiting for transfers between devices: 44.2 us -> 20.6 us  [body(): lax.ppermute(send_b, 'azim', coeff_b + (sample_b if k else []))]
    ppermute x33 -> x22, waiting for transfers between devices: 15.3 us -> 37.4 us  [xor_permute(): return lax.ppermute(value, axis, [(i, i ^ step) for i in range(count)])]
    ppermute x4, waiting for transfers between devices: 0.01 us -> 18.9 us  [body(): lax.ppermute(send_a, 'azim', coeff_a + (sample_a if k else []))]
    all_gather x1 -> x0, blocking collectives: 16.7 us -> none  [body(): plan = lax.all_gather(local_plan, 'tm', axis=0, tiled=True)]
    ppermute x33 -> x22, starting transfers between devices: 31.2 us -> 24.1 us  [xor_permute(): return lax.ppermute(value, axis, [(i, i ^ step) for i in range(count)])]
    ppermute x4, starting transfers between devices: 13.1 us -> 6.09 us  [body(): lax.ppermute(send_b, 'azim', coeff_b + (sample_b if k else []))]
    pallas_call x17 -> x22, Pallas kernels: 21.4 us -> 27.4 us  [call(): pl.pallas_call(run, name=kernel.func.__name__, out_shape=[jax.ShapeDtypeS...]
    ppermute x2, starting transfers between devices: 5.9 us -> 3.79 us  [the longest x1 2.49 us: body(): slot_b = lax.ppermute(send_b, 'azim', sample_b)]
  transfers between devices with their start and end apart: 43 -> 32, of which waited for: 16 -> 19; matrix products, arithmetic and copies ran while one was open for 0% -> 0% of each run, Pallas kernels for 8% -> 12%
where the time goes in v2:
time: 166 us
  waiting for transfers between devices  87.5 us (53%)
  starting transfers between devices  46.3 us (28%)
  Pallas kernels  27.4 us (17%)
  local copies, waits for them, and re-layouts  3.62 us (2%)
    ppermute x22, waiting for transfers between devices, xor_permute(): return lax.ppermute(value, axis, [(i, i ^ step) for i in range(count)])  37.4 us
    pallas_call x22, Pallas kernels, call(): pl.pallas_call(run, name=kernel.func.__name__, out_shape=[jax.ShapeDtypeS...  27.4 us
    ppermute x22, starting transfers between devices, xor_permute(): return lax.ppermute(value, axis, [(i, i ^ step) for i in range(count)])  24.1 us
    ppermute x4, waiting for transfers between devices, body(): lax.ppermute(send_b, 'azim', coeff_b + (sample_b if k else []))  20.6 us
    ppermute x4, waiting for transfers between devices, body(): lax.ppermute(send_a, 'azim', coeff_a + (sample_a if k else []))  18.9 us
    ppermute x4, starting transfers between devices, body(): lax.ppermute(send_a, 'azim', coeff_a + (sample_a if k else []))  12.3 us
    ppermute x1, waiting for transfers between devices, body(): slot_b = lax.ppermute(send_b, 'azim', sample_b)  6.46 us
    ppermute x4, starting transfers between devices, body(): lax.ppermute(send_b, 'azim', coeff_b + (sample_b if k else []))  6.09 us
  transfers between devices with their start and end apart: 32, of which 19 were waited for; matrix products, arithmetic and copies ran while one was open for 0% of the time, Pallas kernels for 12%

profile of v2, /device:TPU:0, one launch (start us, length us, event | category | flops | bytes accessed | tf_op | source)
XLA Modules:
  0.0 165.7 jit_solution(14485413344181421602)
XLA Ops:
  0.6 2.8 %head_kernel.1 = (f32[3,16,1024]{2,1,0:T(8,128)}, f32[3,16,1024]{2,1,0:T(8,128)}, f32[3,16,1024]{2,1,0:T(8,128)}, f32[3,16,1024]{2,1,0:T(8,128)}, f32[8,128]{1,0:T(8,128)}) custom-call(s32[2]{0:T(128)} %pad_add_fusion.refs_0_, f32[16,2,128,128]{3,2,1,0:T(8,128)} %bitcast.8, s32[16]{0:T(128)} %refs_2_.1, s32[2,16]{1,0:T(2,128)} %bitcast.15), custom_call_target="tpu_custom_call" | custom-call | bytes 2883784 | tf_op jit(solution)/shard_map/head_kernel/pallas_call | solution.py:74
  3.4 3.0 %collective-permute-start = (f32[3,16,1024]{2,1,0:T(8,128)}, f32[3,16,1024]{2,1,0:T(8,128)S(1)}, u32[]{:S(2)}, u32[]{:S(2)}) collective-permute-start(f32[3,16,1024]{2,1,0:T(8,128)} %get-tuple-element.71), channel_id=1, source_target_pairs={{0,8},{8,0},{16,24},{24,16},{1,9},{9,1},{17,25},{25,17},{2,10},{10... | collective-permute-start | bytes 589832 | tf_op jit(solution)/shard_map/ppermute | solution.py:88
  6.4 1.5 collective-permute-start.1
  8.0 1.6 copy-done.2
  11.3 1.1 collective-permute-done.refs_2_
  12.3 4.8 %collective-permute-done.1.refs_3_ = f32[3,16,1024]{2,1,0:T(8,128)S(1)} collective-permute-done((f32[3,16,1024]{2,1,0:T(8,128)}, f32[3,16,1024]{2,1,0:T(8,128)S(1)}, u32[]{:S(2)}, u32[]{:S(2)}) %collective-permute-start.1) | collective-permute-done | bytes 196640 | tf_op jit(solution)/shard_map/ppermute | solution.py:88
  17.8 4.5 %collective-permute-start.10 = (f32[2,64,1024]{2,1,0:T(8,128)S(1)}, f32[2,64,1024]{2,1,0:T(8,128)S(1)}, u32[]{:S(2)}, u32[]{:S(2)}) collective-permute-start(f32[2,64,1024]{2,1,0:T(8,128)S(1)} %get-tuple-element.88.refs_3_), channel_id=1, source_target_pairs={{0,4},{1,5},{6,2},{7,3},{8,12},{9,13},{14,10},{15,11},{16,20},{17,... | collective-permute-start | bytes 1572872 | tf_op jit(solution)/shard_map/ppermute | solution.py:433
  22.4 1.3 collective-permute-start.9
  23.7 1.3 collective-permute-start.3
  25.8 1.4 collective-permute-start.5
  27.2 8.6 %collective-permute-done.3.refs_2_ = f32[2,16,3072]{2,1,0:T(8,128)S(1)} collective-permute-done((f32[2,16,3072]{2,1,0:T(8,128)S(1)}, f32[2,16,3072]{2,1,0:T(8,128)S(1)}, u32[]{:S(2)}, u32[]{:S(2)}) %collective-permute-start.3) | collective-permute-done | bytes 393248 | tf_op jit(solution)/shard_map/ppermute | solution.py:88
  35.8 7.0 %collective-permute-done.4.refs_3_ = f32[2,16,3072]{2,1,0:T(8,128)S(1)} collective-permute-done((f32[2,16,3072]{2,1,0:T(8,128)S(1)}, f32[2,16,3072]{2,1,0:T(8,128)S(1)}, u32[]{:S(2)}, u32[]{:S(2)}) %collective-permute-start.4) | collective-permute-done | bytes 393248 | tf_op jit(solution)/shard_map/ppermute | solution.py:88
  43.5 1.2 first_kernel.4
  44.7 3.6 %collective-permute-start.11 = (f32[2,64,1024]{2,1,0:T(8,128)S(1)}, f32[2,64,1024]{2,1,0:T(8,128)S(1)}, u32[]{:S(2)}, u32[]{:S(2)}) collective-permute-start(f32[2,64,1024]{2,1,0:T(8,128)S(1)} %get-tuple-element.92), channel_id=1, source_target_pairs={{0,4},{1,5},{6,2},{7,3},{2,0},{3,1},{4,6},{5,7},{8,12},{9,13},{14,... | collective-permute-start | bytes 1572872 | tf_op jit(solution)/shard_map/ppermute | solution.py:433
  48.4 1.6 second_kernel.4
  49.9 1.1 pack_kernel.3
  51.1 13.9 %collective-permute-done.11.refs_4_.refs_2_ = f32[2,64,1024]{2,1,0:T(8,128)S(1)} collective-permute-done((f32[2,64,1024]{2,1,0:T(8,128)S(1)}, f32[2,64,1024]{2,1,0:T(8,128)S(1)}, u32[]{:S(2)}, u32[]{:S(2)}) %collective-permute-start.11) | collective-permute-done | bytes 524320 | tf_op jit(solution)/shard_map/ppermute | solution.py:433
  65.0 1.2 first_kernel.5
  66.6 7.0 %collective-permute-done.12.refs_4_.refs_3_ = f32[2,64,1024]{2,1,0:T(8,128)S(1)} collective-permute-done((f32[2,64,1024]{2,1,0:T(8,128)S(1)}, f32[2,64,1024]{2,1,0:T(8,128)S(1)}, u32[]{:S(2)}, u32[]{:S(2)}) %collective-permute-start.12) | collective-permute-done | bytes 524320 | tf_op jit(solution)/shard_map/ppermute | solution.py:434
  75.8 1.2 collective-permute-start.7
  76.9 1.6 collective-permute-start.8
  79.1 3.9 %collective-permute-done.13.refs_4_.refs_2_ = f32[2,64,1024]{2,1,0:T(8,128)S(1)} collective-permute-done((f32[2,64,1024]{2,1,0:T(8,128)S(1)}, f32[2,64,1024]{2,1,0:T(8,128)S(1)}, u32[]{:S(2)}, u32[]{:S(2)}) %collective-permute-start.13) | collective-permute-done | bytes 524320 | tf_op jit(solution)/shard_map/ppermute | solution.py:433
  83.0 1.2 first_kernel.6
  84.2 3.7 %collective-permute-start.20 = (f32[2,64,1024]{2,1,0:T(8,128)S(1)}, f32[2,64,1024]{2,1,0:T(8,128)S(1)}, u32[]{:S(2)}, u32[]{:S(2)}) collective-permute-start(f32[2,64,1024]{2,1,0:T(8,128)S(1)} %get-tuple-element.112), channel_id=1, source_target_pairs={{0,4},{1,5},{6,2},{7,3},{2,0},{3,1},{4,6},{5,7},{8,12},{9,13},{14,... | collective-permute-start | bytes 1572872 | tf_op jit(solution)/shard_map/ppermute | solution.py:433
  88.0 6.3 %collective-permute-done.14.refs_4_.refs_3_ = f32[2,64,1024]{2,1,0:T(8,128)S(1)} collective-permute-done((f32[2,64,1024]{2,1,0:T(8,128)S(1)}, f32[2,64,1024]{2,1,0:T(8,128)S(1)}, u32[]{:S(2)}, u32[]{:S(2)}) %collective-permute-start.14) | collective-permute-done | bytes 524320 | tf_op jit(solution)/shard_map/ppermute | solution.py:434
  95.2 4.4 %collective-permute-start.21 = (f32[2,64,1024]{2,1,0:T(8,128)S(1)}, f32[2,64,1024]{2,1,0:T(8,128)S(1)}, u32[]{:S(2)}, u32[]{:S(2)}) collective-permute-start(f32[2,64,1024]{2,1,0:T(8,128)S(1)} %get-tuple-element.113), channel_id=1, source_target_pairs={{2,6},{3,7},{4,0},{5,1},{0,2},{1,3},{6,4},{7,5},{10,14},{11,15},{1... | collective-permute-start | bytes 1572872 | tf_op jit(solution)/shard_map/ppermute | solution.py:434
  100.9 1.3 copy-done
  103.5 1.1 collective-permute-done.20.refs_4_.refs_2_
  104.6 1.2 first_kernel.7
  105.8 7.2 %collective-permute-done.21.refs_4_.refs_3_ = f32[2,64,1024]{2,1,0:T(8,128)S(1)} collective-permute-done((f32[2,64,1024]{2,1,0:T(8,128)S(1)}, f32[2,64,1024]{2,1,0:T(8,128)S(1)}, u32[]{:S(2)}, u32[]{:S(2)}) %collective-permute-start.21) | collective-permute-done | bytes 524320 | tf_op jit(solution)/shard_map/ppermute | solution.py:434
  114.8 2.5 %collective-permute-start.27 = (f32[2,64,1024]{2,1,0:T(8,128)S(1)}, f32[2,64,1024]{2,1,0:T(8,128)S(1)}, u32[]{:S(2)}, u32[]{:S(2)}) collective-permute-start(f32[2,64,1024]{2,1,0:T(8,128)S(1)} %get-tuple-element.125), channel_id=1, source_target_pairs={{0,2},{1,3},{6,4},{7,5},{8,10},{9,11},{14,12},{15,13},{16,18},{17,... | collective-permute-start | bytes 1572872 | tf_op jit(solution)/shard_map/ppermute | solution.py:465
  117.3 1.3 collective-permute-start.26
  118.6 2.8 %flux_kernel.3 = (f32[2,16,2048]{2,1,0:T(8,128)S(1)}, f32[2,16,2048]{2,1,0:T(8,128)S(1)}, f32[2,16,2048]{2,1,0:T(8,128)S(1)}, f32[2,16,2048]{2,1,0:T(8,128)S(1)}, f32[8,128]{1,0:T(8,128)S(1)}) custom-call(s32[2]{0:T(128)S(1)} %copy-done.8, bf16[64,192]{1,0:T(8,128)(2,1)S(1)} %copy-done.7, s32[3,64,128]{2,1,0:T(8,128)S(1)} %get-tuple-element.76.refs_2_, ...), custom_call_target="tpu_custom_call" | custom-call | flops 100663296 | bytes 7553032 | tf_op jit(solution)/shard_map/flux_kernel/pallas_call | solution.py:74
  121.4 1.1 flux_kernel.4
  122.6 6.5 %collective-permute-done.27.refs_3_ = f32[2,64,1024]{2,1,0:T(8,128)S(1)} collective-permute-done((f32[2,64,1024]{2,1,0:T(8,128)S(1)}, f32[2,64,1024]{2,1,0:T(8,128)S(1)}, u32[]{:S(2)}, u32[]{:S(2)}) %collective-permute-start.27) | collective-permute-done | bytes 524320 | tf_op jit(solution)/shard_map/ppermute | solution.py:465
  129.0 4.1 %collective-permute-done.26.refs_2_ = f32[2,64,1024]{2,1,0:T(8,128)S(1)} collective-permute-done((f32[2,64,1024]{2,1,0:T(8,128)S(1)}, f32[2,64,1024]{2,1,0:T(8,128)S(1)}, u32[]{:S(2)}, u32[]{:S(2)}) %collective-permute-start.26) | collective-permute-done | bytes 524320 | tf_op jit(solution)/shard_map/ppermute | solution.py:464
  133.2 1.2 pair_kernel.7
  134.4 3.4 %collective-permute-start.17 = (f32[2,16,2048]{2,1,0:T(8,128)S(1)}, f32[2,16,2048]{2,1,0:T(8,128)S(1)}, u32[]{:S(2)}, u32[]{:S(2)}) collective-permute-start(f32[2,16,2048]{2,1,0:T(8,128)S(1)} %get-tuple-element.108), channel_id=1, source_target_pairs={{0,8},{8,0},{16,24},{24,16},{1,9},{9,1},{17,25},{25,17},{2,10},{10... | collective-permute-start | bytes 786440 | tf_op jit(solution)/shard_map/ppermute | solution.py:88
  138.1 1.1 collective-permute-start.19
  139.2 2.0 %collective-permute-start.23 = (f32[2,16,1024]{2,1,0:T(8,128)S(1)}, f32[2,16,1024]{2,1,0:T(8,128)S(1)}, u32[]{:S(2)}, u32[]{:S(2)}) collective-permute-start(f32[2,16,1024]{2,1,0:T(8,128)S(1)} %get-tuple-element.120), channel_id=1, source_target_pairs={{0,8},{8,0},{16,24},{24,16},{1,9},{9,1},{17,25},{25,17},{2,10},{10... | collective-permute-start | bytes 393224 | tf_op jit(solution)/shard_map/ppermute | solution.py:88
  141.6 1.5 flux_kernel.5
  143.1 1.8 %collective-permute-done.17.refs_3_ = f32[2,16,2048]{2,1,0:T(8,128)S(1)} collective-permute-done((f32[2,16,2048]{2,1,0:T(8,128)S(1)}, f32[2,16,2048]{2,1,0:T(8,128)S(1)}, u32[]{:S(2)}, u32[]{:S(2)}) %collective-permute-start.17) | collective-permute-done | bytes 262176 | tf_op jit(solution)/shard_map/ppermute | solution.py:88
  144.9 1.7 %collective-permute-start.25 = (f32[2,16,1024]{2,1,0:T(8,128)S(1)}, f32[2,16,1024]{2,1,0:T(8,128)S(1)}, u32[]{:S(2)}, u32[]{:S(2)}) collective-permute-start(f32[2,16,1024]{2,1,0:T(8,128)S(1)} %get-tuple-element.122), channel_id=1, source_target_pairs={{0,24},{8,16},{16,8},{24,0},{1,25},{9,17},{17,9},{25,1},{2,26},{10... | collective-permute-start | bytes 393224 | tf_op jit(solution)/shard_map/ppermute | solution.py:88
  146.6 5.9 %collective-permute-done.18.refs_4_ = f32[2,16,2048]{2,1,0:T(8,128)S(1)} collective-permute-done((f32[2,16,2048]{2,1,0:T(8,128)S(1)}, f32[2,16,2048]{2,1,0:T(8,128)S(1)}, u32[]{:S(2)}, u32[]{:S(2)}) %collective-permute-start.18) | collective-permute-done | bytes 262176 | tf_op jit(solution)/shard_map/ppermute | solution.py:88
  153.4 2.6 %collective-permute-start.31 = (f32[2,16,1024]{2,1,0:T(8,128)S(1)}, f32[2,16,1024]{2,1,0:T(8,128)S(1)}, u32[]{:S(2)}, u32[]{:S(2)}) collective-permute-start(f32[2,16,1024]{2,1,0:T(8,128)S(1)} %get-tuple-element.133), channel_id=1, source_target_pairs={{0,24},{8,16},{16,8},{24,0},{1,25},{9,17},{17,9},{25,1},{2,26},{10... | collective-permute-start | bytes 393224 | tf_op jit(solution)/shard_map/ppermute | solution.py:88
  156.0 2.1 %collective-permute-done.24.refs_8_ = f32[2,16,1024]{2,1,0:T(8,128)S(1)} collective-permute-done((f32[2,16,1024]{2,1,0:T(8,128)S(1)}, f32[2,16,1024]{2,1,0:T(8,128)S(1)}, u32[]{:S(2)}, u32[]{:S(2)}) %collective-permute-start.24) | collective-permute-done | bytes 131104 | tf_op jit(solution)/shard_map/ppermute | solution.py:88
  159.1 4.0 %collective-permute-done.30.refs_12_ = f32[2,16,1024]{2,1,0:T(8,128)S(1)} collective-permute-done((f32[2,16,1024]{2,1,0:T(8,128)S(1)}, f32[2,16,1024]{2,1,0:T(8,128)S(1)}, u32[]{:S(2)}, u32[]{:S(2)}) %collective-permute-start.30) | collective-permute-done | bytes 131104 | tf_op jit(solution)/shard_map/ppermute | solution.py:88
  163.1 2.6 %finish_kernel.1 = (f32[16,2,128,128]{3,2,1,0:T(8,128)}, f32[8,128]{1,0:T(8,128)}) custom-call(s32[2]{0:T(128)S(1)} %copy-done.8, f32[16,2,128,128]{3,2,1,0:T(8,128)S(1)} %bitcast.11, f32[2,16,2048]{2,1,0:T(8,128)S(1)} %get-tuple-element.107.refs_2_, f32[2,16,2048]{2,1,0:T(8,128)S(1)} %collective-permute-done.17.refs_3_, ...), custom_call_target="tpu_custom_call" | custom-call | bytes 6291464 | tf_op jit(solution)/shard_map/finish_kernel/pallas_call | solution.py:74
  (61 shorter events, 15.2 us)
Async XLA Ops:
  0.6 7.3 %copy-start.8 = (s32[2]{0:T(128)S(1)}, s32[2]{0:T(128)}, u32[]{:S(2)}) copy-start(s32[2]{0:T(128)} %pad_add_fusion.refs_0_) | copy-start | bytes 28
  3.4 8.9 %collective-permute-start = (f32[3,16,1024]{2,1,0:T(8,128)}, f32[3,16,1024]{2,1,0:T(8,128)S(1)}, u32[]{:S(2)}, u32[]{:S(2)}) collective-permute-start(f32[3,16,1024]{2,1,0:T(8,128)} %get-tuple-element.71), channel_id=1, source_target_pairs={{0,8},{8,0},{16,24},{24,16},{1,9},{9,1},{17,25},{25,17},{2,10},{10... | collective-permute-start | bytes 589832 | tf_op jit(solution)/shard_map/ppermute | solution.py:88
  6.4 10.8 %collective-permute-start.1 = (f32[3,16,1024]{2,1,0:T(8,128)}, f32[3,16,1024]{2,1,0:T(8,128)S(1)}, u32[]{:S(2)}, u32[]{:S(2)}) collective-permute-start(f32[3,16,1024]{2,1,0:T(8,128)} %get-tuple-element.72), channel_id=1, source_target_pairs={{0,16},{8,24},{16,0},{24,8},{1,17},{9,25},{17,1},{25,9},{2,18},{10... | collective-permute-start | bytes 589832 | tf_op jit(solution)/shard_map/ppermute | solution.py:88
  7.9 9.3 %collective-permute-start.2 = (f32[3,16,1024]{2,1,0:T(8,128)}, f32[3,16,1024]{2,1,0:T(8,128)S(1)}, u32[]{:S(2)}, u32[]{:S(2)}) collective-permute-start(f32[3,16,1024]{2,1,0:T(8,128)} %get-tuple-element.73), channel_id=1, source_target_pairs={{0,24},{8,16},{16,8},{24,0},{1,25},{9,17},{17,9},{25,1},{2,26},{10... | collective-permute-start | bytes 589832 | tf_op jit(solution)/shard_map/ppermute | solution.py:88
  7.9 1.6 copy-start.2
  9.5 0.7 copy-start.10
  10.2 7.0 %copy-start.9 = (f32[3,16,1024]{2,1,0:T(8,128)S(1)}, f32[3,16,1024]{2,1,0:T(8,128)}, u32[]{:S(2)}) copy-start(f32[3,16,1024]{2,1,0:T(8,128)} %get-tuple-element.70.refs_1_) | copy-start | bytes 589828
  10.2 33.3 %copy-start.3 = (bf16[64,192]{1,0:T(8,128)(2,1)S(1)}, bf16[64,192]{1,0:T(8,128)(2,1)}, u32[]{:S(2)}) copy-start(bf16[64,192]{1,0:T(8,128)(2,1)} %constant.12.clone.refs_1_) | copy-start | bytes 73732
  17.8 25.7 %collective-permute-start.10 = (f32[2,64,1024]{2,1,0:T(8,128)S(1)}, f32[2,64,1024]{2,1,0:T(8,128)S(1)}, u32[]{:S(2)}, u32[]{:S(2)}) collective-permute-start(f32[2,64,1024]{2,1,0:T(8,128)S(1)} %get-tuple-element.88.refs_3_), channel_id=1, source_target_pairs={{0,4},{1,5},{6,2},{7,3},{8,12},{9,13},{14,10},{15,11},{16,20},{17,... | collective-permute-start | bytes 1572872 | tf_op jit(solution)/shard_map/ppermute | solution.py:433
  22.4 26.0 %collective-permute-start.9 = (f32[2,64,1024]{2,1,0:T(8,128)S(1)}, f32[2,64,1024]{2,1,0:T(8,128)S(1)}, u32[]{:S(2)}, u32[]{:S(2)}) collective-permute-start(f32[2,64,1024]{2,1,0:T(8,128)S(1)} %get-tuple-element.88.refs_3_), channel_id=1, source_target_pairs={{2,6},{3,7},{4,0},{5,1},{10,14},{11,15},{12,8},{13,9},{18,22},{19,... | collective-permute-start | bytes 1572872 | tf_op jit(solution)/shard_map/ppermute | solution.py:434
  23.7 12.1 %collective-permute-start.3 = (f32[2,16,3072]{2,1,0:T(8,128)S(1)}, f32[2,16,3072]{2,1,0:T(8,128)S(1)}, u32[]{:S(2)}, u32[]{:S(2)}) collective-permute-start(f32[2,16,3072]{2,1,0:T(8,128)S(1)} %get-tuple-element.78), channel_id=1, source_target_pairs={{0,8},{8,0},{16,24},{24,16},{1,9},{9,1},{17,25},{25,17},{2,10},{10... | collective-permute-start | bytes 1179656 | tf_op jit(solution)/shard_map/ppermute | solution.py:88
  25.0 17.8 %collective-permute-start.4 = (f32[2,16,3072]{2,1,0:T(8,128)S(1)}, f32[2,16,3072]{2,1,0:T(8,128)S(1)}, u32[]{:S(2)}, u32[]{:S(2)}) collective-permute-start(f32[2,16,3072]{2,1,0:T(8,128)S(1)} %get-tuple-element.79), channel_id=1, source_target_pairs={{0,16},{8,24},{16,0},{24,8},{1,17},{9,25},{17,1},{25,9},{2,18},{10... | collective-permute-start | bytes 1179656 | tf_op jit(solution)/shard_map/ppermute | solution.py:88
  25.8 17.0 %collective-permute-start.5 = (f32[2,16,3072]{2,1,0:T(8,128)S(1)}, f32[2,16,3072]{2,1,0:T(8,128)S(1)}, u32[]{:S(2)}, u32[]{:S(2)}) collective-permute-start(f32[2,16,3072]{2,1,0:T(8,128)S(1)} %get-tuple-element.80), channel_id=1, source_target_pairs={{0,24},{8,16},{16,8},{24,0},{1,25},{9,17},{17,9},{25,1},{2,26},{10... | collective-permute-start | bytes 1179656 | tf_op jit(solution)/shard_map/ppermute | solution.py:88
  43.5 6.5 %copy-start.4 = (f32[16,2,1,16384]{3,2,1,0:T(1,128)S(1)}, f32[16,2,1,16384]{3,2,1,0:T(1,128)}, u32[]{:S(2)}) copy-start(f32[16,2,1,16384]{3,2,1,0:T(1,128)} %param.9) | copy-start | bytes 6291460
  44.7 20.3 %collective-permute-start.11 = (f32[2,64,1024]{2,1,0:T(8,128)S(1)}, f32[2,64,1024]{2,1,0:T(8,128)S(1)}, u32[]{:S(2)}, u32[]{:S(2)}) collective-permute-start(f32[2,64,1024]{2,1,0:T(8,128)S(1)} %get-tuple-element.92), channel_id=1, source_target_pairs={{0,4},{1,5},{6,2},{7,3},{2,0},{3,1},{4,6},{5,7},{8,12},{9,13},{14,... | collective-permute-start | bytes 1572872 | tf_op jit(solution)/shard_map/ppermute | solution.py:433
  49.9 23.7 %collective-permute-start.12 = (f32[2,64,1024]{2,1,0:T(8,128)S(1)}, f32[2,64,1024]{2,1,0:T(8,128)S(1)}, u32[]{:S(2)}, u32[]{:S(2)}) collective-permute-start(f32[2,64,1024]{2,1,0:T(8,128)S(1)} %get-tuple-element.93), channel_id=1, source_target_pairs={{2,6},{3,7},{4,0},{5,1},{0,2},{1,3},{6,4},{7,5},{10,14},{11,15},{1... | collective-permute-start | bytes 1572872 | tf_op jit(solution)/shard_map/ppermute | solution.py:434
  66.2 16.8 %collective-permute-start.13 = (f32[2,64,1024]{2,1,0:T(8,128)S(1)}, f32[2,64,1024]{2,1,0:T(8,128)S(1)}, u32[]{:S(2)}, u32[]{:S(2)}) collective-permute-start(f32[2,64,1024]{2,1,0:T(8,128)S(1)} %get-tuple-element.100), channel_id=1, source_target_pairs={{0,4},{1,5},{6,2},{7,3},{2,0},{3,1},{4,6},{5,7},{8,12},{9,13},{14,... | collective-permute-start | bytes 1572872 | tf_op jit(solution)/shard_map/ppermute | solution.py:433
  74.7 19.6 %collective-permute-start.14 = (f32[2,64,1024]{2,1,0:T(8,128)S(1)}, f32[2,64,1024]{2,1,0:T(8,128)S(1)}, u32[]{:S(2)}, u32[]{:S(2)}) collective-permute-start(f32[2,64,1024]{2,1,0:T(8,128)S(1)} %get-tuple-element.101), channel_id=1, source_target_pairs={{2,6},{3,7},{4,0},{5,1},{0,2},{1,3},{6,4},{7,5},{10,14},{11,15},{1... | collective-permute-start | bytes 1572872 | tf_op jit(solution)/shard_map/ppermute | solution.py:434
  75.0 24.7 %collective-permute-start.6 = (f32[2,16,4096]{2,1,0:T(8,128)S(1)}, f32[2,16,4096]{2,1,0:T(8,128)S(1)}, u32[]{:S(2)}, u32[]{:S(2)}) collective-permute-start(f32[2,16,4096]{2,1,0:T(8,128)S(1)} %get-tuple-element.84), channel_id=1, source_target_pairs={{0,8},{8,0},{16,24},{24,16},{1,9},{9,1},{17,25},{25,17},{2,10},{10... | collective-permute-start | bytes 1572872 | tf_op jit(solution)/shard_map/ppermute | solution.py:88
  75.8 24.5 %collective-permute-start.7 = (f32[2,16,4096]{2,1,0:T(8,128)S(1)}, f32[2,16,4096]{2,1,0:T(8,128)S(1)}, u32[]{:S(2)}, u32[]{:S(2)}) collective-permute-start(f32[2,16,4096]{2,1,0:T(8,128)S(1)} %get-tuple-element.85), channel_id=1, source_target_pairs={{0,16},{8,24},{16,0},{24,8},{1,17},{9,25},{17,1},{25,9},{2,18},{10... | collective-permute-start | bytes 1572872 | tf_op jit(solution)/shard_map/ppermute | solution.py:88
  76.9 23.3 %collective-permute-start.8 = (f32[2,16,4096]{2,1,0:T(8,128)S(1)}, f32[2,16,4096]{2,1,0:T(8,128)S(1)}, u32[]{:S(2)}, u32[]{:S(2)}) collective-permute-start(f32[2,16,4096]{2,1,0:T(8,128)S(1)} %get-tuple-element.86), channel_id=1, source_target_pairs={{0,24},{8,16},{16,8},{24,0},{1,25},{9,17},{17,9},{25,1},{2,26},{10... | collective-permute-start | bytes 1572872 | tf_op jit(solution)/shard_map/ppermute | solution.py:88
  84.2 20.3 %collective-permute-start.20 = (f32[2,64,1024]{2,1,0:T(8,128)S(1)}, f32[2,64,1024]{2,1,0:T(8,128)S(1)}, u32[]{:S(2)}, u32[]{:S(2)}) collective-permute-start(f32[2,64,1024]{2,1,0:T(8,128)S(1)} %get-tuple-element.112), channel_id=1, source_target_pairs={{0,4},{1,5},{6,2},{7,3},{2,0},{3,1},{4,6},{5,7},{8,12},{9,13},{14,... | collective-permute-start | bytes 1572872 | tf_op jit(solution)/shard_map/ppermute | solution.py:433
  95.2 17.8 %collective-permute-start.21 = (f32[2,64,1024]{2,1,0:T(8,128)S(1)}, f32[2,64,1024]{2,1,0:T(8,128)S(1)}, u32[]{:S(2)}, u32[]{:S(2)}) collective-permute-start(f32[2,64,1024]{2,1,0:T(8,128)S(1)} %get-tuple-element.113), channel_id=1, source_target_pairs={{2,6},{3,7},{4,0},{5,1},{0,2},{1,3},{6,4},{7,5},{10,14},{11,15},{1... | collective-permute-start | bytes 1572872 | tf_op jit(solution)/shard_map/ppermute | solution.py:434
  100.9 1.3 copy-start
  102.3 16.3 %collective-permute-start.15 = (f32[4,64,1024]{2,1,0:T(8,128)S(1)}, f32[4,64,1024]{2,1,0:T(8,128)S(1)}, u32[]{:S(2)}, u32[]{:S(2)}) collective-permute-start(f32[4,64,1024]{2,1,0:T(8,128)S(1)} %get-tuple-element.98.refs_5_), channel_id=1, source_target_pairs={{0,1},{1,0},{2,3},{3,2},{4,5},{5,4},{6,7},{7,6},{8,9},{9,8},{10,11... | collective-permute-start | bytes 3145736 | tf_op jit(solution)/shard_map/ppermute | solution.py:88
  102.9 15.7 %collective-permute-start.16 = (f32[4,64,1024]{2,1,0:T(8,128)S(1)}, f32[4,64,1024]{2,1,0:T(8,128)S(1)}, u32[]{:S(2)}, u32[]{:S(2)}) collective-permute-start(f32[4,64,1024]{2,1,0:T(8,128)S(1)} %get-tuple-element.106.refs_6_), channel_id=1, source_target_pairs={{0,1},{1,0},{2,3},{3,2},{4,5},{5,4},{6,7},{7,6},{8,9},{9,8},{10,11... | collective-permute-start | bytes 3145736 | tf_op jit(solution)/shard_map/ppermute | solution.py:88
  105.8 12.8 %copy-start.6 = (f32[1,16384]{1,0:T(1,128)S(1)}, f32[1,16384]{1,0:T(1,128)}, u32[]{:S(2)}) copy-start(f32[1,16384]{1,0:T(1,128)} %param.12) | copy-start | bytes 196612
  105.8 12.8 %copy-start.7 = (bf16[64,192]{1,0:T(8,128)(2,1)S(1)}, bf16[64,192]{1,0:T(8,128)(2,1)}, u32[]{:S(2)}) copy-start(bf16[64,192]{1,0:T(8,128)(2,1)} %constant.13.clone.refs_1_) | copy-start | bytes 73732
  114.6 6.8 %collective-permute-start.22 = (f32[4,64,1024]{2,1,0:T(8,128)S(1)}, f32[4,64,1024]{2,1,0:T(8,128)S(1)}, u32[]{:S(2)}, u32[]{:S(2)}) collective-permute-start(f32[4,64,1024]{2,1,0:T(8,128)S(1)} %get-tuple-element.118.refs_5_), channel_id=1, source_target_pairs={{0,1},{1,0},{2,3},{3,2},{4,5},{5,4},{6,7},{7,6},{8,9},{9,8},{10,11... | collective-permute-start | bytes 3145736 | tf_op jit(solution)/shard_map/ppermute | solution.py:88
  114.8 14.3 %collective-permute-start.27 = (f32[2,64,1024]{2,1,0:T(8,128)S(1)}, f32[2,64,1024]{2,1,0:T(8,128)S(1)}, u32[]{:S(2)}, u32[]{:S(2)}) collective-permute-start(f32[2,64,1024]{2,1,0:T(8,128)S(1)} %get-tuple-element.125), channel_id=1, source_target_pairs={{0,2},{1,3},{6,4},{7,5},{8,10},{9,11},{14,12},{15,13},{16,18},{17,... | collective-permute-start | bytes 1572872 | tf_op jit(solution)/shard_map/ppermute | solution.py:465
  117.3 15.9 %collective-permute-start.26 = (f32[2,64,1024]{2,1,0:T(8,128)S(1)}, f32[2,64,1024]{2,1,0:T(8,128)S(1)}, u32[]{:S(2)}, u32[]{:S(2)}) collective-permute-start(f32[2,64,1024]{2,1,0:T(8,128)S(1)} %get-tuple-element.124), channel_id=1, source_target_pairs={{2,0},{3,1},{4,6},{5,7},{10,8},{11,9},{12,14},{13,15},{18,16},{19,... | collective-permute-start | bytes 1572872 | tf_op jit(solution)/shard_map/ppermute | solution.py:464
  118.6 2.8 %copy-start.1 = (f32[2,64,4096]{2,1,0:T(8,128)S(1)}, f32[2,64,4096]{2,1,0:T(8,128)}, u32[]{:S(2)}) copy-start(f32[2,64,4096]{2,1,0:T(8,128)} %copy-done) | copy-start | bytes 6291460
  134.4 6.9 %collective-permute-start.28 = (f32[4,64,1024]{2,1,0:T(8,128)S(1)}, f32[4,64,1024]{2,1,0:T(8,128)S(1)}, u32[]{:S(2)}, u32[]{:S(2)}) collective-permute-start(f32[4,64,1024]{2,1,0:T(8,128)S(1)} %get-tuple-element.129.refs_5_), channel_id=1, source_target_pairs={{0,1},{1,0},{2,3},{3,2},{4,5},{5,4},{6,7},{7,6},{8,9},{9,8},{10,11... | collective-permute-start | bytes 3145736 | tf_op jit(solution)/shard_map/ppermute | solution.py:88
  134.4 10.5 %collective-permute-start.17 = (f32[2,16,2048]{2,1,0:T(8,128)S(1)}, f32[2,16,2048]{2,1,0:T(8,128)S(1)}, u32[]{:S(2)}, u32[]{:S(2)}) collective-permute-start(f32[2,16,2048]{2,1,0:T(8,128)S(1)} %get-tuple-element.108), channel_id=1, source_target_pairs={{0,8},{8,0},{16,24},{24,16},{1,9},{9,1},{17,25},{25,17},{2,10},{10... | collective-permute-start | bytes 786440 | tf_op jit(solution)/shard_map/ppermute | solution.py:88
  137.8 14.8 %collective-permute-start.18 = (f32[2,16,2048]{2,1,0:T(8,128)S(1)}, f32[2,16,2048]{2,1,0:T(8,128)S(1)}, u32[]{:S(2)}, u32[]{:S(2)}) collective-permute-start(f32[2,16,2048]{2,1,0:T(8,128)S(1)} %get-tuple-element.109), channel_id=1, source_target_pairs={{0,16},{8,24},{16,0},{24,8},{1,17},{9,25},{17,1},{25,9},{2,18},{10... | collective-permute-start | bytes 786440 | tf_op jit(solution)/shard_map/ppermute | solution.py:88
  138.1 14.4 %collective-permute-start.19 = (f32[2,16,2048]{2,1,0:T(8,128)S(1)}, f32[2,16,2048]{2,1,0:T(8,128)S(1)}, u32[]{:S(2)}, u32[]{:S(2)}) collective-permute-start(f32[2,16,2048]{2,1,0:T(8,128)S(1)} %get-tuple-element.110), channel_id=1, source_target_pairs={{0,24},{8,16},{16,8},{24,0},{1,25},{9,17},{17,9},{25,1},{2,26},{10... | collective-permute-start | bytes 786440 | tf_op jit(solution)/shard_map/ppermute | solution.py:88
  139.2 14.2 %collective-permute-start.23 = (f32[2,16,1024]{2,1,0:T(8,128)S(1)}, f32[2,16,1024]{2,1,0:T(8,128)S(1)}, u32[]{:S(2)}, u32[]{:S(2)}) collective-permute-start(f32[2,16,1024]{2,1,0:T(8,128)S(1)} %get-tuple-element.120), channel_id=1, source_target_pairs={{0,8},{8,0},{16,24},{24,16},{1,9},{9,1},{17,25},{25,17},{2,10},{10... | collective-permute-start | bytes 393224 | tf_op jit(solution)/shard_map/ppermute | solution.py:88
  141.3 21.8 %copy-start.5 = (f32[16,2,1,16384]{3,2,1,0:T(1,128)S(1)}, f32[16,2,1,16384]{3,2,1,0:T(1,128)}, u32[]{:S(2)}) copy-start(f32[16,2,1,16384]{3,2,1,0:T(1,128)} %param.13) | copy-start | bytes 6291460
  141.3 16.9 %collective-permute-start.24 = (f32[2,16,1024]{2,1,0:T(8,128)S(1)}, f32[2,16,1024]{2,1,0:T(8,128)S(1)}, u32[]{:S(2)}, u32[]{:S(2)}) collective-permute-start(f32[2,16,1024]{2,1,0:T(8,128)S(1)} %get-tuple-element.121), channel_id=1, source_target_pairs={{0,16},{8,24},{16,0},{24,8},{1,17},{9,25},{17,1},{25,9},{2,18},{10... | collective-permute-start | bytes 393224 | tf_op jit(solution)/shard_map/ppermute | solution.py:88
  144.9 13.2 %collective-permute-start.25 = (f32[2,16,1024]{2,1,0:T(8,128)S(1)}, f32[2,16,1024]{2,1,0:T(8,128)S(1)}, u32[]{:S(2)}, u32[]{:S(2)}) collective-permute-start(f32[2,16,1024]{2,1,0:T(8,128)S(1)} %get-tuple-element.122), channel_id=1, source_target_pairs={{0,24},{8,16},{16,8},{24,0},{1,25},{9,17},{17,9},{25,1},{2,26},{10... | collective-permute-start | bytes 393224 | tf_op jit(solution)/shard_map/ppermute | solution.py:88
  152.5 6.5 %collective-permute-start.29 = (f32[2,16,1024]{2,1,0:T(8,128)S(1)}, f32[2,16,1024]{2,1,0:T(8,128)S(1)}, u32[]{:S(2)}, u32[]{:S(2)}) collective-permute-start(f32[2,16,1024]{2,1,0:T(8,128)S(1)} %get-tuple-element.131), channel_id=1, source_target_pairs={{0,8},{8,0},{16,24},{24,16},{1,9},{9,1},{17,25},{25,17},{2,10},{10... | collective-permute-start | bytes 393224 | tf_op jit(solution)/shard_map/ppermute | solution.py:88
  152.5 10.5 %collective-permute-start.30 = (f32[2,16,1024]{2,1,0:T(8,128)S(1)}, f32[2,16,1024]{2,1,0:T(8,128)S(1)}, u32[]{:S(2)}, u32[]{:S(2)}) collective-permute-start(f32[2,16,1024]{2,1,0:T(8,128)S(1)} %get-tuple-element.132), channel_id=1, source_target_pairs={{0,16},{8,24},{16,0},{24,8},{1,17},{9,25},{17,1},{25,9},{2,18},{10... | collective-permute-start | bytes 393224 | tf_op jit(solution)/shard_map/ppermute | solution.py:88
  153.4 9.7 %collective-permute-start.31 = (f32[2,16,1024]{2,1,0:T(8,128)S(1)}, f32[2,16,1024]{2,1,0:T(8,128)S(1)}, u32[]{:S(2)}, u32[]{:S(2)}) collective-permute-start(f32[2,16,1024]{2,1,0:T(8,128)S(1)} %get-tuple-element.133), channel_id=1, source_target_pairs={{0,24},{8,16},{16,8},{24,0},{1,25},{9,17},{17,9},{25,1},{2,26},{10... | collective-permute-start | bytes 393224 | tf_op jit(solution)/shard_map/ppermute | solution.py:88

commit v3 on v2

--- a/solution.py
+++ b/solution.py
@@ -11,7 +11,7 @@
 
 LANES = 128
 CHUNK_SHARES = (8, 8, 8, 8)
-FLUX_GROUPS = ((0, 1), (2,), (3,))
+FLUX_GROUPS = ((0,), (1,), (2,), (3,))
 WEIGHTS_TOGETHER = False
 RESULTS_TOGETHER = False
 REST_TOGETHER = False
@@ -19,7 +19,9 @@
 PAIR_AFTER = True
 PAIR_GATE = 1
 FLUX_GATE = 2
-SEEN_GATE = 9
+SEEN_GATE = 2
+SEEN_GROUPS = (0, 1)
+TAIL_PAIR = 0
 PACK_GATE = 1
 WEIGHT_GATE = 3
 REST_FIRST = True
@@ -134,7 +136,10 @@
         numbers = jnp.where(lane == 0, shifts[j], jnp.where(lane == 1, offsets[0, j], offsets[1, j]))
         plan = jnp.where(row == j, numbers, plan)
     for i in range(parts):
-        outs[i * len(spans)][2, :, :LANES] = plan.astype(jnp.float32)
+        out = outs[i * len(spans)]
+        behind = spans[0][1] * LANES
+        out[0, :, behind:] = plan.astype(jnp.float32)
+        out[1, :, behind:] = jnp.zeros(plan.shape, jnp.float32)
 
 
 def seen_kernel(place, *pieces):
@@ -151,7 +156,7 @@
         first = i * rows if together else pl.multiple_of((place[0] ^ i) * rows, rows)
         lane = 0
         for out in outs:
-            out[:, pl.ds(first, rows), :] = pieces[i][:2, :, lane : lane + out.shape[2]]
+            out[:, pl.ds(first, rows), :] = pieces[i][:, :, lane : lane + out.shape[2]]
             lane += out.shape[2]
 
 
@@ -161,7 +166,7 @@
     rows = pieces[0].shape[1]
     for i in range(parts):
         first = pl.multiple_of((place[0] ^ i) * rows, rows)
-        numbers = pieces[i][2, :, :LANES].astype(jnp.int32)
+        numbers = pieces[i][0, :, own.shape[2] :].astype(jnp.int32)
         for n in range(3):
             plan[n, pl.ds(first, rows), :] = jnp.broadcast_to(numbers[:, n : n + 1], (rows, LANES))
 
@@ -341,7 +346,7 @@
     def pack(x, spans, after=(), plan=(), together=False):
         low = spans[0][0] // SUBLANES * SUBLANES
         high = -(-(spans[-1][0] + spans[-1][1]) // SUBLANES) * SUBLANES
-        shape = (3 if plan else 2, x.shape[0], spans[0][1] * LANES)
+        shape = (2, x.shape[0], (spans[0][1] + bool(plan)) * LANES)
         *outs, token = call(
             functools.partial(head_kernel if plan else pack_kernel, parts, spans, together),
             [f32(parts, *shape)] if together else [f32(*shape)] * parts,
@@ -458,9 +463,9 @@
                     made, token = flux(group, pairs)
                     pieces += made
                     gates.setdefault(min(k + FLUX_GATE, chunks), []).append(token)
-                    if k + SEEN_GATE <= chunks:
+                    if group[-1] in SEEN_GROUPS:
                         (token,) = call(functools.partial(seen_kernel), [], (place, *made))
-                        gates.setdefault(k + SEEN_GATE, []).append(token)
+                        gates.setdefault(min(k + SEEN_GATE, chunks), []).append(token)
     slot_a = lax.ppermute(send_a, "azim", sample_a)
     slot_b = lax.ppermute(send_b, "azim", sample_b)
     *pair, _ = neighbours(keeps[-1], slot_a, slot_b, gates.get(chunks, ()))

time: 166 us -> 157 us (0.946)
  waiting for transfers between devices: 87.5 us -> 75 us
  starting transfers between devices: 46.3 us -> 50.4 us
    ppermute x22 -> x25, waiting for transfers between devices: 37.4 us -> 46 us  [xor_permute(): return lax.ppermute(value, axis, [(i, i ^ step) for i in range(count)])]
    ppermute x22 -> x25, starting transfers between devices: 24.1 us -> 32.6 us  [xor_permute(): return lax.ppermute(value, axis, [(i, i ^ step) for i in range(count)])]
    ppermute x4, waiting for transfers between devices: 20.6 us -> 13.4 us  [body(): lax.ppermute(send_b, 'azim', coeff_b + (sample_b if k else []))]
    ppermute x1, waiting for transfers between devices: 6.46 us -> 0.01 us  [body(): slot_b = lax.ppermute(send_b, 'azim', sample_b)]
    ppermute x1, waiting for transfers between devices: 4.15 us -> 0.01 us  [body(): slot_a = lax.ppermute(send_a, 'azim', sample_a)]
    ppermute x4, waiting for transfers between devices: 18.9 us -> 15.6 us  [body(): lax.ppermute(send_a, 'azim', coeff_a + (sample_a if k else []))]
    ppermute x4, starting transfers between devices: 12.3 us -> 8.99 us  [body(): lax.ppermute(send_a, 'azim', coeff_a + (sample_a if k else []))]
    ppermute x4, starting transfers between devices: 6.09 us -> 2.9 us  [body(): lax.ppermute(send_b, 'azim', coeff_b + (sample_b if k else []))]
  transfers between devices with their start and end apart: 32 -> 35, of which waited for: 19 -> 19; matrix products, arithmetic and copies ran while one was open for 0% -> 0% of each run, Pallas kernels for 12% -> 13%
where the time goes in v3:
time: 157 us; the launch traced here: 156 us
  waiting for transfers between devices  75 us (48%)
  starting transfers between devices  50.4 us (32%)
  Pallas kernels  27.9 us (18%)
  local copies, waits for them, and re-layouts  2.29 us (1%)
    ppermute x25, waiting for transfers between devices, xor_permute(): return lax.ppermute(value, axis, [(i, i ^ step) for i in range(count)])  46 us
    ppermute x25, starting transfers between devices, xor_permute(): return lax.ppermute(value, axis, [(i, i ^ step) for i in range(count)])  32.6 us
    pallas_call x25, Pallas kernels, call(): pl.pallas_call(run, name=kernel.func.__name__, out_shape=[jax.ShapeDtypeS...  27.9 us
    ppermute x4, waiting for transfers between devices, body(): lax.ppermute(send_a, 'azim', coeff_a + (sample_a if k else []))  15.6 us
    ppermute x4, waiting for transfers between devices, body(): lax.ppermute(send_b, 'azim', coeff_b + (sample_b if k else []))  13.4 us
    ppermute x4, starting transfers between devices, body(): lax.ppermute(send_a, 'azim', coeff_a + (sample_a if k else []))  8.99 us
    ppermute x1, starting transfers between devices, body(): slot_b = lax.ppermute(send_b, 'azim', sample_b)  4.61 us
  transfers between devices with their start and end apart: 35, of which 19 were waited for; matrix products, arithmetic and copies ran while one was open for 0% of the time, Pallas kernels for 13%

profile of v3, /device:TPU:0, one launch (start us, length us, event | category | flops | bytes accessed | tf_op | source)
XLA Modules:
  0.0 156.5 jit_solution(15462950285591315652)
XLA Ops:
  0.6 2.7 %head_kernel.1 = (f32[2,16,1152]{2,1,0:T(8,128)}, f32[2,16,1152]{2,1,0:T(8,128)}, f32[2,16,1152]{2,1,0:T(8,128)}, f32[2,16,1152]{2,1,0:T(8,128)}, f32[8,128]{1,0:T(8,128)}) custom-call(s32[2]{0:T(128)} %pad_add_fusion.refs_0_, f32[16,2,128,128]{3,2,1,0:T(8,128)} %bitcast.8, s32[16]{0:T(128)} %refs_2_.1, s32[2,16]{1,0:T(2,128)} %bitcast.16), custom_call_target="tpu_custom_call" | custom-call | bytes 2687176 | tf_op jit(solution)/shard_map/head_kernel/pallas_call | solution.py:76
  3.3 3.0 %collective-permute-start = (f32[2,16,1152]{2,1,0:T(8,128)}, f32[2,16,1152]{2,1,0:T(8,128)S(1)}, u32[]{:S(2)}, u32[]{:S(2)}) collective-permute-start(f32[2,16,1152]{2,1,0:T(8,128)} %get-tuple-element.76), channel_id=1, source_target_pairs={{0,8},{8,0},{16,24},{24,16},{1,9},{9,1},{17,25},{25,17},{2,10},{10... | collective-permute-start | bytes 442376 | tf_op jit(solution)/shard_map/ppermute | solution.py:90
  6.3 1.5 collective-permute-start.1
  7.8 1.6 %copy-done = f32[16,2,1,16384]{3,2,1,0:T(1,128)S(1)} copy-done((f32[16,2,1,16384]{3,2,1,0:T(1,128)S(1)}, f32[16,2,1,16384]{3,2,1,0:T(1,128)}, u32[]{:S(2)}) %copy-start) | copy-done | bytes 2097176
  11.2 3.8 %collective-permute-done.1.refs_3_ = f32[2,16,1152]{2,1,0:T(8,128)S(1)} collective-permute-done((f32[2,16,1152]{2,1,0:T(8,128)}, f32[2,16,1152]{2,1,0:T(8,128)S(1)}, u32[]{:S(2)}, u32[]{:S(2)}) %collective-permute-start.1) | collective-permute-done | bytes 147488 | tf_op jit(solution)/shard_map/ppermute | solution.py:90
  15.6 4.5 %collective-permute-start.10 = (f32[2,64,1024]{2,1,0:T(8,128)S(1)}, f32[2,64,1024]{2,1,0:T(8,128)S(1)}, u32[]{:S(2)}, u32[]{:S(2)}) collective-permute-start(f32[2,64,1024]{2,1,0:T(8,128)S(1)} %get-tuple-element.93.refs_3_), channel_id=1, source_target_pairs={{0,4},{1,5},{6,2},{7,3},{8,12},{9,13},{14,10},{15,11},{16,20},{17,... | collective-permute-start | bytes 1572872 | tf_op jit(solution)/shard_map/ppermute | solution.py:438
  20.2 1.3 collective-permute-start.9
  21.5 1.3 collective-permute-start.3
  23.6 1.4 collective-permute-start.5
  25.0 8.6 %collective-permute-done.3.refs_2_ = f32[2,16,3072]{2,1,0:T(8,128)S(1)} collective-permute-done((f32[2,16,3072]{2,1,0:T(8,128)S(1)}, f32[2,16,3072]{2,1,0:T(8,128)S(1)}, u32[]{:S(2)}, u32[]{:S(2)}) %collective-permute-start.3) | collective-permute-done | bytes 393248 | tf_op jit(solution)/shard_map/ppermute | solution.py:90
  33.6 7.0 %collective-permute-done.4.refs_3_ = f32[2,16,3072]{2,1,0:T(8,128)S(1)} collective-permute-done((f32[2,16,3072]{2,1,0:T(8,128)S(1)}, f32[2,16,3072]{2,1,0:T(8,128)S(1)}, u32[]{:S(2)}, u32[]{:S(2)}) %collective-permute-start.4) | collective-permute-done | bytes 393248 | tf_op jit(solution)/shard_map/ppermute | solution.py:90
  41.3 1.2 first_kernel.4
  42.5 3.6 %collective-permute-start.11 = (f32[2,64,1024]{2,1,0:T(8,128)S(1)}, f32[2,64,1024]{2,1,0:T(8,128)S(1)}, u32[]{:S(2)}, u32[]{:S(2)}) collective-permute-start(f32[2,64,1024]{2,1,0:T(8,128)S(1)} %get-tuple-element.97), channel_id=1, source_target_pairs={{0,4},{1,5},{6,2},{7,3},{2,0},{3,1},{4,6},{5,7},{8,12},{9,13},{14,... | collective-permute-start | bytes 1572872 | tf_op jit(solution)/shard_map/ppermute | solution.py:438
  46.2 1.6 %second_kernel.4 = (f32[2,64,1024]{2,1,0:T(8,128)S(1)}, f32[2,64,1024]{2,1,0:T(8,128)S(1)}, f32[8,128]{1,0:T(8,128)}) custom-call(s32[2]{0:T(128)S(1)} %copy-done.6, bf16[64,192]{1,0:T(8,128)(2,1)S(1)} %copy-done.1, s32[3,64,128]{2,1,0:T(8,128)S(1)} %get-tuple-element.81.refs_2_, f32[2,64,1024]{2,1,0:T(8,128)S(1)} %get-tuple-element.93.refs_3_, ...), custom_call_target="tpu_custom_call" | custom-call | flops 100663296 | bytes 3293192 | tf_op jit(solution)/shard_map/second_kernel/pallas_call | solution.py:76
  47.7 1.1 pack_kernel.3
  48.9 13.9 %collective-permute-done.11.refs_4_.refs_2_ = f32[2,64,1024]{2,1,0:T(8,128)S(1)} collective-permute-done((f32[2,64,1024]{2,1,0:T(8,128)S(1)}, f32[2,64,1024]{2,1,0:T(8,128)S(1)}, u32[]{:S(2)}, u32[]{:S(2)}) %collective-permute-start.11) | collective-permute-done | bytes 524320 | tf_op jit(solution)/shard_map/ppermute | solution.py:438
  62.8 1.2 first_kernel.5
  64.4 7.2 %collective-permute-done.12.refs_4_.refs_3_ = f32[2,64,1024]{2,1,0:T(8,128)S(1)} collective-permute-done((f32[2,64,1024]{2,1,0:T(8,128)S(1)}, f32[2,64,1024]{2,1,0:T(8,128)S(1)}, u32[]{:S(2)}, u32[]{:S(2)}) %collective-permute-start.12) | collective-permute-done | bytes 524320 | tf_op jit(solution)/shard_map/ppermute | solution.py:439
  75.4 1.7 %collective-permute-done.17.refs_4_.refs_2_ = f32[2,64,1024]{2,1,0:T(8,128)S(1)} collective-permute-done((f32[2,64,1024]{2,1,0:T(8,128)S(1)}, f32[2,64,1024]{2,1,0:T(8,128)S(1)}, u32[]{:S(2)}, u32[]{:S(2)}) %collective-permute-start.17) | collective-permute-done | bytes 524320 | tf_op jit(solution)/shard_map/ppermute | solution.py:438
  77.1 4.8 %collective-permute-start.8 = (f32[2,16,4096]{2,1,0:T(8,128)S(1)}, f32[2,16,4096]{2,1,0:T(8,128)S(1)}, u32[]{:S(2)}, u32[]{:S(2)}) collective-permute-start(f32[2,16,4096]{2,1,0:T(8,128)S(1)} %get-tuple-element.91), channel_id=1, source_target_pairs={{0,24},{8,16},{16,8},{24,0},{1,25},{9,17},{17,9},{25,1},{2,26},{10... | collective-permute-start | bytes 1572872 | tf_op jit(solution)/shard_map/ppermute | solution.py:90
  81.9 1.2 first_kernel.6
  83.1 5.5 %collective-permute-done.18.refs_4_.refs_3_ = f32[2,64,1024]{2,1,0:T(8,128)S(1)} collective-permute-done((f32[2,64,1024]{2,1,0:T(8,128)S(1)}, f32[2,64,1024]{2,1,0:T(8,128)S(1)}, u32[]{:S(2)}, u32[]{:S(2)}) %collective-permute-start.18) | collective-permute-done | bytes 524320 | tf_op jit(solution)/shard_map/ppermute | solution.py:439
  90.0 1.3 collective-permute-start.24
  91.3 8.1 %collective-permute-done.7.refs_3_ = f32[2,16,4096]{2,1,0:T(8,128)S(1)} collective-permute-done((f32[2,16,4096]{2,1,0:T(8,128)S(1)}, f32[2,16,4096]{2,1,0:T(8,128)S(1)}, u32[]{:S(2)}, u32[]{:S(2)}) %collective-permute-start.7) | collective-permute-done | bytes 524320 | tf_op jit(solution)/shard_map/ppermute | solution.py:90
  101.2 1.3 collective-permute-start.14
  103.8 2.4 %collective-permute-done.14.refs_2_.refs_3_ = f32[2,16,1024]{2,1,0:T(8,128)S(1)} collective-permute-done((f32[2,16,1024]{2,1,0:T(8,128)S(1)}, f32[2,16,1024]{2,1,0:T(8,128)S(1)}, u32[]{:S(2)}, u32[]{:S(2)}) %collective-permute-start.14) | collective-permute-done | bytes 131104 | tf_op jit(solution)/shard_map/ppermute | solution.py:90
  106.3 1.2 collective-permute-start.16
  107.5 3.1 %collective-permute-done.15.refs_3_.refs_4_ = f32[2,16,1024]{2,1,0:T(8,128)S(1)} collective-permute-done((f32[2,16,1024]{2,1,0:T(8,128)S(1)}, f32[2,16,1024]{2,1,0:T(8,128)S(1)}, u32[]{:S(2)}, u32[]{:S(2)}) %collective-permute-start.15) | collective-permute-done | bytes 131104 | tf_op jit(solution)/shard_map/ppermute | solution.py:90
  110.6 1.6 collective-permute-done.16.refs_4_.refs_5_
  112.7 1.2 first_kernel.7
  116.3 1.3 collective-permute-start.29
  117.6 4.6 %collective-permute-start.30 = (f32[2,64,1024]{2,1,0:T(8,128)S(1)}, f32[2,64,1024]{2,1,0:T(8,128)S(1)}, u32[]{:S(2)}, u32[]{:S(2)}) collective-permute-start(f32[2,64,1024]{2,1,0:T(8,128)S(1)} %get-tuple-element.135), channel_id=1, source_target_pairs={{0,2},{1,3},{6,4},{7,5},{8,10},{9,11},{14,12},{15,13},{16,18},{17,... | collective-permute-start | bytes 1572872 | tf_op jit(solution)/shard_map/ppermute | solution.py:470
  122.3 1.1 flux_kernel.5
  123.4 2.1 %collective-permute-start.20 = (f32[2,16,1024]{2,1,0:T(8,128)S(1)}, f32[2,16,1024]{2,1,0:T(8,128)S(1)}, u32[]{:S(2)}, u32[]{:S(2)}) collective-permute-start(f32[2,16,1024]{2,1,0:T(8,128)S(1)} %get-tuple-element.117), channel_id=1, source_target_pairs={{0,8},{8,0},{16,24},{24,16},{1,9},{9,1},{17,25},{25,17},{2,10},{10... | collective-permute-start | bytes 393224 | tf_op jit(solution)/shard_map/ppermute | solution.py:90
  125.5 1.8 %collective-permute-start.21 = (f32[2,16,1024]{2,1,0:T(8,128)S(1)}, f32[2,16,1024]{2,1,0:T(8,128)S(1)}, u32[]{:S(2)}, u32[]{:S(2)}) collective-permute-start(f32[2,16,1024]{2,1,0:T(8,128)S(1)} %get-tuple-element.118), channel_id=1, source_target_pairs={{0,16},{8,24},{16,0},{24,8},{1,17},{9,25},{17,1},{25,9},{2,18},{10... | collective-permute-start | bytes 393224 | tf_op jit(solution)/shard_map/ppermute | solution.py:90
  127.3 1.8 %collective-permute-done.20.refs_2_.refs_7_ = f32[2,16,1024]{2,1,0:T(8,128)S(1)} collective-permute-done((f32[2,16,1024]{2,1,0:T(8,128)S(1)}, f32[2,16,1024]{2,1,0:T(8,128)S(1)}, u32[]{:S(2)}, u32[]{:S(2)}) %collective-permute-start.20) | collective-permute-done | bytes 131104 | tf_op jit(solution)/shard_map/ppermute | solution.py:90
  129.1 3.0 %collective-permute-start.22 = (f32[2,16,1024]{2,1,0:T(8,128)S(1)}, f32[2,16,1024]{2,1,0:T(8,128)S(1)}, u32[]{:S(2)}, u32[]{:S(2)}) collective-permute-start(f32[2,16,1024]{2,1,0:T(8,128)S(1)} %get-tuple-element.119), channel_id=1, source_target_pairs={{0,24},{8,16},{16,8},{24,0},{1,25},{9,17},{17,9},{25,1},{2,26},{10... | collective-permute-start | bytes 393224 | tf_op jit(solution)/shard_map/ppermute | solution.py:90
  132.1 2.9 %collective-permute-done.22.refs_4_.refs_9_ = f32[2,16,1024]{2,1,0:T(8,128)S(1)} collective-permute-done((f32[2,16,1024]{2,1,0:T(8,128)S(1)}, f32[2,16,1024]{2,1,0:T(8,128)S(1)}, u32[]{:S(2)}, u32[]{:S(2)}) %collective-permute-start.22) | collective-permute-done | bytes 131104 | tf_op jit(solution)/shard_map/ppermute | solution.py:90
  135.6 1.1 flux_kernel.6
  136.8 1.2 pair_kernel.7
  138.0 1.7 %collective-permute-start.26 = (f32[2,16,1024]{2,1,0:T(8,128)S(1)}, f32[2,16,1024]{2,1,0:T(8,128)S(1)}, u32[]{:S(2)}, u32[]{:S(2)}) collective-permute-start(f32[2,16,1024]{2,1,0:T(8,128)S(1)} %get-tuple-element.130), channel_id=1, source_target_pairs={{0,8},{8,0},{16,24},{24,16},{1,9},{9,1},{17,25},{25,17},{2,10},{10... | collective-permute-start | bytes 393224 | tf_op jit(solution)/shard_map/ppermute | solution.py:90
  139.7 1.8 %collective-permute-start.27 = (f32[2,16,1024]{2,1,0:T(8,128)S(1)}, f32[2,16,1024]{2,1,0:T(8,128)S(1)}, u32[]{:S(2)}, u32[]{:S(2)}) collective-permute-start(f32[2,16,1024]{2,1,0:T(8,128)S(1)} %get-tuple-element.131), channel_id=1, source_target_pairs={{0,16},{8,24},{16,0},{24,8},{1,17},{9,25},{17,1},{25,9},{2,18},{10... | collective-permute-start | bytes 393224 | tf_op jit(solution)/shard_map/ppermute | solution.py:90
  141.6 1.5 flux_kernel.7
  143.1 1.6 %collective-permute-start.32 = (f32[2,16,1024]{2,1,0:T(8,128)S(1)}, f32[2,16,1024]{2,1,0:T(8,128)S(1)}, u32[]{:S(2)}, u32[]{:S(2)}) collective-permute-start(f32[2,16,1024]{2,1,0:T(8,128)S(1)} %get-tuple-element.141), channel_id=1, source_target_pairs={{0,8},{8,0},{16,24},{24,16},{1,9},{9,1},{17,25},{25,17},{2,10},{10... | collective-permute-start | bytes 393224 | tf_op jit(solution)/shard_map/ppermute | solution.py:90
  144.7 1.8 %collective-permute-start.33 = (f32[2,16,1024]{2,1,0:T(8,128)S(1)}, f32[2,16,1024]{2,1,0:T(8,128)S(1)}, u32[]{:S(2)}, u32[]{:S(2)}) collective-permute-start(f32[2,16,1024]{2,1,0:T(8,128)S(1)} %get-tuple-element.142), channel_id=1, source_target_pairs={{0,16},{8,24},{16,0},{24,8},{1,17},{9,25},{17,1},{25,9},{2,18},{10... | collective-permute-start | bytes 393224 | tf_op jit(solution)/shard_map/ppermute | solution.py:90
  148.8 1.6 collective-permute-done.32.refs_15_
  150.4 2.7 %collective-permute-done.33.refs_16_ = f32[2,16,1024]{2,1,0:T(8,128)S(1)} collective-permute-done((f32[2,16,1024]{2,1,0:T(8,128)S(1)}, f32[2,16,1024]{2,1,0:T(8,128)S(1)}, u32[]{:S(2)}, u32[]{:S(2)}) %collective-permute-start.33) | collective-permute-done | bytes 131104 | tf_op jit(solution)/shard_map/ppermute | solution.py:90
  153.9 2.6 %finish_kernel.1 = (f32[16,2,128,128]{3,2,1,0:T(8,128)}, f32[8,128]{1,0:T(8,128)}) custom-call(s32[2]{0:T(128)S(1)} %copy-done.6, f32[16,2,128,128]{3,2,1,0:T(8,128)S(1)} %bitcast.11, f32[2,16,1024]{2,1,0:T(8,128)S(1)} %get-tuple-element.104.refs_1_.refs_2_, f32[2,16,1024]{2,1,0:T(8,128)S(1)} %collective-permute-done.14.refs_2_.refs_3_, ...), custom_call_target="tpu_custom_call" | custom-call | bytes 6291464 | tf_op jit(solution)/shard_map/finish_kernel/pallas_call | solution.py:76
  (66 shorter events, 19.9 us)
Async XLA Ops:
  0.6 7.3 %copy-start.6 = (s32[2]{0:T(128)S(1)}, s32[2]{0:T(128)}, u32[]{:S(2)}) copy-start(s32[2]{0:T(128)} %pad_add_fusion.refs_0_) | copy-start | bytes 28
  3.3 7.9 %collective-permute-start = (f32[2,16,1152]{2,1,0:T(8,128)}, f32[2,16,1152]{2,1,0:T(8,128)S(1)}, u32[]{:S(2)}, u32[]{:S(2)}) collective-permute-start(f32[2,16,1152]{2,1,0:T(8,128)} %get-tuple-element.76), channel_id=1, source_target_pairs={{0,8},{8,0},{16,24},{24,16},{1,9},{9,1},{17,25},{25,17},{2,10},{10... | collective-permute-start | bytes 442376 | tf_op jit(solution)/shard_map/ppermute | solution.py:90
  6.3 8.7 %collective-permute-start.1 = (f32[2,16,1152]{2,1,0:T(8,128)}, f32[2,16,1152]{2,1,0:T(8,128)S(1)}, u32[]{:S(2)}, u32[]{:S(2)}) collective-permute-start(f32[2,16,1152]{2,1,0:T(8,128)} %get-tuple-element.77), channel_id=1, source_target_pairs={{0,16},{8,24},{16,0},{24,8},{1,17},{9,25},{17,1},{25,9},{2,18},{10... | collective-permute-start | bytes 442376 | tf_op jit(solution)/shard_map/ppermute | solution.py:90
  7.8 7.2 %collective-permute-start.2 = (f32[2,16,1152]{2,1,0:T(8,128)}, f32[2,16,1152]{2,1,0:T(8,128)S(1)}, u32[]{:S(2)}, u32[]{:S(2)}) collective-permute-start(f32[2,16,1152]{2,1,0:T(8,128)} %get-tuple-element.78), channel_id=1, source_target_pairs={{0,24},{8,16},{16,8},{24,0},{1,25},{9,17},{17,9},{25,1},{2,26},{10... | collective-permute-start | bytes 442376 | tf_op jit(solution)/shard_map/ppermute | solution.py:90
  7.8 1.6 %copy-start = (f32[16,2,1,16384]{3,2,1,0:T(1,128)S(1)}, f32[16,2,1,16384]{3,2,1,0:T(1,128)}, u32[]{:S(2)}) copy-start(f32[16,2,1,16384]{3,2,1,0:T(1,128)} %param.8) | copy-start | bytes 6291460
  9.4 0.7 copy-start.8
  10.1 4.9 %copy-start.7 = (f32[2,16,1152]{2,1,0:T(8,128)S(1)}, f32[2,16,1152]{2,1,0:T(8,128)}, u32[]{:S(2)}) copy-start(f32[2,16,1152]{2,1,0:T(8,128)} %get-tuple-element.75.refs_1_) | copy-start | bytes 442372
  10.1 31.2 %copy-start.1 = (bf16[64,192]{1,0:T(8,128)(2,1)S(1)}, bf16[64,192]{1,0:T(8,128)(2,1)}, u32[]{:S(2)}) copy-start(bf16[64,192]{1,0:T(8,128)(2,1)} %constant.12.clone.refs_1_) | copy-start | bytes 73732
  15.6 25.7 %collective-permute-start.10 = (f32[2,64,1024]{2,1,0:T(8,128)S(1)}, f32[2,64,1024]{2,1,0:T(8,128)S(1)}, u32[]{:S(2)}, u32[]{:S(2)}) collective-permute-start(f32[2,64,1024]{2,1,0:T(8,128)S(1)} %get-tuple-element.93.refs_3_), channel_id=1, source_target_pairs={{0,4},{1,5},{6,2},{7,3},{8,12},{9,13},{14,10},{15,11},{16,20},{17,... | collective-permute-start | bytes 1572872 | tf_op jit(solution)/shard_map/ppermute | solution.py:438
  20.2 26.0 %collective-permute-start.9 = (f32[2,64,1024]{2,1,0:T(8,128)S(1)}, f32[2,64,1024]{2,1,0:T(8,128)S(1)}, u32[]{:S(2)}, u32[]{:S(2)}) collective-permute-start(f32[2,64,1024]{2,1,0:T(8,128)S(1)} %get-tuple-element.93.refs_3_), channel_id=1, source_target_pairs={{2,6},{3,7},{4,0},{5,1},{10,14},{11,15},{12,8},{13,9},{18,22},{19,... | collective-permute-start | bytes 1572872 | tf_op jit(solution)/shard_map/ppermute | solution.py:439
  21.5 12.1 %collective-permute-start.3 = (f32[2,16,3072]{2,1,0:T(8,128)S(1)}, f32[2,16,3072]{2,1,0:T(8,128)S(1)}, u32[]{:S(2)}, u32[]{:S(2)}) collective-permute-start(f32[2,16,3072]{2,1,0:T(8,128)S(1)} %get-tuple-element.83), channel_id=1, source_target_pairs={{0,8},{8,0},{16,24},{24,16},{1,9},{9,1},{17,25},{25,17},{2,10},{10... | collective-permute-start | bytes 1179656 | tf_op jit(solution)/shard_map/ppermute | solution.py:90
  22.8 17.8 %collective-permute-start.4 = (f32[2,16,3072]{2,1,0:T(8,128)S(1)}, f32[2,16,3072]{2,1,0:T(8,128)S(1)}, u32[]{:S(2)}, u32[]{:S(2)}) collective-permute-start(f32[2,16,3072]{2,1,0:T(8,128)S(1)} %get-tuple-element.84), channel_id=1, source_target_pairs={{0,16},{8,24},{16,0},{24,8},{1,17},{9,25},{17,1},{25,9},{2,18},{10... | collective-permute-start | bytes 1179656 | tf_op jit(solution)/shard_map/ppermute | solution.py:90
  23.6 17.0 %collective-permute-start.5 = (f32[2,16,3072]{2,1,0:T(8,128)S(1)}, f32[2,16,3072]{2,1,0:T(8,128)S(1)}, u32[]{:S(2)}, u32[]{:S(2)}) collective-permute-start(f32[2,16,3072]{2,1,0:T(8,128)S(1)} %get-tuple-element.85), channel_id=1, source_target_pairs={{0,24},{8,16},{16,8},{24,0},{1,25},{9,17},{17,9},{25,1},{2,26},{10... | collective-permute-start | bytes 1179656 | tf_op jit(solution)/shard_map/ppermute | solution.py:90
  41.3 6.5 %copy-start.2 = (f32[16,2,1,16384]{3,2,1,0:T(1,128)S(1)}, f32[16,2,1,16384]{3,2,1,0:T(1,128)}, u32[]{:S(2)}) copy-start(f32[16,2,1,16384]{3,2,1,0:T(1,128)} %param.9) | copy-start | bytes 6291460
  42.5 20.3 %collective-permute-start.11 = (f32[2,64,1024]{2,1,0:T(8,128)S(1)}, f32[2,64,1024]{2,1,0:T(8,128)S(1)}, u32[]{:S(2)}, u32[]{:S(2)}) collective-permute-start(f32[2,64,1024]{2,1,0:T(8,128)S(1)} %get-tuple-element.97), channel_id=1, source_target_pairs={{0,4},{1,5},{6,2},{7,3},{2,0},{3,1},{4,6},{5,7},{8,12},{9,13},{14,... | collective-permute-start | bytes 1572872 | tf_op jit(solution)/shard_map/ppermute | solution.py:438
  47.7 23.9 %collective-permute-start.12 = (f32[2,64,1024]{2,1,0:T(8,128)S(1)}, f32[2,64,1024]{2,1,0:T(8,128)S(1)}, u32[]{:S(2)}, u32[]{:S(2)}) collective-permute-start(f32[2,64,1024]{2,1,0:T(8,128)S(1)} %get-tuple-element.98), channel_id=1, source_target_pairs={{2,6},{3,7},{4,0},{5,1},{0,2},{1,3},{6,4},{7,5},{10,14},{11,15},{1... | collective-permute-start | bytes 1572872 | tf_op jit(solution)/shard_map/ppermute | solution.py:439
  64.0 13.1 %collective-permute-start.17 = (f32[2,64,1024]{2,1,0:T(8,128)S(1)}, f32[2,64,1024]{2,1,0:T(8,128)S(1)}, u32[]{:S(2)}, u32[]{:S(2)}) collective-permute-start(f32[2,64,1024]{2,1,0:T(8,128)S(1)} %get-tuple-element.109), channel_id=1, source_target_pairs={{0,4},{1,5},{6,2},{7,3},{2,0},{3,1},{4,6},{5,7},{8,12},{9,13},{14,... | collective-permute-start | bytes 1572872 | tf_op jit(solution)/shard_map/ppermute | solution.py:438
  73.2 26.8 %collective-permute-start.13 = (f32[4,64,1024]{2,1,0:T(8,128)S(1)}, f32[4,64,1024]{2,1,0:T(8,128)S(1)}, u32[]{:S(2)}, u32[]{:S(2)}) collective-permute-start(f32[4,64,1024]{2,1,0:T(8,128)S(1)} %get-tuple-element.103.refs_5_), channel_id=1, source_target_pairs={{0,1},{1,0},{2,3},{3,2},{4,5},{5,4},{6,7},{7,6},{8,9},{9,8},{10,11... | collective-permute-start | bytes 3145736 | tf_op jit(solution)/shard_map/ppermute | solution.py:90
  73.3 15.2 %collective-permute-start.18 = (f32[2,64,1024]{2,1,0:T(8,128)S(1)}, f32[2,64,1024]{2,1,0:T(8,128)S(1)}, u32[]{:S(2)}, u32[]{:S(2)}) collective-permute-start(f32[2,64,1024]{2,1,0:T(8,128)S(1)} %get-tuple-element.110), channel_id=1, source_target_pairs={{2,6},{3,7},{4,0},{5,1},{0,2},{1,3},{6,4},{7,5},{10,14},{11,15},{1... | collective-permute-start | bytes 1572872 | tf_op jit(solution)/shard_map/ppermute | solution.py:439
  73.6 16.3 %collective-permute-start.6 = (f32[2,16,4096]{2,1,0:T(8,128)S(1)}, f32[2,16,4096]{2,1,0:T(8,128)S(1)}, u32[]{:S(2)}, u32[]{:S(2)}) collective-permute-start(f32[2,16,4096]{2,1,0:T(8,128)S(1)} %get-tuple-element.89), channel_id=1, source_target_pairs={{0,8},{8,0},{16,24},{24,16},{1,9},{9,1},{17,25},{25,17},{2,10},{10... | collective-permute-start | bytes 1572872 | tf_op jit(solution)/shard_map/ppermute | solution.py:90
  74.4 24.9 %collective-permute-start.7 = (f32[2,16,4096]{2,1,0:T(8,128)S(1)}, f32[2,16,4096]{2,1,0:T(8,128)S(1)}, u32[]{:S(2)}, u32[]{:S(2)}) collective-permute-start(f32[2,16,4096]{2,1,0:T(8,128)S(1)} %get-tuple-element.90), channel_id=1, source_target_pairs={{0,16},{8,24},{16,0},{24,8},{1,17},{9,25},{17,1},{25,9},{2,18},{10... | collective-permute-start | bytes 1572872 | tf_op jit(solution)/shard_map/ppermute | solution.py:90
  77.1 22.3 %collective-permute-start.8 = (f32[2,16,4096]{2,1,0:T(8,128)S(1)}, f32[2,16,4096]{2,1,0:T(8,128)S(1)}, u32[]{:S(2)}, u32[]{:S(2)}) collective-permute-start(f32[2,16,4096]{2,1,0:T(8,128)S(1)} %get-tuple-element.91), channel_id=1, source_target_pairs={{0,24},{8,16},{16,8},{24,0},{1,25},{9,17},{17,9},{25,1},{2,26},{10... | collective-permute-start | bytes 1572872 | tf_op jit(solution)/shard_map/ppermute | solution.py:90
  88.6 24.1 %collective-permute-start.23 = (f32[2,64,1024]{2,1,0:T(8,128)S(1)}, f32[2,64,1024]{2,1,0:T(8,128)S(1)}, u32[]{:S(2)}, u32[]{:S(2)}) collective-permute-start(f32[2,64,1024]{2,1,0:T(8,128)S(1)} %get-tuple-element.121), channel_id=1, source_target_pairs={{0,4},{1,5},{6,2},{7,3},{2,0},{3,1},{4,6},{5,7},{8,12},{9,13},{14,... | collective-permute-start | bytes 1572872 | tf_op jit(solution)/shard_map/ppermute | solution.py:438
  89.0 11.1 %copy-start.4 = (f32[1,16384]{1,0:T(1,128)S(1)}, f32[1,16384]{1,0:T(1,128)}, u32[]{:S(2)}) copy-start(f32[1,16384]{1,0:T(1,128)} %param.12) | copy-start | bytes 196612
  89.0 11.1 %copy-start.5 = (bf16[64,192]{1,0:T(8,128)(2,1)S(1)}, bf16[64,192]{1,0:T(8,128)(2,1)}, u32[]{:S(2)}) copy-start(bf16[64,192]{1,0:T(8,128)(2,1)} %constant.13.clone.refs_1_) | copy-start | bytes 73732
  90.0 24.7 %collective-permute-start.24 = (f32[2,64,1024]{2,1,0:T(8,128)S(1)}, f32[2,64,1024]{2,1,0:T(8,128)S(1)}, u32[]{:S(2)}, u32[]{:S(2)}) collective-permute-start(f32[2,64,1024]{2,1,0:T(8,128)S(1)} %get-tuple-element.122), channel_id=1, source_target_pairs={{2,6},{3,7},{4,0},{5,1},{0,2},{1,3},{6,4},{7,5},{10,14},{11,15},{1... | collective-permute-start | bytes 1572872 | tf_op jit(solution)/shard_map/ppermute | solution.py:439
  101.2 5.0 %collective-permute-start.14 = (f32[2,16,1024]{2,1,0:T(8,128)S(1)}, f32[2,16,1024]{2,1,0:T(8,128)S(1)}, u32[]{:S(2)}, u32[]{:S(2)}) collective-permute-start(f32[2,16,1024]{2,1,0:T(8,128)S(1)} %get-tuple-element.105), channel_id=1, source_target_pairs={{0,8},{8,0},{16,24},{24,16},{1,9},{9,1},{17,25},{25,17},{2,10},{10... | collective-permute-start | bytes 393224 | tf_op jit(solution)/shard_map/ppermute | solution.py:90
  103.2 19.1 %collective-permute-start.19 = (f32[4,64,1024]{2,1,0:T(8,128)S(1)}, f32[4,64,1024]{2,1,0:T(8,128)S(1)}, u32[]{:S(2)}, u32[]{:S(2)}) collective-permute-start(f32[4,64,1024]{2,1,0:T(8,128)S(1)} %get-tuple-element.115.refs_5_), channel_id=1, source_target_pairs={{0,1},{1,0},{2,3},{3,2},{4,5},{5,4},{6,7},{7,6},{8,9},{9,8},{10,11... | collective-permute-start | bytes 3145736 | tf_op jit(solution)/shard_map/ppermute | solution.py:90
  103.3 7.3 %collective-permute-start.15 = (f32[2,16,1024]{2,1,0:T(8,128)S(1)}, f32[2,16,1024]{2,1,0:T(8,128)S(1)}, u32[]{:S(2)}, u32[]{:S(2)}) collective-permute-start(f32[2,16,1024]{2,1,0:T(8,128)S(1)} %get-tuple-element.106), channel_id=1, source_target_pairs={{0,16},{8,24},{16,0},{24,8},{1,17},{9,25},{17,1},{25,9},{2,18},{10... | collective-permute-start | bytes 393224 | tf_op jit(solution)/shard_map/ppermute | solution.py:90
  106.3 5.9 %collective-permute-start.16 = (f32[2,16,1024]{2,1,0:T(8,128)S(1)}, f32[2,16,1024]{2,1,0:T(8,128)S(1)}, u32[]{:S(2)}, u32[]{:S(2)}) collective-permute-start(f32[2,16,1024]{2,1,0:T(8,128)S(1)} %get-tuple-element.107), channel_id=1, source_target_pairs={{0,24},{8,16},{16,8},{24,0},{1,25},{9,17},{17,9},{25,1},{2,26},{10... | collective-permute-start | bytes 393224 | tf_op jit(solution)/shard_map/ppermute | solution.py:90
  116.3 19.3 %collective-permute-start.25 = (f32[4,64,1024]{2,1,0:T(8,128)S(1)}, f32[4,64,1024]{2,1,0:T(8,128)S(1)}, u32[]{:S(2)}, u32[]{:S(2)}) collective-permute-start(f32[4,64,1024]{2,1,0:T(8,128)S(1)} %get-tuple-element.128.refs_5_), channel_id=1, source_target_pairs={{0,1},{1,0},{2,3},{3,2},{4,5},{5,4},{6,7},{7,6},{8,9},{9,8},{10,11... | collective-permute-start | bytes 3145736 | tf_op jit(solution)/shard_map/ppermute | solution.py:90
  116.3 20.4 %collective-permute-start.29 = (f32[2,64,1024]{2,1,0:T(8,128)S(1)}, f32[2,64,1024]{2,1,0:T(8,128)S(1)}, u32[]{:S(2)}, u32[]{:S(2)}) collective-permute-start(f32[2,64,1024]{2,1,0:T(8,128)S(1)} %get-tuple-element.134), channel_id=1, source_target_pairs={{2,0},{3,1},{4,6},{5,7},{10,8},{11,9},{12,14},{13,15},{18,16},{19,... | collective-permute-start | bytes 1572872 | tf_op jit(solution)/shard_map/ppermute | solution.py:469
  117.6 19.1 %collective-permute-start.30 = (f32[2,64,1024]{2,1,0:T(8,128)S(1)}, f32[2,64,1024]{2,1,0:T(8,128)S(1)}, u32[]{:S(2)}, u32[]{:S(2)}) collective-permute-start(f32[2,64,1024]{2,1,0:T(8,128)S(1)} %get-tuple-element.135), channel_id=1, source_target_pairs={{0,2},{1,3},{6,4},{7,5},{8,10},{9,11},{14,12},{15,13},{16,18},{17,... | collective-permute-start | bytes 1572872 | tf_op jit(solution)/shard_map/ppermute | solution.py:470
  123.4 5.7 %collective-permute-start.20 = (f32[2,16,1024]{2,1,0:T(8,128)S(1)}, f32[2,16,1024]{2,1,0:T(8,128)S(1)}, u32[]{:S(2)}, u32[]{:S(2)}) collective-permute-start(f32[2,16,1024]{2,1,0:T(8,128)S(1)} %get-tuple-element.117), channel_id=1, source_target_pairs={{0,8},{8,0},{16,24},{24,16},{1,9},{9,1},{17,25},{25,17},{2,10},{10... | collective-permute-start | bytes 393224 | tf_op jit(solution)/shard_map/ppermute | solution.py:90
  125.5 6.6 %collective-permute-start.21 = (f32[2,16,1024]{2,1,0:T(8,128)S(1)}, f32[2,16,1024]{2,1,0:T(8,128)S(1)}, u32[]{:S(2)}, u32[]{:S(2)}) collective-permute-start(f32[2,16,1024]{2,1,0:T(8,128)S(1)} %get-tuple-element.118), channel_id=1, source_target_pairs={{0,16},{8,24},{16,0},{24,8},{1,17},{9,25},{17,1},{25,9},{2,18},{10... | collective-permute-start | bytes 393224 | tf_op jit(solution)/shard_map/ppermute | solution.py:90
  129.1 5.9 %collective-permute-start.22 = (f32[2,16,1024]{2,1,0:T(8,128)S(1)}, f32[2,16,1024]{2,1,0:T(8,128)S(1)}, u32[]{:S(2)}, u32[]{:S(2)}) collective-permute-start(f32[2,16,1024]{2,1,0:T(8,128)S(1)} %get-tuple-element.119), channel_id=1, source_target_pairs={{0,24},{8,16},{16,8},{24,0},{1,25},{9,17},{17,9},{25,1},{2,26},{10... | collective-permute-start | bytes 393224 | tf_op jit(solution)/shard_map/ppermute | solution.py:90
  138.0 3.6 %collective-permute-start.31 = (f32[4,64,1024]{2,1,0:T(8,128)S(1)}, f32[4,64,1024]{2,1,0:T(8,128)S(1)}, u32[]{:S(2)}, u32[]{:S(2)}) collective-permute-start(f32[4,64,1024]{2,1,0:T(8,128)S(1)} %get-tuple-element.139.refs_5_), channel_id=1, source_target_pairs={{0,1},{1,0},{2,3},{3,2},{4,5},{5,4},{6,7},{7,6},{8,9},{9,8},{10,11... | collective-permute-start | bytes 3145736 | tf_op jit(solution)/shard_map/ppermute | solution.py:90
  138.0 8.5 %collective-permute-start.26 = (f32[2,16,1024]{2,1,0:T(8,128)S(1)}, f32[2,16,1024]{2,1,0:T(8,128)S(1)}, u32[]{:S(2)}, u32[]{:S(2)}) collective-permute-start(f32[2,16,1024]{2,1,0:T(8,128)S(1)} %get-tuple-element.130), channel_id=1, source_target_pairs={{0,8},{8,0},{16,24},{24,16},{1,9},{9,1},{17,25},{25,17},{2,10},{10... | collective-permute-start | bytes 393224 | tf_op jit(solution)/shard_map/ppermute | solution.py:90
  139.7 8.3 %collective-permute-start.27 = (f32[2,16,1024]{2,1,0:T(8,128)S(1)}, f32[2,16,1024]{2,1,0:T(8,128)S(1)}, u32[]{:S(2)}, u32[]{:S(2)}) collective-permute-start(f32[2,16,1024]{2,1,0:T(8,128)S(1)} %get-tuple-element.131), channel_id=1, source_target_pairs={{0,16},{8,24},{16,0},{24,8},{1,17},{9,25},{17,1},{25,9},{2,18},{10... | collective-permute-start | bytes 393224 | tf_op jit(solution)/shard_map/ppermute | solution.py:90
  141.5 12.4 %copy-start.3 = (f32[16,2,1,16384]{3,2,1,0:T(1,128)S(1)}, f32[16,2,1,16384]{3,2,1,0:T(1,128)}, u32[]{:S(2)}) copy-start(f32[16,2,1,16384]{3,2,1,0:T(1,128)} %param.13) | copy-start | bytes 6291460
  141.5 7.3 %collective-permute-start.28 = (f32[2,16,1024]{2,1,0:T(8,128)S(1)}, f32[2,16,1024]{2,1,0:T(8,128)S(1)}, u32[]{:S(2)}, u32[]{:S(2)}) collective-permute-start(f32[2,16,1024]{2,1,0:T(8,128)S(1)} %get-tuple-element.132), channel_id=1, source_target_pairs={{0,24},{8,16},{16,8},{24,0},{1,25},{9,17},{17,9},{25,1},{2,26},{10... | collective-permute-start | bytes 393224 | tf_op jit(solution)/shard_map/ppermute | solution.py:90
  143.1 7.2 %collective-permute-start.32 = (f32[2,16,1024]{2,1,0:T(8,128)S(1)}, f32[2,16,1024]{2,1,0:T(8,128)S(1)}, u32[]{:S(2)}, u32[]{:S(2)}) collective-permute-start(f32[2,16,1024]{2,1,0:T(8,128)S(1)} %get-tuple-element.141), channel_id=1, source_target_pairs={{0,8},{8,0},{16,24},{24,16},{1,9},{9,1},{17,25},{25,17},{2,10},{10... | collective-permute-start | bytes 393224 | tf_op jit(solution)/shard_map/ppermute | solution.py:90
  144.7 8.3 %collective-permute-start.33 = (f32[2,16,1024]{2,1,0:T(8,128)S(1)}, f32[2,16,1024]{2,1,0:T(8,128)S(1)}, u32[]{:S(2)}, u32[]{:S(2)}) collective-permute-start(f32[2,16,1024]{2,1,0:T(8,128)S(1)} %get-tuple-element.142), channel_id=1, source_target_pairs={{0,16},{8,24},{16,0},{24,8},{1,17},{9,25},{17,1},{25,9},{2,18},{10... | collective-permute-start | bytes 393224 | tf_op jit(solution)/shard_map/ppermute | solution.py:90
  146.5 7.4 %collective-permute-start.34 = (f32[2,16,1024]{2,1,0:T(8,128)S(1)}, f32[2,16,1024]{2,1,0:T(8,128)S(1)}, u32[]{:S(2)}, u32[]{:S(2)}) collective-permute-start(f32[2,16,1024]{2,1,0:T(8,128)S(1)} %get-tuple-element.143), channel_id=1, source_target_pairs={{0,24},{8,16},{16,8},{24,0},{1,25},{9,17},{17,9},{25,1},{2,26},{10... | collective-permute-start | bytes 393224 | tf_op jit(solution)/shard_map/ppermute | solution.py:90

commit v4 on v3

--- a/solution.py
+++ b/solution.py
@@ -11,21 +11,8 @@
 
 LANES = 128
 CHUNK_SHARES = (8, 8, 8, 8)
-FLUX_GROUPS = ((0,), (1,), (2,), (3,))
-WEIGHTS_TOGETHER = False
-RESULTS_TOGETHER = False
-REST_TOGETHER = False
-RELEASE = 2
-PAIR_AFTER = True
-PAIR_GATE = 1
-FLUX_GATE = 2
-SEEN_GATE = 2
-SEEN_GROUPS = (0, 1)
-TAIL_PAIR = 0
-PACK_GATE = 1
-WEIGHT_GATE = 3
-REST_FIRST = True
-HEAD_LIMIT = True
+FLUX_GATE = 3
+SEEN = (0, 1)
 VMEM = pl.BlockSpec(memory_space=pltpu.VMEM)
 SMEM = pl.BlockSpec(memory_space=pltpu.SMEM)
 HBM = pl.BlockSpec(memory_space=pltpu.HBM)
@@ -99,16 +86,13 @@
                 out[:, lane : lane + LANES] = turned[r]
 
 
-def pack_kernel(parts, spans, together, place, x, *refs):
+def pack_kernel(parts, spans, place, x, *refs):
     outs, (staged, sems) = refs[:-2], refs[-2:]
-    if together:
-        outs = [out.at[i] for i in range(parts) for out in outs]
     share_rows = x.shape[2] // parts
     low = spans[0][0] // SUBLANES * SUBLANES
     copies = []
     for i in range(parts):
-        part = i if together else place[0] ^ i
-        first = pl.multiple_of(part * share_rows + low, SUBLANES)
+        first = pl.multiple_of((place[0] ^ i) * share_rows + low, SUBLANES)
         copies.append(
             pltpu.make_async_copy(x.at[:, :, pl.ds(first, staged.shape[3]), :], staged.at[i], sems.at[i])
         )
@@ -125,9 +109,9 @@
                 )
 
 
-def head_kernel(parts, spans, together, place, x, shifts, offsets, *refs):
+def plan_pack_kernel(parts, spans, place, x, shifts, offsets, *refs):
     outs = refs[: parts * len(spans)]
-    pack_kernel(parts, spans, together, place, x, *refs)
+    pack_kernel(parts, spans, place, x, *refs)
     rows = shifts.shape[0]
     row = lax.broadcasted_iota(jnp.int32, (rows, LANES), 0)
     lane = lax.broadcasted_iota(jnp.int32, (rows, LANES), 1)
@@ -146,27 +130,25 @@
     pass
 
 
-def gather_kernel(parts, together, place, *refs):
-    if together:
-        pieces, outs = [refs[0].at[q] for q in range(parts)], refs[1:]
-    else:
-        pieces, outs = refs[:parts], refs[parts:]
+def gather_kernel(parts, place, *refs):
+    pieces, outs = refs[:parts], refs[parts:]
     rows = pieces[0].shape[1]
     for i in range(parts):
-        first = i * rows if together else pl.multiple_of((place[0] ^ i) * rows, rows)
+        first = pl.multiple_of((place[0] ^ i) * rows, rows)
         lane = 0
         for out in outs:
             out[:, pl.ds(first, rows), :] = pieces[i][:, :, lane : lane + out.shape[2]]
             lane += out.shape[2]
 
 
-def head_gather_kernel(parts, place, *refs):
-    pieces, (own, plan) = refs[:parts], refs[parts:]
-    gather_kernel(parts, False, place, *pieces, own)
+def plan_gather_kernel(parts, place, *refs):
+    pieces, (*outs, plan) = refs[:parts], refs[parts:]
+    gather_kernel(parts, place, *pieces, *outs)
     rows = pieces[0].shape[1]
+    behind = sum(out.shape[2] for out in outs)
     for i in range(parts):
         first = pl.multiple_of((place[0] ^ i) * rows, rows)
-        numbers = pieces[i][0, :, own.shape[2] :].astype(jnp.int32)
+        numbers = pieces[i][0, :, behind:].astype(jnp.int32)
         for n in range(3):
             plan[n, pl.ds(first, rows), :] = jnp.broadcast_to(numbers[:, n : n + 1], (rows, LANES))
 
@@ -257,10 +239,8 @@
         pair[2:4] = slot_b[:, :, : pair.shape[2]]
 
 
-def flux_kernel(parts, together, chunks, row0, place, table, plan, iron, weights, *refs):
-    pairs, fars = refs[:chunks], refs[chunks : 2 * chunks]
-    flux, result = refs[-2:]
-    outs = [refs[2 * chunks].at[q] for q in range(parts)] if together else refs[2 * chunks : -2]
+def flux_kernel(parts, row0, place, table, plan, iron, weights, pair, far, *refs):
+    *outs, flux, result = refs
     total = outs[0].shape[2]
     tm, me = place[0], place[1]
     source = [((me + plan[1 + m] - plan[0]) ^ me) & 3 for m in range(2)]
@@ -268,49 +248,44 @@
     is_two = [s == 2 for s in source]
     is_one = [s == 1 for s in source]
     quarter = tm * (iron.shape[0] // parts) + row0
-    lane = 0
-    for k in range(chunks):
-        for inner in range(0, pairs[k].shape[2], LANES):
-            here = slice(inner, inner + LANES)
-            there = slice(row0 * LANES + lane, row0 * LANES + lane + LANES)
-            field = []
-            for comp in range(2):
-                blocks = [ref[c, :, here] for ref in (pairs[k], fars[k]) for c in (comp, 2 + comp)]
-                terms = [
-                    weights[m, :, there]
-                    * jnp.where(
-                        is_near[m],
-                        blocks[0],
-                        jnp.where(is_two[m], blocks[1], jnp.where(is_one[m], blocks[2], blocks[3])),
-                    )
-                    for m in range(2)
-                ]
-                field.append(terms[0] + terms[1])
-            square = field[0] * field[0] + field[1] * field[1]
-            gain = iron[pl.ds(quarter + lane // LANES, 1), :] * (1.0 + square / (1.0 + square))
-            for comp in range(2):
-                flux[:, comp * total + lane : comp * total + lane + LANES] = gain * field[comp]
-            lane += LANES
+    for lane in range(0, total, LANES):
+        here = slice(lane, lane + LANES)
+        there = slice(row0 * LANES + lane, row0 * LANES + lane + LANES)
+        field = []
+        for comp in range(2):
+            blocks = [ref[c, :, here] for ref in (pair, far) for c in (comp, 2 + comp)]
+            terms = [
+                weights[m, :, there]
+                * jnp.where(
+                    is_near[m],
+                    blocks[0],
+                    jnp.where(is_two[m], blocks[1], jnp.where(is_one[m], blocks[2], blocks[3])),
+                )
+                for m in range(2)
+            ]
+            field.append(terms[0] + terms[1])
+        square = field[0] * field[0] + field[1] * field[1]
+        gain = iron[pl.ds(quarter + lane // LANES, 1), :] * (1.0 + square / (1.0 + square))
+        for comp in range(2):
+            flux[:, comp * total + lane : comp * total + lane + LANES] = gain * field[comp]
     result[...] = table_dot(table[...], flux[...])
     rows = result.shape[0] // parts
     for i in range(parts):
-        first = i * rows if together else pl.multiple_of((tm ^ i) * rows, rows)
+        first = pl.multiple_of((tm ^ i) * rows, rows)
         for comp in range(2):
             outs[i][comp] = result[pl.ds(first, rows), comp * total : (comp + 1) * total]
 
 
-def finish_kernel(parts, together, groups, place, source, *refs):
+def finish_kernel(parts, chunks, place, source, *refs):
     pieces, (out, made, sems) = refs[:-3], refs[-3:]
-    if together:
-        pieces = [piece.at[q] for piece in pieces for q in range(parts)]
     share_rows = source.shape[2] // parts
     copies = []
     for i in range(parts):
-        first = pl.multiple_of((i if together else place[0] ^ i) * share_rows, SUBLANES)
+        first = pl.multiple_of((place[0] ^ i) * share_rows, SUBLANES)
         for comp in range(2):
             rows = [
                 pieces[g * parts + i][comp, :, lane : lane + LANES]
-                for g in range(groups)
+                for g in range(chunks)
                 for lane in range(0, pieces[g * parts].shape[2], LANES)
             ]
             for row in range(0, share_rows, SUBLANES):
@@ -343,13 +318,13 @@
     def in_rows(x):
         return x.reshape(x.shape[0], comps, nodes // LANES, LANES)
 
-    def pack(x, spans, after=(), plan=(), together=False):
+    def pack(x, spans, after=(), plan=(), limit=LIMIT):
         low = spans[0][0] // SUBLANES * SUBLANES
         high = -(-(spans[-1][0] + spans[-1][1]) // SUBLANES) * SUBLANES
         shape = (2, x.shape[0], (spans[0][1] + bool(plan)) * LANES)
         *outs, token = call(
-            functools.partial(head_kernel if plan else pack_kernel, parts, spans, together),
-            [f32(parts, *shape)] if together else [f32(*shape)] * parts,
+            functools.partial(plan_pack_kernel if plan else pack_kernel, parts, spans),
+            [f32(*shape)] * parts,
             (place, in_rows(x), *plan),
             after=after,
             scratch=(
@@ -358,42 +333,41 @@
             ),
             smem=(0, 2, 3) if plan else (0,),
             hbm=(1,),
-            limit=FULL if plan else LIMIT,
+            limit=limit,
         )
         return outs, token
 
     def swap(pieces):
-        if len(pieces) == 1:
-            return [lax.all_to_all(pieces[0], "tm", split_axis=0, concat_axis=0, tiled=True)]
         return [pieces[0]] + [xor_permute(pieces[i], "tm", i) for i in range(1, parts)]
 
     def gather(pieces, lanes, rows, after=()):
         *outs, token = call(
-            functools.partial(gather_kernel, parts, len(pieces) == 1),
+            functools.partial(gather_kernel, parts),
             [f32(2, rows, w) for w in lanes],
             (place, *pieces),
             after=after,
         )
         return outs, token
 
-    head, token = pack(rotor_coeffs, [(0, heights[0])], plan=(block_shifts, stencil_offsets.T))
-    rest_span = [(heights[0], share_rows - heights[0])]
-    if REST_FIRST:
-        rest, token = pack(rotor_coeffs, rest_span, after=(token,), together=REST_TOGETHER)
-    own_first, plan, token = call(
-        functools.partial(head_gather_kernel, parts),
-        [f32(2, coeffs, widths[0]), jax.ShapeDtypeStruct((3, samples, LANES), jnp.int32)],
-        (place, *swap(head)),
-        after=(token,) if REST_FIRST else (),
+    head, token = pack(rotor_coeffs, [(0, heights[0])], limit=FULL)
+    rest, token = pack(
+        rotor_coeffs,
+        [(heights[0], share_rows - heights[0])],
+        after=(token,),
+        plan=(block_shifts, stencil_offsets.T),
     )
-    if not REST_FIRST:
-        rest, token = pack(rotor_coeffs, rest_span, after=(token,), together=REST_TOGETHER)
-    own_rest, token = gather(swap(rest), widths[1:], coeffs, (token,))
+    (own_first,), token = gather(swap(head), widths[:1], coeffs, (token,))
+    *own_rest, plan, token = call(
+        functools.partial(plan_gather_kernel, parts),
+        [f32(2, coeffs, w) for w in widths[1:]] + [jax.ShapeDtypeStruct((3, samples, LANES), jnp.int32)],
+        (place, *swap(rest)),
+        after=(token,),
+    )
     own = [own_first] + own_rest
-    weights, token = pack(mortar_weights, [(0, share_rows)], after=(token,), together=WEIGHTS_TOGETHER)
-    gates[PACK_GATE] = [token]
+    weights, token = pack(mortar_weights, [(0, share_rows)], after=(token,))
+    gates[1] = [token]
     (weights,), token = gather(swap(weights), [share_rows * LANES], samples)
-    gates.setdefault(WEIGHT_GATE, []).append(token)
+    gates[3] = [token]
 
     half, fourth = count // 2, count // 4
     outer = [d for d in range(count) if is_outer(d, count)]
@@ -421,18 +395,18 @@
 
     iron = reluctivity.reshape(nodes // LANES, LANES)
 
-    def flux(group, pairs):
-        total = sum(widths[k] for k in group)
+    def flux(k, pair, far):
+        total = widths[k]
         *made, token = call(
-            functools.partial(flux_kernel, parts, RESULTS_TOGETHER, len(group), sum(heights[: group[0]])),
-            [f32(parts, 2, coeff_rows, total)] if RESULTS_TOGETHER else [f32(2, coeff_rows, total)] * parts,
-            (place, backward, plan, iron, weights, *[pairs[k][0] for k in group], *[pairs[k][1] for k in group]),
+            functools.partial(flux_kernel, parts, sum(heights[:k])),
+            [f32(2, coeff_rows, total)] * parts,
+            (place, backward, plan, iron, weights, pair, far),
             scratch=(pltpu.VMEM((samples, 2 * total), jnp.float32), pltpu.VMEM((coeffs, 2 * total), jnp.float32)),
             flops=4 * samples * 3 * coeffs * total,
         )
         return swap(made), token
 
-    slots_a, slots_b, keeps, pairs, pieces = [], [], [], [], []
+    slots_a, slots_b, keeps, pieces = [], [], [], []
     send_a = send_b = own[0]
     for k in range(chunks):
         slots_a.append(lax.ppermute(send_a, "azim", coeff_a + (sample_a if k else [])))
@@ -455,24 +429,20 @@
         )
         keeps.append(kept)
         if k:
-            *pair, token = neighbours(keeps[k - 1], slots_a[k], slots_b[k], (token,) if PAIR_AFTER else ())
-            gates.setdefault(k + PAIR_GATE, []).append(token)
-            pairs.append(pair)
-            for group in FLUX_GROUPS:
-                if group[-1] == k - 1:
-                    made, token = flux(group, pairs)
-                    pieces += made
-                    gates.setdefault(min(k + FLUX_GATE, chunks), []).append(token)
-                    if group[-1] in SEEN_GROUPS:
-                        (token,) = call(functools.partial(seen_kernel), [], (place, *made))
-                        gates.setdefault(min(k + SEEN_GATE, chunks), []).append(token)
+            *pair, token = neighbours(keeps[k - 1], slots_a[k], slots_b[k], (token,))
+            gates.setdefault(k + 1, []).append(token)
+            made, token = flux(k - 1, *pair)
+            pieces += made
+            gate = gates.setdefault(min(k - 1 + FLUX_GATE, chunks), [])
+            gate.append(token)
+            if k - 1 in SEEN:
+                gate += call(functools.partial(seen_kernel), [], (place, *made))
     slot_a = lax.ppermute(send_a, "azim", sample_a)
     slot_b = lax.ppermute(send_b, "azim", sample_b)
     *pair, _ = neighbours(keeps[-1], slot_a, slot_b, gates.get(chunks, ()))
-    pairs.append(pair)
-    pieces += flux(FLUX_GROUPS[-1], pairs)[0]
+    pieces += flux(chunks - 1, *pair)[0]
     out, _ = call(
-        functools.partial(finish_kernel, parts, RESULTS_TOGETHER, len(FLUX_GROUPS)),
+        functools.partial(finish_kernel, parts, chunks),
         [f32(coeff_rows, comps, nodes // LANES, LANES)],
         (place, in_rows(source), *pieces),
         scratch=(

time: 157 us -> 157 us (level)
  waiting for transfers between devices: 75 us -> 73.2 us
  starting transfers between devices: 50.4 us -> 52.1 us
    ppermute x25, starting transfers between devices: 32.6 us -> 34.2 us  [xor_permute(): return lax.ppermute(value, axis, [(i, i ^ step) for i in range(count)])]
  transfers between devices with their start and end apart: 35 -> 35, of which waited for: 19 -> 18; matrix products, arithmetic and copies ran while one was open for 0% -> 0% of each run, Pallas kernels for 13% -> 13%
where the time goes in v4:
time: 157 us; the launch traced here: 156 us
  waiting for transfers between devices  73.2 us (47%)
  starting transfers between devices  52.1 us (33%)
  Pallas kernels  27.8 us (18%)
  local copies, waits for them, and re-layouts  2.3 us (1%)
    ppermute x25, waiting for transfers between devices, xor_permute(): return lax.ppermute(value, axis, [(i, i ^ step) for i in range(count)])  45.1 us
    ppermute x25, starting transfers between devices, xor_permute(): return lax.ppermute(value, axis, [(i, i ^ step) for i in range(count)])  34.2 us
    pallas_call x25, Pallas kernels, call(): pl.pallas_call(run, name=kernel.func.__name__, out_shape=[jax.ShapeDtypeS...  27.8 us
    ppermute x4, waiting for transfers between devices, body(): lax.ppermute(send_a, 'azim', coeff_a + (sample_a if k else []))  14.9 us
    ppermute x4, waiting for transfers between devices, body(): lax.ppermute(send_b, 'azim', coeff_b + (sample_b if k else []))  13.2 us
    ppermute x4, starting transfers between devices, body(): lax.ppermute(send_a, 'azim', coeff_a + (sample_a if k else []))  9.08 us
    ppermute x1, starting transfers between devices, body(): slot_b = lax.ppermute(send_b, 'azim', sample_b)  4.61 us
  transfers between devices with their start and end apart: 35, of which 18 were waited for; matrix products, arithmetic and copies ran while one was open for 0% of the time, Pallas kernels for 13%

profile of v4, /device:TPU:0, one launch (start us, length us, event | category | flops | bytes accessed | tf_op | source)
XLA Modules:
  0.0 156.3 jit_solution(10304936373265504752)
XLA Ops:
  0.6 2.7 %pack_kernel.2 = (f32[2,16,1024]{2,1,0:T(8,128)}, f32[2,16,1024]{2,1,0:T(8,128)}, f32[2,16,1024]{2,1,0:T(8,128)}, f32[2,16,1024]{2,1,0:T(8,128)}, f32[8,128]{1,0:T(8,128)}) custom-call(s32[2]{0:T(128)} %pad_add_fusion.refs_0_, f32[16,2,128,128]{3,2,1,0:T(8,128)} %bitcast.8), custom_call_target="tpu_custom_call" | custom-call | bytes 2621448 | tf_op jit(solution)/shard_map/pack_kernel/pallas_call | solution.py:63
  3.3 3.0 %collective-permute-start.3 = (f32[2,16,1024]{2,1,0:T(8,128)}, f32[2,16,1024]{2,1,0:T(8,128)S(1)}, u32[]{:S(2)}, u32[]{:S(2)}) collective-permute-start(f32[2,16,1024]{2,1,0:T(8,128)} %get-tuple-element.81), channel_id=1, source_target_pairs={{0,8},{8,0},{16,24},{24,16},{1,9},{9,1},{17,25},{25,17},{2,10},{10... | collective-permute-start | bytes 393224 | tf_op jit(solution)/shard_map/ppermute | solution.py:77
  6.3 1.5 collective-permute-start.4
  7.8 1.6 %copy-done = f32[16,2,1,16384]{3,2,1,0:T(1,128)S(1)} copy-done((f32[16,2,1,16384]{3,2,1,0:T(1,128)S(1)}, f32[16,2,1,16384]{3,2,1,0:T(1,128)}, u32[]{:S(2)}) %copy-start) | copy-done | bytes 2097176
  11.2 3.1 %collective-permute-done.4.refs_3_ = f32[2,16,1024]{2,1,0:T(8,128)S(1)} collective-permute-done((f32[2,16,1024]{2,1,0:T(8,128)}, f32[2,16,1024]{2,1,0:T(8,128)S(1)}, u32[]{:S(2)}, u32[]{:S(2)}) %collective-permute-start.4) | collective-permute-done | bytes 131104 | tf_op jit(solution)/shard_map/ppermute | solution.py:77
  14.8 4.5 %collective-permute-start.10 = (f32[2,64,1024]{2,1,0:T(8,128)S(1)}, f32[2,64,1024]{2,1,0:T(8,128)S(1)}, u32[]{:S(2)}, u32[]{:S(2)}) collective-permute-start(f32[2,64,1024]{2,1,0:T(8,128)S(1)} %get-tuple-element.93.refs_3_), channel_id=1, source_target_pairs={{0,4},{1,5},{6,2},{7,3},{8,12},{9,13},{14,10},{15,11},{16,20},{17,... | collective-permute-start | bytes 1572872 | tf_op jit(solution)/shard_map/ppermute | solution.py:412
  19.4 1.3 collective-permute-start.9
  20.7 1.3 collective-permute-start
  22.8 1.4 collective-permute-start.2
  24.2 8.9 %collective-permute-done.refs_2_ = f32[2,16,3200]{2,1,0:T(8,128)S(1)} collective-permute-done((f32[2,16,3200]{2,1,0:T(8,128)S(1)}, f32[2,16,3200]{2,1,0:T(8,128)S(1)}, u32[]{:S(2)}, u32[]{:S(2)}) %collective-permute-start) | collective-permute-done | bytes 409632 | tf_op jit(solution)/shard_map/ppermute | solution.py:77
  33.1 7.4 %collective-permute-done.1.refs_3_ = f32[2,16,3200]{2,1,0:T(8,128)S(1)} collective-permute-done((f32[2,16,3200]{2,1,0:T(8,128)S(1)}, f32[2,16,3200]{2,1,0:T(8,128)S(1)}, u32[]{:S(2)}, u32[]{:S(2)}) %collective-permute-start.1) | collective-permute-done | bytes 409632 | tf_op jit(solution)/shard_map/ppermute | solution.py:77
  41.2 1.2 first_kernel.4
  42.4 3.6 %collective-permute-start.11 = (f32[2,64,1024]{2,1,0:T(8,128)S(1)}, f32[2,64,1024]{2,1,0:T(8,128)S(1)}, u32[]{:S(2)}, u32[]{:S(2)}) collective-permute-start(f32[2,64,1024]{2,1,0:T(8,128)S(1)} %get-tuple-element.97), channel_id=1, source_target_pairs={{0,4},{1,5},{6,2},{7,3},{2,0},{3,1},{4,6},{5,7},{8,12},{9,13},{14,... | collective-permute-start | bytes 1572872 | tf_op jit(solution)/shard_map/ppermute | solution.py:412
  46.1 1.6 %second_kernel.4 = (f32[2,64,1024]{2,1,0:T(8,128)S(1)}, f32[2,64,1024]{2,1,0:T(8,128)S(1)}, f32[8,128]{1,0:T(8,128)}) custom-call(s32[2]{0:T(128)S(1)} %copy-done.6, bf16[64,192]{1,0:T(8,128)(2,1)S(1)} %copy-done.1, s32[3,64,128]{2,1,0:T(8,128)S(1)} %get-tuple-element.86.refs_2_, f32[2,64,1024]{2,1,0:T(8,128)S(1)} %get-tuple-element.93.refs_3_, ...), custom_call_target="tpu_custom_call" | custom-call | flops 100663296 | bytes 3293192 | tf_op jit(solution)/shard_map/second_kernel/pallas_call | solution.py:63
  47.6 1.1 pack_kernel.3
  48.8 13.9 %collective-permute-done.11.refs_4_.refs_2_ = f32[2,64,1024]{2,1,0:T(8,128)S(1)} collective-permute-done((f32[2,64,1024]{2,1,0:T(8,128)S(1)}, f32[2,64,1024]{2,1,0:T(8,128)S(1)}, u32[]{:S(2)}, u32[]{:S(2)}) %collective-permute-start.11) | collective-permute-done | bytes 524320 | tf_op jit(solution)/shard_map/ppermute | solution.py:412
  62.7 1.2 first_kernel.5
  64.4 7.0 %collective-permute-done.12.refs_4_.refs_3_ = f32[2,64,1024]{2,1,0:T(8,128)S(1)} collective-permute-done((f32[2,64,1024]{2,1,0:T(8,128)S(1)}, f32[2,64,1024]{2,1,0:T(8,128)S(1)}, u32[]{:S(2)}, u32[]{:S(2)}) %collective-permute-start.12) | collective-permute-done | bytes 524320 | tf_op jit(solution)/shard_map/ppermute | solution.py:413
  74.0 1.4 collective-permute-start.7
  76.3 5.5 %collective-permute-start.8 = (f32[2,16,4096]{2,1,0:T(8,128)S(1)}, f32[2,16,4096]{2,1,0:T(8,128)S(1)}, u32[]{:S(2)}, u32[]{:S(2)}) collective-permute-start(f32[2,16,4096]{2,1,0:T(8,128)S(1)} %get-tuple-element.91), channel_id=1, source_target_pairs={{0,24},{8,16},{16,8},{24,0},{1,25},{9,17},{17,9},{25,1},{2,26},{10... | collective-permute-start | bytes 1572872 | tf_op jit(solution)/shard_map/ppermute | solution.py:77
  81.8 1.2 first_kernel.6
  83.0 5.3 %collective-permute-done.18.refs_4_.refs_3_ = f32[2,64,1024]{2,1,0:T(8,128)S(1)} collective-permute-done((f32[2,64,1024]{2,1,0:T(8,128)S(1)}, f32[2,64,1024]{2,1,0:T(8,128)S(1)}, u32[]{:S(2)}, u32[]{:S(2)}) %collective-permute-start.18) | collective-permute-done | bytes 524320 | tf_op jit(solution)/shard_map/ppermute | solution.py:413
  89.8 1.2 collective-permute-start.24
  91.0 7.9 %collective-permute-done.7.refs_3_ = f32[2,16,4096]{2,1,0:T(8,128)S(1)} collective-permute-done((f32[2,16,4096]{2,1,0:T(8,128)S(1)}, f32[2,16,4096]{2,1,0:T(8,128)S(1)}, u32[]{:S(2)}, u32[]{:S(2)}) %collective-permute-start.7) | collective-permute-done | bytes 524320 | tf_op jit(solution)/shard_map/ppermute | solution.py:77
  99.7 1.1 flux_kernel.4
  100.8 1.5 collective-permute-start.14
  103.8 2.1 %collective-permute-done.14.refs_2_.refs_3_ = f32[2,16,1024]{2,1,0:T(8,128)S(1)} collective-permute-done((f32[2,16,1024]{2,1,0:T(8,128)S(1)}, f32[2,16,1024]{2,1,0:T(8,128)S(1)}, u32[]{:S(2)}, u32[]{:S(2)}) %collective-permute-start.14) | collective-permute-done | bytes 131104 | tf_op jit(solution)/shard_map/ppermute | solution.py:77
  105.8 1.6 %collective-permute-start.16 = (f32[2,16,1024]{2,1,0:T(8,128)S(1)}, f32[2,16,1024]{2,1,0:T(8,128)S(1)}, u32[]{:S(2)}, u32[]{:S(2)}) collective-permute-start(f32[2,16,1024]{2,1,0:T(8,128)S(1)} %get-tuple-element.107), channel_id=1, source_target_pairs={{0,24},{8,16},{16,8},{24,0},{1,25},{9,17},{17,9},{25,1},{2,26},{10... | collective-permute-start | bytes 393224 | tf_op jit(solution)/shard_map/ppermute | solution.py:77
  107.4 3.0 %collective-permute-done.15.refs_3_.refs_4_ = f32[2,16,1024]{2,1,0:T(8,128)S(1)} collective-permute-done((f32[2,16,1024]{2,1,0:T(8,128)S(1)}, f32[2,16,1024]{2,1,0:T(8,128)S(1)}, u32[]{:S(2)}, u32[]{:S(2)}) %collective-permute-start.15) | collective-permute-done | bytes 131104 | tf_op jit(solution)/shard_map/ppermute | solution.py:77
  110.4 1.4 collective-permute-done.16.refs_4_.refs_5_
  112.3 1.2 first_kernel.7
  116.1 1.3 collective-permute-start.29
  117.4 4.6 %collective-permute-start.30 = (f32[2,64,1024]{2,1,0:T(8,128)S(1)}, f32[2,64,1024]{2,1,0:T(8,128)S(1)}, u32[]{:S(2)}, u32[]{:S(2)}) collective-permute-start(f32[2,64,1024]{2,1,0:T(8,128)S(1)} %get-tuple-element.135), channel_id=1, source_target_pairs={{0,2},{1,3},{6,4},{7,5},{8,10},{9,11},{14,12},{15,13},{16,18},{17,... | collective-permute-start | bytes 1572872 | tf_op jit(solution)/shard_map/ppermute | solution.py:441
  123.2 2.2 %collective-permute-start.20 = (f32[2,16,1024]{2,1,0:T(8,128)S(1)}, f32[2,16,1024]{2,1,0:T(8,128)S(1)}, u32[]{:S(2)}, u32[]{:S(2)}) collective-permute-start(f32[2,16,1024]{2,1,0:T(8,128)S(1)} %get-tuple-element.117), channel_id=1, source_target_pairs={{0,8},{8,0},{16,24},{24,16},{1,9},{9,1},{17,25},{25,17},{2,10},{10... | collective-permute-start | bytes 393224 | tf_op jit(solution)/shard_map/ppermute | solution.py:77
  125.5 1.8 %collective-permute-start.21 = (f32[2,16,1024]{2,1,0:T(8,128)S(1)}, f32[2,16,1024]{2,1,0:T(8,128)S(1)}, u32[]{:S(2)}, u32[]{:S(2)}) collective-permute-start(f32[2,16,1024]{2,1,0:T(8,128)S(1)} %get-tuple-element.118), channel_id=1, source_target_pairs={{0,16},{8,24},{16,0},{24,8},{1,17},{9,25},{17,1},{25,9},{2,18},{10... | collective-permute-start | bytes 393224 | tf_op jit(solution)/shard_map/ppermute | solution.py:77
  127.2 1.8 %collective-permute-done.20.refs_2_.refs_7_ = f32[2,16,1024]{2,1,0:T(8,128)S(1)} collective-permute-done((f32[2,16,1024]{2,1,0:T(8,128)S(1)}, f32[2,16,1024]{2,1,0:T(8,128)S(1)}, u32[]{:S(2)}, u32[]{:S(2)}) %collective-permute-start.20) | collective-permute-done | bytes 131104 | tf_op jit(solution)/shard_map/ppermute | solution.py:77
  129.0 3.0 %collective-permute-start.22 = (f32[2,16,1024]{2,1,0:T(8,128)S(1)}, f32[2,16,1024]{2,1,0:T(8,128)S(1)}, u32[]{:S(2)}, u32[]{:S(2)}) collective-permute-start(f32[2,16,1024]{2,1,0:T(8,128)S(1)} %get-tuple-element.119), channel_id=1, source_target_pairs={{0,24},{8,16},{16,8},{24,0},{1,25},{9,17},{17,9},{25,1},{2,26},{10... | collective-permute-start | bytes 393224 | tf_op jit(solution)/shard_map/ppermute | solution.py:77
  132.0 2.9 %collective-permute-done.22.refs_4_.refs_9_ = f32[2,16,1024]{2,1,0:T(8,128)S(1)} collective-permute-done((f32[2,16,1024]{2,1,0:T(8,128)S(1)}, f32[2,16,1024]{2,1,0:T(8,128)S(1)}, u32[]{:S(2)}, u32[]{:S(2)}) %collective-permute-start.22) | collective-permute-done | bytes 131104 | tf_op jit(solution)/shard_map/ppermute | solution.py:77
  135.5 1.1 flux_kernel.6
  136.7 1.2 pair_kernel.7
  137.9 1.7 %collective-permute-start.26 = (f32[2,16,1024]{2,1,0:T(8,128)S(1)}, f32[2,16,1024]{2,1,0:T(8,128)S(1)}, u32[]{:S(2)}, u32[]{:S(2)}) collective-permute-start(f32[2,16,1024]{2,1,0:T(8,128)S(1)} %get-tuple-element.130), channel_id=1, source_target_pairs={{0,8},{8,0},{16,24},{24,16},{1,9},{9,1},{17,25},{25,17},{2,10},{10... | collective-permute-start | bytes 393224 | tf_op jit(solution)/shard_map/ppermute | solution.py:77
  139.6 1.8 %collective-permute-start.27 = (f32[2,16,1024]{2,1,0:T(8,128)S(1)}, f32[2,16,1024]{2,1,0:T(8,128)S(1)}, u32[]{:S(2)}, u32[]{:S(2)}) collective-permute-start(f32[2,16,1024]{2,1,0:T(8,128)S(1)} %get-tuple-element.131), channel_id=1, source_target_pairs={{0,16},{8,24},{16,0},{24,8},{1,17},{9,25},{17,1},{25,9},{2,18},{10... | collective-permute-start | bytes 393224 | tf_op jit(solution)/shard_map/ppermute | solution.py:77
  141.4 1.5 flux_kernel.7
  142.9 1.7 %collective-permute-start.32 = (f32[2,16,1024]{2,1,0:T(8,128)S(1)}, f32[2,16,1024]{2,1,0:T(8,128)S(1)}, u32[]{:S(2)}, u32[]{:S(2)}) collective-permute-start(f32[2,16,1024]{2,1,0:T(8,128)S(1)} %get-tuple-element.141), channel_id=1, source_target_pairs={{0,8},{8,0},{16,24},{24,16},{1,9},{9,1},{17,25},{25,17},{2,10},{10... | collective-permute-start | bytes 393224 | tf_op jit(solution)/shard_map/ppermute | solution.py:77
  144.6 1.8 %collective-permute-start.33 = (f32[2,16,1024]{2,1,0:T(8,128)S(1)}, f32[2,16,1024]{2,1,0:T(8,128)S(1)}, u32[]{:S(2)}, u32[]{:S(2)}) collective-permute-start(f32[2,16,1024]{2,1,0:T(8,128)S(1)} %get-tuple-element.142), channel_id=1, source_target_pairs={{0,16},{8,24},{16,0},{24,8},{1,17},{9,25},{17,1},{25,9},{2,18},{10... | collective-permute-start | bytes 393224 | tf_op jit(solution)/shard_map/ppermute | solution.py:77
  148.7 1.6 %collective-permute-done.32.refs_15_ = f32[2,16,1024]{2,1,0:T(8,128)S(1)} collective-permute-done((f32[2,16,1024]{2,1,0:T(8,128)S(1)}, f32[2,16,1024]{2,1,0:T(8,128)S(1)}, u32[]{:S(2)}, u32[]{:S(2)}) %collective-permute-start.32) | collective-permute-done | bytes 131104 | tf_op jit(solution)/shard_map/ppermute | solution.py:77
  150.3 3.4 %collective-permute-done.33.refs_16_ = f32[2,16,1024]{2,1,0:T(8,128)S(1)} collective-permute-done((f32[2,16,1024]{2,1,0:T(8,128)S(1)}, f32[2,16,1024]{2,1,0:T(8,128)S(1)}, u32[]{:S(2)}, u32[]{:S(2)}) %collective-permute-start.33) | collective-permute-done | bytes 131104 | tf_op jit(solution)/shard_map/ppermute | solution.py:77
  153.7 2.6 %finish_kernel.1 = (f32[16,2,128,128]{3,2,1,0:T(8,128)}, f32[8,128]{1,0:T(8,128)}) custom-call(s32[2]{0:T(128)S(1)} %copy-done.6, f32[16,2,128,128]{3,2,1,0:T(8,128)S(1)} %bitcast.11, f32[2,16,1024]{2,1,0:T(8,128)S(1)} %get-tuple-element.104.refs_1_.refs_2_, f32[2,16,1024]{2,1,0:T(8,128)S(1)} %collective-permute-done.14.refs_2_.refs_3_, ...), custom_call_target="tpu_custom_call" | custom-call | bytes 6291464 | tf_op jit(solution)/shard_map/finish_kernel/pallas_call | solution.py:63
  (70 shorter events, 19.1 us)
Async XLA Ops:
  0.0 7.8 %copy-start.10 = (s32[16]{0:T(128)S(1)}, s32[16]{0:T(128)}, u32[]{:S(2)}) copy-start(s32[16]{0:T(128)} %refs_2_.1) | copy-start | bytes 196
  0.0 7.8 %copy-start.9 = (s32[16,2]{0,1:T(2,128)S(1)}, s32[16,2]{0,1:T(2,128)}, u32[]{:S(2)}) copy-start(s32[16,2]{0,1:T(2,128)} %param.11) | copy-start | bytes 388
  0.6 7.2 %copy-start.6 = (s32[2]{0:T(128)S(1)}, s32[2]{0:T(128)}, u32[]{:S(2)}) copy-start(s32[2]{0:T(128)} %pad_add_fusion.refs_0_) | copy-start | bytes 28
  3.3 7.9 %collective-permute-start.3 = (f32[2,16,1024]{2,1,0:T(8,128)}, f32[2,16,1024]{2,1,0:T(8,128)S(1)}, u32[]{:S(2)}, u32[]{:S(2)}) collective-permute-start(f32[2,16,1024]{2,1,0:T(8,128)} %get-tuple-element.81), channel_id=1, source_target_pairs={{0,8},{8,0},{16,24},{24,16},{1,9},{9,1},{17,25},{25,17},{2,10},{10... | collective-permute-start | bytes 393224 | tf_op jit(solution)/shard_map/ppermute | solution.py:77
  6.3 8.0 %collective-permute-start.4 = (f32[2,16,1024]{2,1,0:T(8,128)}, f32[2,16,1024]{2,1,0:T(8,128)S(1)}, u32[]{:S(2)}, u32[]{:S(2)}) collective-permute-start(f32[2,16,1024]{2,1,0:T(8,128)} %get-tuple-element.82), channel_id=1, source_target_pairs={{0,16},{8,24},{16,0},{24,8},{1,17},{9,25},{17,1},{25,9},{2,18},{10... | collective-permute-start | bytes 393224 | tf_op jit(solution)/shard_map/ppermute | solution.py:77
  7.8 6.5 %collective-permute-start.5 = (f32[2,16,1024]{2,1,0:T(8,128)}, f32[2,16,1024]{2,1,0:T(8,128)S(1)}, u32[]{:S(2)}, u32[]{:S(2)}) collective-permute-start(f32[2,16,1024]{2,1,0:T(8,128)} %get-tuple-element.83), channel_id=1, source_target_pairs={{0,24},{8,16},{16,8},{24,0},{1,25},{9,17},{17,9},{25,1},{2,26},{10... | collective-permute-start | bytes 393224 | tf_op jit(solution)/shard_map/ppermute | solution.py:77
  7.8 1.6 %copy-start = (f32[16,2,1,16384]{3,2,1,0:T(1,128)S(1)}, f32[16,2,1,16384]{3,2,1,0:T(1,128)}, u32[]{:S(2)}) copy-start(f32[16,2,1,16384]{3,2,1,0:T(1,128)} %param.8) | copy-start | bytes 6291460
  9.4 0.7 copy-start.8
  10.1 4.2 %copy-start.7 = (f32[2,16,1024]{2,1,0:T(8,128)S(1)}, f32[2,16,1024]{2,1,0:T(8,128)}, u32[]{:S(2)}) copy-start(f32[2,16,1024]{2,1,0:T(8,128)} %get-tuple-element.80.refs_1_) | copy-start | bytes 393220
  10.1 31.1 %copy-start.1 = (bf16[64,192]{1,0:T(8,128)(2,1)S(1)}, bf16[64,192]{1,0:T(8,128)(2,1)}, u32[]{:S(2)}) copy-start(bf16[64,192]{1,0:T(8,128)(2,1)} %constant.12.clone.refs_1_) | copy-start | bytes 73732
  14.8 26.4 %collective-permute-start.10 = (f32[2,64,1024]{2,1,0:T(8,128)S(1)}, f32[2,64,1024]{2,1,0:T(8,128)S(1)}, u32[]{:S(2)}, u32[]{:S(2)}) collective-permute-start(f32[2,64,1024]{2,1,0:T(8,128)S(1)} %get-tuple-element.93.refs_3_), channel_id=1, source_target_pairs={{0,4},{1,5},{6,2},{7,3},{8,12},{9,13},{14,10},{15,11},{16,20},{17,... | collective-permute-start | bytes 1572872 | tf_op jit(solution)/shard_map/ppermute | solution.py:412
  19.4 26.7 %collective-permute-start.9 = (f32[2,64,1024]{2,1,0:T(8,128)S(1)}, f32[2,64,1024]{2,1,0:T(8,128)S(1)}, u32[]{:S(2)}, u32[]{:S(2)}) collective-permute-start(f32[2,64,1024]{2,1,0:T(8,128)S(1)} %get-tuple-element.93.refs_3_), channel_id=1, source_target_pairs={{2,6},{3,7},{4,0},{5,1},{10,14},{11,15},{12,8},{13,9},{18,22},{19,... | collective-permute-start | bytes 1572872 | tf_op jit(solution)/shard_map/ppermute | solution.py:413
  20.7 12.5 %collective-permute-start = (f32[2,16,3200]{2,1,0:T(8,128)S(1)}, f32[2,16,3200]{2,1,0:T(8,128)S(1)}, u32[]{:S(2)}, u32[]{:S(2)}) collective-permute-start(f32[2,16,3200]{2,1,0:T(8,128)S(1)} %get-tuple-element.77), channel_id=1, source_target_pairs={{0,8},{8,0},{16,24},{24,16},{1,9},{9,1},{17,25},{25,17},{2,10},{10... | collective-permute-start | bytes 1228808 | tf_op jit(solution)/shard_map/ppermute | solution.py:77
  22.0 18.6 %collective-permute-start.1 = (f32[2,16,3200]{2,1,0:T(8,128)S(1)}, f32[2,16,3200]{2,1,0:T(8,128)S(1)}, u32[]{:S(2)}, u32[]{:S(2)}) collective-permute-start(f32[2,16,3200]{2,1,0:T(8,128)S(1)} %get-tuple-element.78), channel_id=1, source_target_pairs={{0,16},{8,24},{16,0},{24,8},{1,17},{9,25},{17,1},{25,9},{2,18},{10... | collective-permute-start | bytes 1228808 | tf_op jit(solution)/shard_map/ppermute | solution.py:77
  22.8 17.7 %collective-permute-start.2 = (f32[2,16,3200]{2,1,0:T(8,128)S(1)}, f32[2,16,3200]{2,1,0:T(8,128)S(1)}, u32[]{:S(2)}, u32[]{:S(2)}) collective-permute-start(f32[2,16,3200]{2,1,0:T(8,128)S(1)} %get-tuple-element.79), channel_id=1, source_target_pairs={{0,24},{8,16},{16,8},{24,0},{1,25},{9,17},{17,9},{25,1},{2,26},{10... | collective-permute-start | bytes 1228808 | tf_op jit(solution)/shard_map/ppermute | solution.py:77
  41.2 6.5 %copy-start.2 = (f32[16,2,1,16384]{3,2,1,0:T(1,128)S(1)}, f32[16,2,1,16384]{3,2,1,0:T(1,128)}, u32[]{:S(2)}) copy-start(f32[16,2,1,16384]{3,2,1,0:T(1,128)} %param.9) | copy-start | bytes 6291460
  42.4 20.3 %collective-permute-start.11 = (f32[2,64,1024]{2,1,0:T(8,128)S(1)}, f32[2,64,1024]{2,1,0:T(8,128)S(1)}, u32[]{:S(2)}, u32[]{:S(2)}) collective-permute-start(f32[2,64,1024]{2,1,0:T(8,128)S(1)} %get-tuple-element.97), channel_id=1, source_target_pairs={{0,4},{1,5},{6,2},{7,3},{2,0},{3,1},{4,6},{5,7},{8,12},{9,13},{14,... | collective-permute-start | bytes 1572872 | tf_op jit(solution)/shard_map/ppermute | solution.py:412
  47.6 23.7 %collective-permute-start.12 = (f32[2,64,1024]{2,1,0:T(8,128)S(1)}, f32[2,64,1024]{2,1,0:T(8,128)S(1)}, u32[]{:S(2)}, u32[]{:S(2)}) collective-permute-start(f32[2,64,1024]{2,1,0:T(8,128)S(1)} %get-tuple-element.98), channel_id=1, source_target_pairs={{2,6},{3,7},{4,0},{5,1},{0,2},{1,3},{6,4},{7,5},{10,14},{11,15},{1... | collective-permute-start | bytes 1572872 | tf_op jit(solution)/shard_map/ppermute | solution.py:413
  64.0 12.3 %collective-permute-start.17 = (f32[2,64,1024]{2,1,0:T(8,128)S(1)}, f32[2,64,1024]{2,1,0:T(8,128)S(1)}, u32[]{:S(2)}, u32[]{:S(2)}) collective-permute-start(f32[2,64,1024]{2,1,0:T(8,128)S(1)} %get-tuple-element.109), channel_id=1, source_target_pairs={{0,4},{1,5},{6,2},{7,3},{2,0},{3,1},{4,6},{5,7},{8,12},{9,13},{14,... | collective-permute-start | bytes 1572872 | tf_op jit(solution)/shard_map/ppermute | solution.py:412
  73.0 26.6 %collective-permute-start.13 = (f32[4,64,1024]{2,1,0:T(8,128)S(1)}, f32[4,64,1024]{2,1,0:T(8,128)S(1)}, u32[]{:S(2)}, u32[]{:S(2)}) collective-permute-start(f32[4,64,1024]{2,1,0:T(8,128)S(1)} %get-tuple-element.103.refs_5_), channel_id=1, source_target_pairs={{0,1},{1,0},{2,3},{3,2},{4,5},{5,4},{6,7},{7,6},{8,9},{9,8},{10,11... | collective-permute-start | bytes 3145736 | tf_op jit(solution)/shard_map/ppermute | solution.py:77
  73.1 15.2 %collective-permute-start.18 = (f32[2,64,1024]{2,1,0:T(8,128)S(1)}, f32[2,64,1024]{2,1,0:T(8,128)S(1)}, u32[]{:S(2)}, u32[]{:S(2)}) collective-permute-start(f32[2,64,1024]{2,1,0:T(8,128)S(1)} %get-tuple-element.110), channel_id=1, source_target_pairs={{2,6},{3,7},{4,0},{5,1},{0,2},{1,3},{6,4},{7,5},{10,14},{11,15},{1... | collective-permute-start | bytes 1572872 | tf_op jit(solution)/shard_map/ppermute | solution.py:413
  73.4 16.3 %collective-permute-start.6 = (f32[2,16,4096]{2,1,0:T(8,128)S(1)}, f32[2,16,4096]{2,1,0:T(8,128)S(1)}, u32[]{:S(2)}, u32[]{:S(2)}) collective-permute-start(f32[2,16,4096]{2,1,0:T(8,128)S(1)} %get-tuple-element.89), channel_id=1, source_target_pairs={{0,8},{8,0},{16,24},{24,16},{1,9},{9,1},{17,25},{25,17},{2,10},{10... | collective-permute-start | bytes 1572872 | tf_op jit(solution)/shard_map/ppermute | solution.py:77
  74.0 24.9 %collective-permute-start.7 = (f32[2,16,4096]{2,1,0:T(8,128)S(1)}, f32[2,16,4096]{2,1,0:T(8,128)S(1)}, u32[]{:S(2)}, u32[]{:S(2)}) collective-permute-start(f32[2,16,4096]{2,1,0:T(8,128)S(1)} %get-tuple-element.90), channel_id=1, source_target_pairs={{0,16},{8,24},{16,0},{24,8},{1,17},{9,25},{17,1},{25,9},{2,18},{10... | collective-permute-start | bytes 1572872 | tf_op jit(solution)/shard_map/ppermute | solution.py:77
  76.3 22.6 %collective-permute-start.8 = (f32[2,16,4096]{2,1,0:T(8,128)S(1)}, f32[2,16,4096]{2,1,0:T(8,128)S(1)}, u32[]{:S(2)}, u32[]{:S(2)}) collective-permute-start(f32[2,16,4096]{2,1,0:T(8,128)S(1)} %get-tuple-element.91), channel_id=1, source_target_pairs={{0,24},{8,16},{16,8},{24,0},{1,25},{9,17},{17,9},{25,1},{2,26},{10... | collective-permute-start | bytes 1572872 | tf_op jit(solution)/shard_map/ppermute | solution.py:77
  88.3 24.0 %collective-permute-start.23 = (f32[2,64,1024]{2,1,0:T(8,128)S(1)}, f32[2,64,1024]{2,1,0:T(8,128)S(1)}, u32[]{:S(2)}, u32[]{:S(2)}) collective-permute-start(f32[2,64,1024]{2,1,0:T(8,128)S(1)} %get-tuple-element.121), channel_id=1, source_target_pairs={{0,4},{1,5},{6,2},{7,3},{2,0},{3,1},{4,6},{5,7},{8,12},{9,13},{14,... | collective-permute-start | bytes 1572872 | tf_op jit(solution)/shard_map/ppermute | solution.py:412
  88.8 10.9 %copy-start.4 = (f32[1,16384]{1,0:T(1,128)S(1)}, f32[1,16384]{1,0:T(1,128)}, u32[]{:S(2)}) copy-start(f32[1,16384]{1,0:T(1,128)} %param.12) | copy-start | bytes 196612
  88.8 10.9 %copy-start.5 = (bf16[64,192]{1,0:T(8,128)(2,1)S(1)}, bf16[64,192]{1,0:T(8,128)(2,1)}, u32[]{:S(2)}) copy-start(bf16[64,192]{1,0:T(8,128)(2,1)} %constant.13.clone.refs_1_) | copy-start | bytes 73732
  89.8 24.7 %collective-permute-start.24 = (f32[2,64,1024]{2,1,0:T(8,128)S(1)}, f32[2,64,1024]{2,1,0:T(8,128)S(1)}, u32[]{:S(2)}, u32[]{:S(2)}) collective-permute-start(f32[2,64,1024]{2,1,0:T(8,128)S(1)} %get-tuple-element.122), channel_id=1, source_target_pairs={{2,6},{3,7},{4,0},{5,1},{0,2},{1,3},{6,4},{7,5},{10,14},{11,15},{1... | collective-permute-start | bytes 1572872 | tf_op jit(solution)/shard_map/ppermute | solution.py:413
  100.8 5.0 %collective-permute-start.14 = (f32[2,16,1024]{2,1,0:T(8,128)S(1)}, f32[2,16,1024]{2,1,0:T(8,128)S(1)}, u32[]{:S(2)}, u32[]{:S(2)}) collective-permute-start(f32[2,16,1024]{2,1,0:T(8,128)S(1)} %get-tuple-element.105), channel_id=1, source_target_pairs={{0,8},{8,0},{16,24},{24,16},{1,9},{9,1},{17,25},{25,17},{2,10},{10... | collective-permute-start | bytes 393224 | tf_op jit(solution)/shard_map/ppermute | solution.py:77
  102.9 19.1 %collective-permute-start.19 = (f32[4,64,1024]{2,1,0:T(8,128)S(1)}, f32[4,64,1024]{2,1,0:T(8,128)S(1)}, u32[]{:S(2)}, u32[]{:S(2)}) collective-permute-start(f32[4,64,1024]{2,1,0:T(8,128)S(1)} %get-tuple-element.115.refs_5_), channel_id=1, source_target_pairs={{0,1},{1,0},{2,3},{3,2},{4,5},{5,4},{6,7},{7,6},{8,9},{9,8},{10,11... | collective-permute-start | bytes 3145736 | tf_op jit(solution)/shard_map/ppermute | solution.py:77
  103.0 7.3 %collective-permute-start.15 = (f32[2,16,1024]{2,1,0:T(8,128)S(1)}, f32[2,16,1024]{2,1,0:T(8,128)S(1)}, u32[]{:S(2)}, u32[]{:S(2)}) collective-permute-start(f32[2,16,1024]{2,1,0:T(8,128)S(1)} %get-tuple-element.106), channel_id=1, source_target_pairs={{0,16},{8,24},{16,0},{24,8},{1,17},{9,25},{17,1},{25,9},{2,18},{10... | collective-permute-start | bytes 393224 | tf_op jit(solution)/shard_map/ppermute | solution.py:77
  105.8 5.9 %collective-permute-start.16 = (f32[2,16,1024]{2,1,0:T(8,128)S(1)}, f32[2,16,1024]{2,1,0:T(8,128)S(1)}, u32[]{:S(2)}, u32[]{:S(2)}) collective-permute-start(f32[2,16,1024]{2,1,0:T(8,128)S(1)} %get-tuple-element.107), channel_id=1, source_target_pairs={{0,24},{8,16},{16,8},{24,0},{1,25},{9,17},{17,9},{25,1},{2,26},{10... | collective-permute-start | bytes 393224 | tf_op jit(solution)/shard_map/ppermute | solution.py:77
  116.1 19.4 %collective-permute-start.25 = (f32[4,64,1024]{2,1,0:T(8,128)S(1)}, f32[4,64,1024]{2,1,0:T(8,128)S(1)}, u32[]{:S(2)}, u32[]{:S(2)}) collective-permute-start(f32[4,64,1024]{2,1,0:T(8,128)S(1)} %get-tuple-element.128.refs_5_), channel_id=1, source_target_pairs={{0,1},{1,0},{2,3},{3,2},{4,5},{5,4},{6,7},{7,6},{8,9},{9,8},{10,11... | collective-permute-start | bytes 3145736 | tf_op jit(solution)/shard_map/ppermute | solution.py:77
  116.1 20.5 %collective-permute-start.29 = (f32[2,64,1024]{2,1,0:T(8,128)S(1)}, f32[2,64,1024]{2,1,0:T(8,128)S(1)}, u32[]{:S(2)}, u32[]{:S(2)}) collective-permute-start(f32[2,64,1024]{2,1,0:T(8,128)S(1)} %get-tuple-element.134), channel_id=1, source_target_pairs={{2,0},{3,1},{4,6},{5,7},{10,8},{11,9},{12,14},{13,15},{18,16},{19,... | collective-permute-start | bytes 1572872 | tf_op jit(solution)/shard_map/ppermute | solution.py:440
  117.4 19.2 %collective-permute-start.30 = (f32[2,64,1024]{2,1,0:T(8,128)S(1)}, f32[2,64,1024]{2,1,0:T(8,128)S(1)}, u32[]{:S(2)}, u32[]{:S(2)}) collective-permute-start(f32[2,64,1024]{2,1,0:T(8,128)S(1)} %get-tuple-element.135), channel_id=1, source_target_pairs={{0,2},{1,3},{6,4},{7,5},{8,10},{9,11},{14,12},{15,13},{16,18},{17,... | collective-permute-start | bytes 1572872 | tf_op jit(solution)/shard_map/ppermute | solution.py:441
  123.2 5.8 %collective-permute-start.20 = (f32[2,16,1024]{2,1,0:T(8,128)S(1)}, f32[2,16,1024]{2,1,0:T(8,128)S(1)}, u32[]{:S(2)}, u32[]{:S(2)}) collective-permute-start(f32[2,16,1024]{2,1,0:T(8,128)S(1)} %get-tuple-element.117), channel_id=1, source_target_pairs={{0,8},{8,0},{16,24},{24,16},{1,9},{9,1},{17,25},{25,17},{2,10},{10... | collective-permute-start | bytes 393224 | tf_op jit(solution)/shard_map/ppermute | solution.py:77
  125.5 6.6 %collective-permute-start.21 = (f32[2,16,1024]{2,1,0:T(8,128)S(1)}, f32[2,16,1024]{2,1,0:T(8,128)S(1)}, u32[]{:S(2)}, u32[]{:S(2)}) collective-permute-start(f32[2,16,1024]{2,1,0:T(8,128)S(1)} %get-tuple-element.118), channel_id=1, source_target_pairs={{0,16},{8,24},{16,0},{24,8},{1,17},{9,25},{17,1},{25,9},{2,18},{10... | collective-permute-start | bytes 393224 | tf_op jit(solution)/shard_map/ppermute | solution.py:77
  129.0 5.9 %collective-permute-start.22 = (f32[2,16,1024]{2,1,0:T(8,128)S(1)}, f32[2,16,1024]{2,1,0:T(8,128)S(1)}, u32[]{:S(2)}, u32[]{:S(2)}) collective-permute-start(f32[2,16,1024]{2,1,0:T(8,128)S(1)} %get-tuple-element.119), channel_id=1, source_target_pairs={{0,24},{8,16},{16,8},{24,0},{1,25},{9,17},{17,9},{25,1},{2,26},{10... | collective-permute-start | bytes 393224 | tf_op jit(solution)/shard_map/ppermute | solution.py:77
  137.9 3.5 %collective-permute-start.31 = (f32[4,64,1024]{2,1,0:T(8,128)S(1)}, f32[4,64,1024]{2,1,0:T(8,128)S(1)}, u32[]{:S(2)}, u32[]{:S(2)}) collective-permute-start(f32[4,64,1024]{2,1,0:T(8,128)S(1)} %get-tuple-element.139.refs_5_), channel_id=1, source_target_pairs={{0,1},{1,0},{2,3},{3,2},{4,5},{5,4},{6,7},{7,6},{8,9},{9,8},{10,11... | collective-permute-start | bytes 3145736 | tf_op jit(solution)/shard_map/ppermute | solution.py:77
  137.9 8.5 %collective-permute-start.26 = (f32[2,16,1024]{2,1,0:T(8,128)S(1)}, f32[2,16,1024]{2,1,0:T(8,128)S(1)}, u32[]{:S(2)}, u32[]{:S(2)}) collective-permute-start(f32[2,16,1024]{2,1,0:T(8,128)S(1)} %get-tuple-element.130), channel_id=1, source_target_pairs={{0,8},{8,0},{16,24},{24,16},{1,9},{9,1},{17,25},{25,17},{2,10},{10... | collective-permute-start | bytes 393224 | tf_op jit(solution)/shard_map/ppermute | solution.py:77
  139.6 8.3 %collective-permute-start.27 = (f32[2,16,1024]{2,1,0:T(8,128)S(1)}, f32[2,16,1024]{2,1,0:T(8,128)S(1)}, u32[]{:S(2)}, u32[]{:S(2)}) collective-permute-start(f32[2,16,1024]{2,1,0:T(8,128)S(1)} %get-tuple-element.131), channel_id=1, source_target_pairs={{0,16},{8,24},{16,0},{24,8},{1,17},{9,25},{17,1},{25,9},{2,18},{10... | collective-permute-start | bytes 393224 | tf_op jit(solution)/shard_map/ppermute | solution.py:77
  141.4 12.3 %copy-start.3 = (f32[16,2,1,16384]{3,2,1,0:T(1,128)S(1)}, f32[16,2,1,16384]{3,2,1,0:T(1,128)}, u32[]{:S(2)}) copy-start(f32[16,2,1,16384]{3,2,1,0:T(1,128)} %param.13) | copy-start | bytes 6291460
  141.4 7.3 %collective-permute-start.28 = (f32[2,16,1024]{2,1,0:T(8,128)S(1)}, f32[2,16,1024]{2,1,0:T(8,128)S(1)}, u32[]{:S(2)}, u32[]{:S(2)}) collective-permute-start(f32[2,16,1024]{2,1,0:T(8,128)S(1)} %get-tuple-element.132), channel_id=1, source_target_pairs={{0,24},{8,16},{16,8},{24,0},{1,25},{9,17},{17,9},{25,1},{2,26},{10... | collective-permute-start | bytes 393224 | tf_op jit(solution)/shard_map/ppermute | solution.py:77
  142.9 7.3 %collective-permute-start.32 = (f32[2,16,1024]{2,1,0:T(8,128)S(1)}, f32[2,16,1024]{2,1,0:T(8,128)S(1)}, u32[]{:S(2)}, u32[]{:S(2)}) collective-permute-start(f32[2,16,1024]{2,1,0:T(8,128)S(1)} %get-tuple-element.141), channel_id=1, source_target_pairs={{0,8},{8,0},{16,24},{24,16},{1,9},{9,1},{17,25},{25,17},{2,10},{10... | collective-permute-start | bytes 393224 | tf_op jit(solution)/shard_map/ppermute | solution.py:77
  144.6 9.1 %collective-permute-start.33 = (f32[2,16,1024]{2,1,0:T(8,128)S(1)}, f32[2,16,1024]{2,1,0:T(8,128)S(1)}, u32[]{:S(2)}, u32[]{:S(2)}) collective-permute-start(f32[2,16,1024]{2,1,0:T(8,128)S(1)} %get-tuple-element.142), channel_id=1, source_target_pairs={{0,16},{8,24},{16,0},{24,8},{1,17},{9,25},{17,1},{25,9},{2,18},{10... | collective-permute-start | bytes 393224 | tf_op jit(solution)/shard_map/ppermute | solution.py:77
  146.4 7.3 %collective-permute-start.34 = (f32[2,16,1024]{2,1,0:T(8,128)S(1)}, f32[2,16,1024]{2,1,0:T(8,128)S(1)}, u32[]{:S(2)}, u32[]{:S(2)}) collective-permute-start(f32[2,16,1024]{2,1,0:T(8,128)S(1)} %get-tuple-element.143), channel_id=1, source_target_pairs={{0,24},{8,16},{16,8},{24,0},{1,25},{9,17},{17,9},{25,1},{2,26},{10... | collective-permute-start | bytes 393224 | tf_op jit(solution)/shard_map/ppermute | solution.py:77

commit v5 on v4

--- a/solution.py
+++ b/solution.py
@@ -276,25 +276,41 @@
             outs[i][comp] = result[pl.ds(first, rows), comp * total : (comp + 1) * total]
 
 
-def finish_kernel(parts, chunks, place, source, *refs):
-    pieces, (out, made, sems) = refs[:-3], refs[-3:]
+def less_source(parts, chunks, row0, height, place, source, pieces, made):
     share_rows = source.shape[2] // parts
-    copies = []
-    for i in range(parts):
-        first = pl.multiple_of((place[0] ^ i) * share_rows, SUBLANES)
+    for i in range(parts):
+        first = pl.multiple_of((place[0] ^ i) * share_rows, SUBLANES) + row0
         for comp in range(2):
             rows = [
                 pieces[g * parts + i][comp, :, lane : lane + LANES]
                 for g in range(chunks)
                 for lane in range(0, pieces[g * parts].shape[2], LANES)
             ]
-            for row in range(0, share_rows, SUBLANES):
+            for row in range(0, height, SUBLANES):
                 turned = jnp.swapaxes(jnp.stack(rows[row : row + SUBLANES]), 0, 1)
-                made[i, :, comp, row : row + SUBLANES, :] = turned - source[:, comp, pl.ds(first + row, SUBLANES), :]
-        copies.append(
-            pltpu.make_async_copy(made.at[i], out.at[:, :, pl.ds(first, share_rows), :], sems.at[i])
-        )
-        copies[i].start()
+                here = pl.ds(pl.multiple_of(first + row, SUBLANES), SUBLANES)
+                made[i, :, comp, row : row + SUBLANES, :] = turned - source[:, comp, here, :]
+
+
+def early_kernel(parts, chunks, place, source, *refs):
+    less_source(parts, chunks, 0, refs[-1].shape[3], place, source, refs[:-1], refs[-1])
+
+
+def finish_kernel(parts, chunks, place, source, early, *refs):
+    pieces, (out, made, sems) = refs[:-3], refs[-3:]
+    share_rows = source.shape[2] // parts
+    early_rows, late_rows = early.shape[3], made.shape[3]
+    copies = []
+    for i in range(parts):
+        first = pl.multiple_of((place[0] ^ i) * share_rows, SUBLANES)
+        here = pl.ds(first, early_rows)
+        there = pl.ds(pl.multiple_of(first + early_rows, SUBLANES), late_rows)
+        copies.append(pltpu.make_async_copy(early.at[i], out.at[:, :, here, :], sems.at[0, i]))
+        copies.append(pltpu.make_async_copy(made.at[i], out.at[:, :, there, :], sems.at[1, i]))
+        copies[2 * i].start()
+    less_source(parts, chunks, early_rows, late_rows, place, source, pieces, made)
+    for i in range(parts):
+        copies[2 * i + 1].start()
     for copy in copies:
         copy.wait()
 
@@ -435,19 +451,27 @@
             pieces += made
             gate = gates.setdefault(min(k - 1 + FLUX_GATE, chunks), [])
             gate.append(token)
-            if k - 1 in SEEN:
+            if k - 1 == SEEN[-1]:
+                early_rows = sum(heights[:k])
+                early, token = call(
+                    functools.partial(early_kernel, parts, k),
+                    [f32(parts, coeff_rows, comps, early_rows, LANES)],
+                    (place, in_rows(source), *pieces),
+                )
+                gate.append(token)
+            elif k - 1 in SEEN:
                 gate += call(functools.partial(seen_kernel), [], (place, *made))
     slot_a = lax.ppermute(send_a, "azim", sample_a)
     slot_b = lax.ppermute(send_b, "azim", sample_b)
     *pair, _ = neighbours(keeps[-1], slot_a, slot_b, gates.get(chunks, ()))
     pieces += flux(chunks - 1, *pair)[0]
     out, _ = call(
-        functools.partial(finish_kernel, parts, chunks),
+        functools.partial(finish_kernel, parts, chunks - len(SEEN)),
         [f32(coeff_rows, comps, nodes // LANES, LANES)],
-        (place, in_rows(source), *pieces),
+        (place, in_rows(source), early, *pieces[len(SEEN) * parts :]),
         scratch=(
-            pltpu.VMEM((parts, coeff_rows, comps, share_rows, LANES), jnp.float32),
-            pltpu.SemaphoreType.DMA((parts,)),
+            pltpu.VMEM((parts, coeff_rows, comps, share_rows - early_rows, LANES), jnp.float32),
+            pltpu.SemaphoreType.DMA((2, parts)),
         ),
         out_hbm=True,
     )

time: 157 us -> 157 us (level)
  no operation moved by 1% of the time
where the time goes in v5:
time: 157 us
  waiting for transfers between devices  73.2 us (47%)
  starting transfers between devices  52.2 us (33%)
  Pallas kernels  27.9 us (18%)
  local copies, waits for them, and re-layouts  2.3 us (1%)
    ppermute x25, waiting for transfers between devices, xor_permute(): return lax.ppermute(value, axis, [(i, i ^ step) for i in range(count)])  45 us
    ppermute x25, starting transfers between devices, xor_permute(): return lax.ppermute(value, axis, [(i, i ^ step) for i in range(count)])  34.2 us
    pallas_call x25, Pallas kernels, call(): pl.pallas_call(run, name=kernel.func.__name__, out_shape=[jax.ShapeDtypeS...  27.9 us
    ppermute x4, waiting for transfers between devices, body(): lax.ppermute(send_a, 'azim', coeff_a + (sample_a if k else []))  14.9 us
    ppermute x4, waiting for transfers between devices, body(): lax.ppermute(send_b, 'azim', coeff_b + (sample_b if k else []))  13.2 us
    ppermute x4, starting transfers between devices, body(): lax.ppermute(send_a, 'azim', coeff_a + (sample_a if k else []))  9.06 us
    ppermute x1, starting transfers between devices, body(): slot_b = lax.ppermute(send_b, 'azim', sample_b)  4.74 us
  transfers between devices with their start and end apart: 35, of which 18 were waited for; matrix products, arithmetic and copies ran while one was open for 0% of the time, Pallas kernels for 13%

profile of v5, /device:TPU:0, one launch (start us, length us, event | category | flops | bytes accessed | tf_op | source)
XLA Modules:
  0.0 156.6 jit_solution(17900839961806618991)
XLA Ops:
  0.6 2.6 %pack_kernel.2 = (f32[2,16,1024]{2,1,0:T(8,128)}, f32[2,16,1024]{2,1,0:T(8,128)}, f32[2,16,1024]{2,1,0:T(8,128)}, f32[2,16,1024]{2,1,0:T(8,128)}, f32[8,128]{1,0:T(8,128)}) custom-call(s32[2]{0:T(128)} %pad_add_fusion.refs_0_, f32[16,2,128,128]{3,2,1,0:T(8,128)} %bitcast.8), custom_call_target="tpu_custom_call" | custom-call | bytes 2621448 | tf_op jit(solution)/shard_map/pack_kernel/pallas_call | solution.py:63
  3.2 3.0 %collective-permute-start.3 = (f32[2,16,1024]{2,1,0:T(8,128)}, f32[2,16,1024]{2,1,0:T(8,128)S(1)}, u32[]{:S(2)}, u32[]{:S(2)}) collective-permute-start(f32[2,16,1024]{2,1,0:T(8,128)} %get-tuple-element.83), channel_id=1, source_target_pairs={{0,8},{8,0},{16,24},{24,16},{1,9},{9,1},{17,25},{25,17},{2,10},{10... | collective-permute-start | bytes 393224 | tf_op jit(solution)/shard_map/ppermute | solution.py:77
  6.2 1.5 collective-permute-start.4
  7.8 1.6 %copy-done = f32[16,2,1,16384]{3,2,1,0:T(1,128)S(1)} copy-done((f32[16,2,1,16384]{3,2,1,0:T(1,128)S(1)}, f32[16,2,1,16384]{3,2,1,0:T(1,128)}, u32[]{:S(2)}) %copy-start) | copy-done | bytes 2097176
  11.2 3.1 %collective-permute-done.4.refs_3_ = f32[2,16,1024]{2,1,0:T(8,128)S(1)} collective-permute-done((f32[2,16,1024]{2,1,0:T(8,128)}, f32[2,16,1024]{2,1,0:T(8,128)S(1)}, u32[]{:S(2)}, u32[]{:S(2)}) %collective-permute-start.4) | collective-permute-done | bytes 131104 | tf_op jit(solution)/shard_map/ppermute | solution.py:77
  14.8 4.5 %collective-permute-start.10 = (f32[2,64,1024]{2,1,0:T(8,128)S(1)}, f32[2,64,1024]{2,1,0:T(8,128)S(1)}, u32[]{:S(2)}, u32[]{:S(2)}) collective-permute-start(f32[2,64,1024]{2,1,0:T(8,128)S(1)} %get-tuple-element.95.refs_3_), channel_id=1, source_target_pairs={{0,4},{1,5},{6,2},{7,3},{8,12},{9,13},{14,10},{15,11},{16,20},{17,... | collective-permute-start | bytes 1572872 | tf_op jit(solution)/shard_map/ppermute | solution.py:428
  19.4 1.3 collective-permute-start.9
  20.7 1.3 collective-permute-start
  22.8 1.4 collective-permute-start.2
  24.2 8.9 %collective-permute-done.refs_2_ = f32[2,16,3200]{2,1,0:T(8,128)S(1)} collective-permute-done((f32[2,16,3200]{2,1,0:T(8,128)S(1)}, f32[2,16,3200]{2,1,0:T(8,128)S(1)}, u32[]{:S(2)}, u32[]{:S(2)}) %collective-permute-start) | collective-permute-done | bytes 409632 | tf_op jit(solution)/shard_map/ppermute | solution.py:77
  33.1 7.4 %collective-permute-done.1.refs_3_ = f32[2,16,3200]{2,1,0:T(8,128)S(1)} collective-permute-done((f32[2,16,3200]{2,1,0:T(8,128)S(1)}, f32[2,16,3200]{2,1,0:T(8,128)S(1)}, u32[]{:S(2)}, u32[]{:S(2)}) %collective-permute-start.1) | collective-permute-done | bytes 409632 | tf_op jit(solution)/shard_map/ppermute | solution.py:77
  41.2 1.2 first_kernel.4
  42.4 3.6 %collective-permute-start.11 = (f32[2,64,1024]{2,1,0:T(8,128)S(1)}, f32[2,64,1024]{2,1,0:T(8,128)S(1)}, u32[]{:S(2)}, u32[]{:S(2)}) collective-permute-start(f32[2,64,1024]{2,1,0:T(8,128)S(1)} %get-tuple-element.99), channel_id=1, source_target_pairs={{0,4},{1,5},{6,2},{7,3},{2,0},{3,1},{4,6},{5,7},{8,12},{9,13},{14,... | collective-permute-start | bytes 1572872 | tf_op jit(solution)/shard_map/ppermute | solution.py:428
  46.1 1.6 second_kernel.4
  47.6 1.1 pack_kernel.3
  48.8 14.0 %collective-permute-done.11.refs_4_.refs_2_ = f32[2,64,1024]{2,1,0:T(8,128)S(1)} collective-permute-done((f32[2,64,1024]{2,1,0:T(8,128)S(1)}, f32[2,64,1024]{2,1,0:T(8,128)S(1)}, u32[]{:S(2)}, u32[]{:S(2)}) %collective-permute-start.11) | collective-permute-done | bytes 524320 | tf_op jit(solution)/shard_map/ppermute | solution.py:428
  62.7 1.2 first_kernel.5
  64.3 7.0 %collective-permute-done.12.refs_4_.refs_3_ = f32[2,64,1024]{2,1,0:T(8,128)S(1)} collective-permute-done((f32[2,64,1024]{2,1,0:T(8,128)S(1)}, f32[2,64,1024]{2,1,0:T(8,128)S(1)}, u32[]{:S(2)}, u32[]{:S(2)}) %collective-permute-start.12) | collective-permute-done | bytes 524320 | tf_op jit(solution)/shard_map/ppermute | solution.py:429
  74.0 1.4 collective-permute-start.7
  76.3 5.5 %collective-permute-start.8 = (f32[2,16,4096]{2,1,0:T(8,128)S(1)}, f32[2,16,4096]{2,1,0:T(8,128)S(1)}, u32[]{:S(2)}, u32[]{:S(2)}) collective-permute-start(f32[2,16,4096]{2,1,0:T(8,128)S(1)} %get-tuple-element.93), channel_id=1, source_target_pairs={{0,24},{8,16},{16,8},{24,0},{1,25},{9,17},{17,9},{25,1},{2,26},{10... | collective-permute-start | bytes 1572872 | tf_op jit(solution)/shard_map/ppermute | solution.py:77
  81.8 1.2 first_kernel.6
  83.0 5.3 %collective-permute-done.18.refs_4_.refs_3_ = f32[2,64,1024]{2,1,0:T(8,128)S(1)} collective-permute-done((f32[2,64,1024]{2,1,0:T(8,128)S(1)}, f32[2,64,1024]{2,1,0:T(8,128)S(1)}, u32[]{:S(2)}, u32[]{:S(2)}) %collective-permute-start.18) | collective-permute-done | bytes 524320 | tf_op jit(solution)/shard_map/ppermute | solution.py:429
  89.8 1.2 collective-permute-start.24
  91.0 7.9 %collective-permute-done.7.refs_3_ = f32[2,16,4096]{2,1,0:T(8,128)S(1)} collective-permute-done((f32[2,16,4096]{2,1,0:T(8,128)S(1)}, f32[2,16,4096]{2,1,0:T(8,128)S(1)}, u32[]{:S(2)}, u32[]{:S(2)}) %collective-permute-start.7) | collective-permute-done | bytes 524320 | tf_op jit(solution)/shard_map/ppermute | solution.py:77
  100.8 1.5 collective-permute-start.14
  103.7 2.1 %collective-permute-done.14.refs_3_.refs_2_ = f32[2,16,1024]{2,1,0:T(8,128)S(1)} collective-permute-done((f32[2,16,1024]{2,1,0:T(8,128)S(1)}, f32[2,16,1024]{2,1,0:T(8,128)S(1)}, u32[]{:S(2)}, u32[]{:S(2)}) %collective-permute-start.14) | collective-permute-done | bytes 131104 | tf_op jit(solution)/shard_map/ppermute | solution.py:77
  105.8 1.6 %collective-permute-start.16 = (f32[2,16,1024]{2,1,0:T(8,128)S(1)}, f32[2,16,1024]{2,1,0:T(8,128)S(1)}, u32[]{:S(2)}, u32[]{:S(2)}) collective-permute-start(f32[2,16,1024]{2,1,0:T(8,128)S(1)} %get-tuple-element.109), channel_id=1, source_target_pairs={{0,24},{8,16},{16,8},{24,0},{1,25},{9,17},{17,9},{25,1},{2,26},{10... | collective-permute-start | bytes 393224 | tf_op jit(solution)/shard_map/ppermute | solution.py:77
  107.4 3.0 %collective-permute-done.15.refs_4_.refs_3_ = f32[2,16,1024]{2,1,0:T(8,128)S(1)} collective-permute-done((f32[2,16,1024]{2,1,0:T(8,128)S(1)}, f32[2,16,1024]{2,1,0:T(8,128)S(1)}, u32[]{:S(2)}, u32[]{:S(2)}) %collective-permute-start.15) | collective-permute-done | bytes 131104 | tf_op jit(solution)/shard_map/ppermute | solution.py:77
  110.3 1.4 collective-permute-done.16.refs_5_.refs_4_
  112.3 1.2 first_kernel.7
  116.1 1.3 collective-permute-start.29
  117.4 4.7 %collective-permute-start.30 = (f32[2,64,1024]{2,1,0:T(8,128)S(1)}, f32[2,64,1024]{2,1,0:T(8,128)S(1)}, u32[]{:S(2)}, u32[]{:S(2)}) collective-permute-start(f32[2,64,1024]{2,1,0:T(8,128)S(1)} %get-tuple-element.138), channel_id=1, source_target_pairs={{0,2},{1,3},{6,4},{7,5},{8,10},{9,11},{14,12},{15,13},{16,18},{17,... | collective-permute-start | bytes 1572872 | tf_op jit(solution)/shard_map/ppermute | solution.py:465
  122.2 1.1 flux_kernel.5
  123.3 2.2 %collective-permute-start.20 = (f32[2,16,1024]{2,1,0:T(8,128)S(1)}, f32[2,16,1024]{2,1,0:T(8,128)S(1)}, u32[]{:S(2)}, u32[]{:S(2)}) collective-permute-start(f32[2,16,1024]{2,1,0:T(8,128)S(1)} %get-tuple-element.119), channel_id=1, source_target_pairs={{0,8},{8,0},{16,24},{24,16},{1,9},{9,1},{17,25},{25,17},{2,10},{10... | collective-permute-start | bytes 393224 | tf_op jit(solution)/shard_map/ppermute | solution.py:77
  125.6 1.8 %collective-permute-start.21 = (f32[2,16,1024]{2,1,0:T(8,128)S(1)}, f32[2,16,1024]{2,1,0:T(8,128)S(1)}, u32[]{:S(2)}, u32[]{:S(2)}) collective-permute-start(f32[2,16,1024]{2,1,0:T(8,128)S(1)} %get-tuple-element.120), channel_id=1, source_target_pairs={{0,16},{8,24},{16,0},{24,8},{1,17},{9,25},{17,1},{25,9},{2,18},{10... | collective-permute-start | bytes 393224 | tf_op jit(solution)/shard_map/ppermute | solution.py:77
  127.4 1.8 %collective-permute-done.20.refs_7_ = f32[2,16,1024]{2,1,0:T(8,128)S(1)} collective-permute-done((f32[2,16,1024]{2,1,0:T(8,128)S(1)}, f32[2,16,1024]{2,1,0:T(8,128)S(1)}, u32[]{:S(2)}, u32[]{:S(2)}) %collective-permute-start.20) | collective-permute-done | bytes 131104 | tf_op jit(solution)/shard_map/ppermute | solution.py:77
  129.2 3.0 %collective-permute-start.22 = (f32[2,16,1024]{2,1,0:T(8,128)S(1)}, f32[2,16,1024]{2,1,0:T(8,128)S(1)}, u32[]{:S(2)}, u32[]{:S(2)}) collective-permute-start(f32[2,16,1024]{2,1,0:T(8,128)S(1)} %get-tuple-element.121), channel_id=1, source_target_pairs={{0,24},{8,16},{16,8},{24,0},{1,25},{9,17},{17,9},{25,1},{2,26},{10... | collective-permute-start | bytes 393224 | tf_op jit(solution)/shard_map/ppermute | solution.py:77
  132.1 2.9 %collective-permute-done.22.refs_9_ = f32[2,16,1024]{2,1,0:T(8,128)S(1)} collective-permute-done((f32[2,16,1024]{2,1,0:T(8,128)S(1)}, f32[2,16,1024]{2,1,0:T(8,128)S(1)}, u32[]{:S(2)}, u32[]{:S(2)}) %collective-permute-start.22) | collective-permute-done | bytes 131104 | tf_op jit(solution)/shard_map/ppermute | solution.py:77
  135.9 1.1 flux_kernel.6
  137.0 1.2 pair_kernel.7
  138.2 1.7 %collective-permute-start.26 = (f32[2,16,1024]{2,1,0:T(8,128)S(1)}, f32[2,16,1024]{2,1,0:T(8,128)S(1)}, u32[]{:S(2)}, u32[]{:S(2)}) collective-permute-start(f32[2,16,1024]{2,1,0:T(8,128)S(1)} %get-tuple-element.133), channel_id=1, source_target_pairs={{0,8},{8,0},{16,24},{24,16},{1,9},{9,1},{17,25},{25,17},{2,10},{10... | collective-permute-start | bytes 393224 | tf_op jit(solution)/shard_map/ppermute | solution.py:77
  139.9 1.8 %collective-permute-start.27 = (f32[2,16,1024]{2,1,0:T(8,128)S(1)}, f32[2,16,1024]{2,1,0:T(8,128)S(1)}, u32[]{:S(2)}, u32[]{:S(2)}) collective-permute-start(f32[2,16,1024]{2,1,0:T(8,128)S(1)} %get-tuple-element.134), channel_id=1, source_target_pairs={{0,16},{8,24},{16,0},{24,8},{1,17},{9,25},{17,1},{25,9},{2,18},{10... | collective-permute-start | bytes 393224 | tf_op jit(solution)/shard_map/ppermute | solution.py:77
  141.7 1.5 flux_kernel.7
  143.3 1.7 %collective-permute-start.32 = (f32[2,16,1024]{2,1,0:T(8,128)S(1)}, f32[2,16,1024]{2,1,0:T(8,128)S(1)}, u32[]{:S(2)}, u32[]{:S(2)}) collective-permute-start(f32[2,16,1024]{2,1,0:T(8,128)S(1)} %get-tuple-element.145), channel_id=1, source_target_pairs={{0,8},{8,0},{16,24},{24,16},{1,9},{9,1},{17,25},{25,17},{2,10},{10... | collective-permute-start | bytes 393224 | tf_op jit(solution)/shard_map/ppermute | solution.py:77
  145.0 1.8 %collective-permute-start.33 = (f32[2,16,1024]{2,1,0:T(8,128)S(1)}, f32[2,16,1024]{2,1,0:T(8,128)S(1)}, u32[]{:S(2)}, u32[]{:S(2)}) collective-permute-start(f32[2,16,1024]{2,1,0:T(8,128)S(1)} %get-tuple-element.146), channel_id=1, source_target_pairs={{0,16},{8,24},{16,0},{24,8},{1,17},{9,25},{17,1},{25,9},{2,18},{10... | collective-permute-start | bytes 393224 | tf_op jit(solution)/shard_map/ppermute | solution.py:77
  149.0 1.6 %collective-permute-done.32.refs_8_ = f32[2,16,1024]{2,1,0:T(8,128)S(1)} collective-permute-done((f32[2,16,1024]{2,1,0:T(8,128)S(1)}, f32[2,16,1024]{2,1,0:T(8,128)S(1)}, u32[]{:S(2)}, u32[]{:S(2)}) %collective-permute-start.32) | collective-permute-done | bytes 131104 | tf_op jit(solution)/shard_map/ppermute | solution.py:77
  150.6 3.4 %collective-permute-done.33.refs_9_ = f32[2,16,1024]{2,1,0:T(8,128)S(1)} collective-permute-done((f32[2,16,1024]{2,1,0:T(8,128)S(1)}, f32[2,16,1024]{2,1,0:T(8,128)S(1)}, u32[]{:S(2)}, u32[]{:S(2)}) %collective-permute-start.33) | collective-permute-done | bytes 131104 | tf_op jit(solution)/shard_map/ppermute | solution.py:77
  154.0 2.5 %finish_kernel.1 = (f32[16,2,128,128]{3,2,1,0:T(8,128)}, f32[8,128]{1,0:T(8,128)}) custom-call(s32[2]{0:T(128)S(1)} %copy-done.6, f32[16,2,128,128]{3,2,1,0:T(8,128)S(1)} %bitcast.11, f32[4,16,2,16,128]{4,3,2,1,0:T(8,128)S(1)} %get-tuple-element.122.refs_2_, f32[2,16,1024]{2,1,0:T(8,128)S(1)} %get-tuple-element.132.refs_3_, ...), custom_call_target="tpu_custom_call" | custom-call | bytes 6291464 | tf_op jit(solution)/shard_map/finish_kernel/pallas_call | solution.py:63
  (70 shorter events, 19.3 us)
Async XLA Ops:
  0.0 7.8 %copy-start.10 = (s32[16]{0:T(128)S(1)}, s32[16]{0:T(128)}, u32[]{:S(2)}) copy-start(s32[16]{0:T(128)} %refs_2_.1) | copy-start | bytes 196
  0.0 7.8 %copy-start.9 = (s32[16,2]{0,1:T(2,128)S(1)}, s32[16,2]{0,1:T(2,128)}, u32[]{:S(2)}) copy-start(s32[16,2]{0,1:T(2,128)} %param.11) | copy-start | bytes 388
  0.6 7.2 %copy-start.6 = (s32[2]{0:T(128)S(1)}, s32[2]{0:T(128)}, u32[]{:S(2)}) copy-start(s32[2]{0:T(128)} %pad_add_fusion.refs_0_) | copy-start | bytes 28
  3.2 7.9 %collective-permute-start.3 = (f32[2,16,1024]{2,1,0:T(8,128)}, f32[2,16,1024]{2,1,0:T(8,128)S(1)}, u32[]{:S(2)}, u32[]{:S(2)}) collective-permute-start(f32[2,16,1024]{2,1,0:T(8,128)} %get-tuple-element.83), channel_id=1, source_target_pairs={{0,8},{8,0},{16,24},{24,16},{1,9},{9,1},{17,25},{25,17},{2,10},{10... | collective-permute-start | bytes 393224 | tf_op jit(solution)/shard_map/ppermute | solution.py:77
  6.2 8.0 %collective-permute-start.4 = (f32[2,16,1024]{2,1,0:T(8,128)}, f32[2,16,1024]{2,1,0:T(8,128)S(1)}, u32[]{:S(2)}, u32[]{:S(2)}) collective-permute-start(f32[2,16,1024]{2,1,0:T(8,128)} %get-tuple-element.84), channel_id=1, source_target_pairs={{0,16},{8,24},{16,0},{24,8},{1,17},{9,25},{17,1},{25,9},{2,18},{10... | collective-permute-start | bytes 393224 | tf_op jit(solution)/shard_map/ppermute | solution.py:77
  7.8 6.5 %collective-permute-start.5 = (f32[2,16,1024]{2,1,0:T(8,128)}, f32[2,16,1024]{2,1,0:T(8,128)S(1)}, u32[]{:S(2)}, u32[]{:S(2)}) collective-permute-start(f32[2,16,1024]{2,1,0:T(8,128)} %get-tuple-element.85), channel_id=1, source_target_pairs={{0,24},{8,16},{16,8},{24,0},{1,25},{9,17},{17,9},{25,1},{2,26},{10... | collective-permute-start | bytes 393224 | tf_op jit(solution)/shard_map/ppermute | solution.py:77
  7.8 1.6 %copy-start = (f32[16,2,1,16384]{3,2,1,0:T(1,128)S(1)}, f32[16,2,1,16384]{3,2,1,0:T(1,128)}, u32[]{:S(2)}) copy-start(f32[16,2,1,16384]{3,2,1,0:T(1,128)} %param.8) | copy-start | bytes 6291460
  9.4 0.7 copy-start.8
  10.1 4.2 %copy-start.7 = (f32[2,16,1024]{2,1,0:T(8,128)S(1)}, f32[2,16,1024]{2,1,0:T(8,128)}, u32[]{:S(2)}) copy-start(f32[2,16,1024]{2,1,0:T(8,128)} %get-tuple-element.82.refs_1_) | copy-start | bytes 393220
  10.1 31.1 %copy-start.2 = (bf16[64,192]{1,0:T(8,128)(2,1)S(1)}, bf16[64,192]{1,0:T(8,128)(2,1)}, u32[]{:S(2)}) copy-start(bf16[64,192]{1,0:T(8,128)(2,1)} %constant.12.clone.refs_1_) | copy-start | bytes 73732
  14.8 26.4 %collective-permute-start.10 = (f32[2,64,1024]{2,1,0:T(8,128)S(1)}, f32[2,64,1024]{2,1,0:T(8,128)S(1)}, u32[]{:S(2)}, u32[]{:S(2)}) collective-permute-start(f32[2,64,1024]{2,1,0:T(8,128)S(1)} %get-tuple-element.95.refs_3_), channel_id=1, source_target_pairs={{0,4},{1,5},{6,2},{7,3},{8,12},{9,13},{14,10},{15,11},{16,20},{17,... | collective-permute-start | bytes 1572872 | tf_op jit(solution)/shard_map/ppermute | solution.py:428
  19.4 26.7 %collective-permute-start.9 = (f32[2,64,1024]{2,1,0:T(8,128)S(1)}, f32[2,64,1024]{2,1,0:T(8,128)S(1)}, u32[]{:S(2)}, u32[]{:S(2)}) collective-permute-start(f32[2,64,1024]{2,1,0:T(8,128)S(1)} %get-tuple-element.95.refs_3_), channel_id=1, source_target_pairs={{2,6},{3,7},{4,0},{5,1},{10,14},{11,15},{12,8},{13,9},{18,22},{19,... | collective-permute-start | bytes 1572872 | tf_op jit(solution)/shard_map/ppermute | solution.py:429
  20.7 12.5 %collective-permute-start = (f32[2,16,3200]{2,1,0:T(8,128)S(1)}, f32[2,16,3200]{2,1,0:T(8,128)S(1)}, u32[]{:S(2)}, u32[]{:S(2)}) collective-permute-start(f32[2,16,3200]{2,1,0:T(8,128)S(1)} %get-tuple-element.79), channel_id=1, source_target_pairs={{0,8},{8,0},{16,24},{24,16},{1,9},{9,1},{17,25},{25,17},{2,10},{10... | collective-permute-start | bytes 1228808 | tf_op jit(solution)/shard_map/ppermute | solution.py:77
  21.9 18.6 %collective-permute-start.1 = (f32[2,16,3200]{2,1,0:T(8,128)S(1)}, f32[2,16,3200]{2,1,0:T(8,128)S(1)}, u32[]{:S(2)}, u32[]{:S(2)}) collective-permute-start(f32[2,16,3200]{2,1,0:T(8,128)S(1)} %get-tuple-element.80), channel_id=1, source_target_pairs={{0,16},{8,24},{16,0},{24,8},{1,17},{9,25},{17,1},{25,9},{2,18},{10... | collective-permute-start | bytes 1228808 | tf_op jit(solution)/shard_map/ppermute | solution.py:77
  22.8 17.7 %collective-permute-start.2 = (f32[2,16,3200]{2,1,0:T(8,128)S(1)}, f32[2,16,3200]{2,1,0:T(8,128)S(1)}, u32[]{:S(2)}, u32[]{:S(2)}) collective-permute-start(f32[2,16,3200]{2,1,0:T(8,128)S(1)} %get-tuple-element.81), channel_id=1, source_target_pairs={{0,24},{8,16},{16,8},{24,0},{1,25},{9,17},{17,9},{25,1},{2,26},{10... | collective-permute-start | bytes 1228808 | tf_op jit(solution)/shard_map/ppermute | solution.py:77
  41.2 6.5 %copy-start.3 = (f32[16,2,1,16384]{3,2,1,0:T(1,128)S(1)}, f32[16,2,1,16384]{3,2,1,0:T(1,128)}, u32[]{:S(2)}) copy-start(f32[16,2,1,16384]{3,2,1,0:T(1,128)} %param.9) | copy-start | bytes 6291460
  42.4 20.3 %collective-permute-start.11 = (f32[2,64,1024]{2,1,0:T(8,128)S(1)}, f32[2,64,1024]{2,1,0:T(8,128)S(1)}, u32[]{:S(2)}, u32[]{:S(2)}) collective-permute-start(f32[2,64,1024]{2,1,0:T(8,128)S(1)} %get-tuple-element.99), channel_id=1, source_target_pairs={{0,4},{1,5},{6,2},{7,3},{2,0},{3,1},{4,6},{5,7},{8,12},{9,13},{14,... | collective-permute-start | bytes 1572872 | tf_op jit(solution)/shard_map/ppermute | solution.py:428
  47.6 23.7 %collective-permute-start.12 = (f32[2,64,1024]{2,1,0:T(8,128)S(1)}, f32[2,64,1024]{2,1,0:T(8,128)S(1)}, u32[]{:S(2)}, u32[]{:S(2)}) collective-permute-start(f32[2,64,1024]{2,1,0:T(8,128)S(1)} %get-tuple-element.100), channel_id=1, source_target_pairs={{2,6},{3,7},{4,0},{5,1},{0,2},{1,3},{6,4},{7,5},{10,14},{11,15},{1... | collective-permute-start | bytes 1572872 | tf_op jit(solution)/shard_map/ppermute | solution.py:429
  64.0 12.3 %collective-permute-start.17 = (f32[2,64,1024]{2,1,0:T(8,128)S(1)}, f32[2,64,1024]{2,1,0:T(8,128)S(1)}, u32[]{:S(2)}, u32[]{:S(2)}) collective-permute-start(f32[2,64,1024]{2,1,0:T(8,128)S(1)} %get-tuple-element.111), channel_id=1, source_target_pairs={{0,4},{1,5},{6,2},{7,3},{2,0},{3,1},{4,6},{5,7},{8,12},{9,13},{14,... | collective-permute-start | bytes 1572872 | tf_op jit(solution)/shard_map/ppermute | solution.py:428
  73.0 26.6 %collective-permute-start.13 = (f32[4,64,1024]{2,1,0:T(8,128)S(1)}, f32[4,64,1024]{2,1,0:T(8,128)S(1)}, u32[]{:S(2)}, u32[]{:S(2)}) collective-permute-start(f32[4,64,1024]{2,1,0:T(8,128)S(1)} %get-tuple-element.105.refs_5_), channel_id=1, source_target_pairs={{0,1},{1,0},{2,3},{3,2},{4,5},{5,4},{6,7},{7,6},{8,9},{9,8},{10,11... | collective-permute-start | bytes 3145736 | tf_op jit(solution)/shard_map/ppermute | solution.py:77
  73.0 15.2 %collective-permute-start.18 = (f32[2,64,1024]{2,1,0:T(8,128)S(1)}, f32[2,64,1024]{2,1,0:T(8,128)S(1)}, u32[]{:S(2)}, u32[]{:S(2)}) collective-permute-start(f32[2,64,1024]{2,1,0:T(8,128)S(1)} %get-tuple-element.112), channel_id=1, source_target_pairs={{2,6},{3,7},{4,0},{5,1},{0,2},{1,3},{6,4},{7,5},{10,14},{11,15},{1... | collective-permute-start | bytes 1572872 | tf_op jit(solution)/shard_map/ppermute | solution.py:429
  73.4 16.3 %collective-permute-start.6 = (f32[2,16,4096]{2,1,0:T(8,128)S(1)}, f32[2,16,4096]{2,1,0:T(8,128)S(1)}, u32[]{:S(2)}, u32[]{:S(2)}) collective-permute-start(f32[2,16,4096]{2,1,0:T(8,128)S(1)} %get-tuple-element.91), channel_id=1, source_target_pairs={{0,8},{8,0},{16,24},{24,16},{1,9},{9,1},{17,25},{25,17},{2,10},{10... | collective-permute-start | bytes 1572872 | tf_op jit(solution)/shard_map/ppermute | solution.py:77
  74.0 24.9 %collective-permute-start.7 = (f32[2,16,4096]{2,1,0:T(8,128)S(1)}, f32[2,16,4096]{2,1,0:T(8,128)S(1)}, u32[]{:S(2)}, u32[]{:S(2)}) collective-permute-start(f32[2,16,4096]{2,1,0:T(8,128)S(1)} %get-tuple-element.92), channel_id=1, source_target_pairs={{0,16},{8,24},{16,0},{24,8},{1,17},{9,25},{17,1},{25,9},{2,18},{10... | collective-permute-start | bytes 1572872 | tf_op jit(solution)/shard_map/ppermute | solution.py:77
  76.3 22.6 %collective-permute-start.8 = (f32[2,16,4096]{2,1,0:T(8,128)S(1)}, f32[2,16,4096]{2,1,0:T(8,128)S(1)}, u32[]{:S(2)}, u32[]{:S(2)}) collective-permute-start(f32[2,16,4096]{2,1,0:T(8,128)S(1)} %get-tuple-element.93), channel_id=1, source_target_pairs={{0,24},{8,16},{16,8},{24,0},{1,25},{9,17},{17,9},{25,1},{2,26},{10... | collective-permute-start | bytes 1572872 | tf_op jit(solution)/shard_map/ppermute | solution.py:77
  88.3 24.0 %collective-permute-start.23 = (f32[2,64,1024]{2,1,0:T(8,128)S(1)}, f32[2,64,1024]{2,1,0:T(8,128)S(1)}, u32[]{:S(2)}, u32[]{:S(2)}) collective-permute-start(f32[2,64,1024]{2,1,0:T(8,128)S(1)} %get-tuple-element.124), channel_id=1, source_target_pairs={{0,4},{1,5},{6,2},{7,3},{2,0},{3,1},{4,6},{5,7},{8,12},{9,13},{14,... | collective-permute-start | bytes 1572872 | tf_op jit(solution)/shard_map/ppermute | solution.py:428
  88.8 10.9 %copy-start.4 = (f32[1,16384]{1,0:T(1,128)S(1)}, f32[1,16384]{1,0:T(1,128)}, u32[]{:S(2)}) copy-start(f32[1,16384]{1,0:T(1,128)} %param.12) | copy-start | bytes 196612
  88.8 10.9 %copy-start.5 = (bf16[64,192]{1,0:T(8,128)(2,1)S(1)}, bf16[64,192]{1,0:T(8,128)(2,1)}, u32[]{:S(2)}) copy-start(bf16[64,192]{1,0:T(8,128)(2,1)} %constant.13.clone.refs_1_) | copy-start | bytes 73732
  89.8 24.7 %collective-permute-start.24 = (f32[2,64,1024]{2,1,0:T(8,128)S(1)}, f32[2,64,1024]{2,1,0:T(8,128)S(1)}, u32[]{:S(2)}, u32[]{:S(2)}) collective-permute-start(f32[2,64,1024]{2,1,0:T(8,128)S(1)} %get-tuple-element.125), channel_id=1, source_target_pairs={{2,6},{3,7},{4,0},{5,1},{0,2},{1,3},{6,4},{7,5},{10,14},{11,15},{1... | collective-permute-start | bytes 1572872 | tf_op jit(solution)/shard_map/ppermute | solution.py:429
  100.8 5.0 %collective-permute-start.14 = (f32[2,16,1024]{2,1,0:T(8,128)S(1)}, f32[2,16,1024]{2,1,0:T(8,128)S(1)}, u32[]{:S(2)}, u32[]{:S(2)}) collective-permute-start(f32[2,16,1024]{2,1,0:T(8,128)S(1)} %get-tuple-element.107), channel_id=1, source_target_pairs={{0,8},{8,0},{16,24},{24,16},{1,9},{9,1},{17,25},{25,17},{2,10},{10... | collective-permute-start | bytes 393224 | tf_op jit(solution)/shard_map/ppermute | solution.py:77
  102.9 19.3 %collective-permute-start.19 = (f32[4,64,1024]{2,1,0:T(8,128)S(1)}, f32[4,64,1024]{2,1,0:T(8,128)S(1)}, u32[]{:S(2)}, u32[]{:S(2)}) collective-permute-start(f32[4,64,1024]{2,1,0:T(8,128)S(1)} %get-tuple-element.117.refs_5_), channel_id=1, source_target_pairs={{0,1},{1,0},{2,3},{3,2},{4,5},{5,4},{6,7},{7,6},{8,9},{9,8},{10,11... | collective-permute-start | bytes 3145736 | tf_op jit(solution)/shard_map/ppermute | solution.py:77
  103.0 7.3 %collective-permute-start.15 = (f32[2,16,1024]{2,1,0:T(8,128)S(1)}, f32[2,16,1024]{2,1,0:T(8,128)S(1)}, u32[]{:S(2)}, u32[]{:S(2)}) collective-permute-start(f32[2,16,1024]{2,1,0:T(8,128)S(1)} %get-tuple-element.108), channel_id=1, source_target_pairs={{0,16},{8,24},{16,0},{24,8},{1,17},{9,25},{17,1},{25,9},{2,18},{10... | collective-permute-start | bytes 393224 | tf_op jit(solution)/shard_map/ppermute | solution.py:77
  105.8 5.9 %collective-permute-start.16 = (f32[2,16,1024]{2,1,0:T(8,128)S(1)}, f32[2,16,1024]{2,1,0:T(8,128)S(1)}, u32[]{:S(2)}, u32[]{:S(2)}) collective-permute-start(f32[2,16,1024]{2,1,0:T(8,128)S(1)} %get-tuple-element.109), channel_id=1, source_target_pairs={{0,24},{8,16},{16,8},{24,0},{1,25},{9,17},{17,9},{25,1},{2,26},{10... | collective-permute-start | bytes 393224 | tf_op jit(solution)/shard_map/ppermute | solution.py:77
  116.0 19.8 %collective-permute-start.25 = (f32[4,64,1024]{2,1,0:T(8,128)S(1)}, f32[4,64,1024]{2,1,0:T(8,128)S(1)}, u32[]{:S(2)}, u32[]{:S(2)}) collective-permute-start(f32[4,64,1024]{2,1,0:T(8,128)S(1)} %get-tuple-element.131.refs_5_), channel_id=1, source_target_pairs={{0,1},{1,0},{2,3},{3,2},{4,5},{5,4},{6,7},{7,6},{8,9},{9,8},{10,11... | collective-permute-start | bytes 3145736 | tf_op jit(solution)/shard_map/ppermute | solution.py:77
  116.1 20.9 %collective-permute-start.29 = (f32[2,64,1024]{2,1,0:T(8,128)S(1)}, f32[2,64,1024]{2,1,0:T(8,128)S(1)}, u32[]{:S(2)}, u32[]{:S(2)}) collective-permute-start(f32[2,64,1024]{2,1,0:T(8,128)S(1)} %get-tuple-element.137), channel_id=1, source_target_pairs={{2,0},{3,1},{4,6},{5,7},{10,8},{11,9},{12,14},{13,15},{18,16},{19,... | collective-permute-start | bytes 1572872 | tf_op jit(solution)/shard_map/ppermute | solution.py:464
  117.4 17.7 %copy-start.1 = (f32[16,2,1,16384]{3,2,1,0:T(1,128)S(1)}, f32[16,2,1,16384]{3,2,1,0:T(1,128)}, u32[]{:S(2)}) copy-start(f32[16,2,1,16384]{3,2,1,0:T(1,128)} %param.13) | copy-start | bytes 6291460
  117.4 19.6 %collective-permute-start.30 = (f32[2,64,1024]{2,1,0:T(8,128)S(1)}, f32[2,64,1024]{2,1,0:T(8,128)S(1)}, u32[]{:S(2)}, u32[]{:S(2)}) collective-permute-start(f32[2,64,1024]{2,1,0:T(8,128)S(1)} %get-tuple-element.138), channel_id=1, source_target_pairs={{0,2},{1,3},{6,4},{7,5},{8,10},{9,11},{14,12},{15,13},{16,18},{17,... | collective-permute-start | bytes 1572872 | tf_op jit(solution)/shard_map/ppermute | solution.py:465
  123.3 5.8 %collective-permute-start.20 = (f32[2,16,1024]{2,1,0:T(8,128)S(1)}, f32[2,16,1024]{2,1,0:T(8,128)S(1)}, u32[]{:S(2)}, u32[]{:S(2)}) collective-permute-start(f32[2,16,1024]{2,1,0:T(8,128)S(1)} %get-tuple-element.119), channel_id=1, source_target_pairs={{0,8},{8,0},{16,24},{24,16},{1,9},{9,1},{17,25},{25,17},{2,10},{10... | collective-permute-start | bytes 393224 | tf_op jit(solution)/shard_map/ppermute | solution.py:77
  125.6 6.6 %collective-permute-start.21 = (f32[2,16,1024]{2,1,0:T(8,128)S(1)}, f32[2,16,1024]{2,1,0:T(8,128)S(1)}, u32[]{:S(2)}, u32[]{:S(2)}) collective-permute-start(f32[2,16,1024]{2,1,0:T(8,128)S(1)} %get-tuple-element.120), channel_id=1, source_target_pairs={{0,16},{8,24},{16,0},{24,8},{1,17},{9,25},{17,1},{25,9},{2,18},{10... | collective-permute-start | bytes 393224 | tf_op jit(solution)/shard_map/ppermute | solution.py:77
  129.2 5.9 %collective-permute-start.22 = (f32[2,16,1024]{2,1,0:T(8,128)S(1)}, f32[2,16,1024]{2,1,0:T(8,128)S(1)}, u32[]{:S(2)}, u32[]{:S(2)}) collective-permute-start(f32[2,16,1024]{2,1,0:T(8,128)S(1)} %get-tuple-element.121), channel_id=1, source_target_pairs={{0,24},{8,16},{16,8},{24,0},{1,25},{9,17},{17,9},{25,1},{2,26},{10... | collective-permute-start | bytes 393224 | tf_op jit(solution)/shard_map/ppermute | solution.py:77
  138.2 3.5 %collective-permute-start.31 = (f32[4,64,1024]{2,1,0:T(8,128)S(1)}, f32[4,64,1024]{2,1,0:T(8,128)S(1)}, u32[]{:S(2)}, u32[]{:S(2)}) collective-permute-start(f32[4,64,1024]{2,1,0:T(8,128)S(1)} %get-tuple-element.143.refs_5_), channel_id=1, source_target_pairs={{0,1},{1,0},{2,3},{3,2},{4,5},{5,4},{6,7},{7,6},{8,9},{9,8},{10,11... | collective-permute-start | bytes 3145736 | tf_op jit(solution)/shard_map/ppermute | solution.py:77
  138.2 8.5 %collective-permute-start.26 = (f32[2,16,1024]{2,1,0:T(8,128)S(1)}, f32[2,16,1024]{2,1,0:T(8,128)S(1)}, u32[]{:S(2)}, u32[]{:S(2)}) collective-permute-start(f32[2,16,1024]{2,1,0:T(8,128)S(1)} %get-tuple-element.133), channel_id=1, source_target_pairs={{0,8},{8,0},{16,24},{24,16},{1,9},{9,1},{17,25},{25,17},{2,10},{10... | collective-permute-start | bytes 393224 | tf_op jit(solution)/shard_map/ppermute | solution.py:77
  139.9 8.4 %collective-permute-start.27 = (f32[2,16,1024]{2,1,0:T(8,128)S(1)}, f32[2,16,1024]{2,1,0:T(8,128)S(1)}, u32[]{:S(2)}, u32[]{:S(2)}) collective-permute-start(f32[2,16,1024]{2,1,0:T(8,128)S(1)} %get-tuple-element.134), channel_id=1, source_target_pairs={{0,16},{8,24},{16,0},{24,8},{1,17},{9,25},{17,1},{25,9},{2,18},{10... | collective-permute-start | bytes 393224 | tf_op jit(solution)/shard_map/ppermute | solution.py:77
  141.7 7.3 %collective-permute-start.28 = (f32[2,16,1024]{2,1,0:T(8,128)S(1)}, f32[2,16,1024]{2,1,0:T(8,128)S(1)}, u32[]{:S(2)}, u32[]{:S(2)}) collective-permute-start(f32[2,16,1024]{2,1,0:T(8,128)S(1)} %get-tuple-element.135), channel_id=1, source_target_pairs={{0,24},{8,16},{16,8},{24,0},{1,25},{9,17},{17,9},{25,1},{2,26},{10... | collective-permute-start | bytes 393224 | tf_op jit(solution)/shard_map/ppermute | solution.py:77
  143.3 7.3 %collective-permute-start.32 = (f32[2,16,1024]{2,1,0:T(8,128)S(1)}, f32[2,16,1024]{2,1,0:T(8,128)S(1)}, u32[]{:S(2)}, u32[]{:S(2)}) collective-permute-start(f32[2,16,1024]{2,1,0:T(8,128)S(1)} %get-tuple-element.145), channel_id=1, source_target_pairs={{0,8},{8,0},{16,24},{24,16},{1,9},{9,1},{17,25},{25,17},{2,10},{10... | collective-permute-start | bytes 393224 | tf_op jit(solution)/shard_map/ppermute | solution.py:77
  145.0 9.1 %collective-permute-start.33 = (f32[2,16,1024]{2,1,0:T(8,128)S(1)}, f32[2,16,1024]{2,1,0:T(8,128)S(1)}, u32[]{:S(2)}, u32[]{:S(2)}) collective-permute-start(f32[2,16,1024]{2,1,0:T(8,128)S(1)} %get-tuple-element.146), channel_id=1, source_target_pairs={{0,16},{8,24},{16,0},{24,8},{1,17},{9,25},{17,1},{25,9},{2,18},{10... | collective-permute-start | bytes 393224 | tf_op jit(solution)/shard_map/ppermute | solution.py:77
  146.8 7.3 %collective-permute-start.34 = (f32[2,16,1024]{2,1,0:T(8,128)S(1)}, f32[2,16,1024]{2,1,0:T(8,128)S(1)}, u32[]{:S(2)}, u32[]{:S(2)}) collective-permute-start(f32[2,16,1024]{2,1,0:T(8,128)S(1)} %get-tuple-element.147), channel_id=1, source_target_pairs={{0,24},{8,16},{16,8},{24,0},{1,25},{9,17},{17,9},{25,1},{2,26},{10... | collective-permute-start | bytes 393224 | tf_op jit(solution)/shard_map/ppermute | solution.py:77
